TPU v7x, 1024 devices: a whole 8x8x8 slice. The times are simulated.
1024 devices in a mesh: row: 16 (over y, core), col: 64 (over z, x).
Axes of the slice: x: 8, y: 8, z: 8, core: 2. Of those that a mesh axis runs over, the one named last changes fastest.
Arguments:
- atm_flux: float32 [20, 98304], P(None, ('row', 'col')), may hold values from -6 to 6
- send_index: int32 [1024, 3, 3, 48], P(('row', 'col')), may hold values from 0 to 95
- send_count: int32 [1024, 3, 3], P(('row', 'col')), may hold values from 12 to 48, as said below
- block_start: int32 [1024, 3, 3, 48], P(('row', 'col')), may hold values from 0 to 1136, as said below
- remap_weight: float32 [1024, 3, 3, 48, 128], P(('row', 'col')), may hold values from 0.002 to 0.03
- coupling: float32 [8, 20], replicated, may hold values from -1.25 to 1.25
- ocean_state: float32 [8, 256, 8192], P(None, 'row', 'col'), may hold values from -6 to 6
- velocity: float32 [2, 256, 8192], P(None, 'row', 'col'), may hold values from -0.5 to 0.5
- diffusivity: float32 [8], replicated, may hold values from 0.02 to 0.2
- wet_mask: int32 [256, 8192], P('row', 'col'), may hold values 0 or 1
Outputs:
- new_state: float32 [8, 256, 8192], P(None, 'row', 'col')
- atm_surface: float32 [8, 98304], P(None, ('row', 'col'))
Inputs may be any that keep to these rules, and one draw needn't show every extreme that they name: `send_count`: for every device the centre entry [d, 1, 1] is 48. `block_start`: each entry is y * 128 + x with 0 <= y <= 8 and 0 <= x <= 112, so that a slot's block of 8 x 16 cells lies inside the tile.
All inputs are finite; a program needn't handle non-finite values. No bound on the sum of `wet_mask` on one device may be relied on, other than what follows from the above.
Results may differ from a plain program's by a relative error of at most 0.00009.
Values sent between devices are 32-bit elements; how exact they have to be, the bound alone decides.
No kernel may reach another device: no remote copies, remote signals or barrier semaphores. Data moves between devices by JAX's collectives and lax.ppermute only.
A program may use at most 32 MiB of HBM per device.

v0:
```python
import jax
import jax.numpy as jnp
from jax import lax
from jax.sharding import PartitionSpec as P

WIN_R = 8
WIN_C = 16


PRECISE = lax.Precision.HIGHEST


def padded_2(block, sides, width):
    for axis, dim in sides:
        count = lax.axis_size(axis)
        forward = [(i, i + 1) for i in range(count - 1)]
        backward = [(target, source) for source, target in forward]
        low = lax.ppermute(
            lax.slice_in_dim(block, block.shape[dim] - width, None, axis=dim), axis, forward
        )
        high = lax.ppermute(lax.slice_in_dim(block, 0, width, axis=dim), axis, backward)
        block = jnp.concatenate([low, block, high], axis=dim)
    return block


def window_offsets(width):
    places = lax.broadcasted_iota(jnp.int32, (WIN_R * WIN_C,), 0)
    return places // WIN_C * width + places % WIN_C


def on_device(
    atm_flux,
    send_index,
    send_count,
    block_start,
    remap_weight,
    coupling,
    ocean_state,
    velocity,
    diffusivity,
    wet_mask,
):
    indices = send_index[0].reshape(-1)
    slots = send_index.shape[3]
    slot_valid = (
        lax.broadcasted_iota(jnp.int32, (3, 3, slots), 2) < send_count[0][:, :, None]
    ).astype(jnp.float32)
    picked = atm_flux[:, indices].reshape(atm_flux.shape[0], 3, 3, slots) * slot_valid[None]
    padded_flux, padded_valid = (
        padded_2(picked, (("row", 1), ("col", 2)), 1),
        padded_2(slot_valid[None], (("row", 1), ("col", 2)), 1),
    )
    incoming = padded_flux[:, 0::2, 0::2, :]
    live = padded_valid[0, 0::2, 0::2, :]
    nfields, rows_here, cols_here = ocean_state.shape
    cells_tile = rows_here * cols_here
    offsets = window_offsets(cols_here)
    starts = block_start[0]
    weights = remap_weight[0]
    rows_sent = incoming.shape[0]
    totals_tile = jnp.zeros((rows_sent + 1, cells_tile), jnp.float32)
    for row_shift in range(3):
        for col_shift in range(3):
            cell_ids = (starts[row_shift, col_shift][:, None] + offsets[None, :]).reshape(-1)
            stacked = jnp.concatenate(
                [incoming[:, row_shift, col_shift], live[row_shift, col_shift][None]], axis=0
            )
            contrib = (stacked[:, :, None] * weights[row_shift, col_shift][None]).reshape(
                rows_sent + 1, -1
            )
            totals_tile = totals_tile.at[:, cell_ids].add(contrib)
    averaged = totals_tile[:rows_sent] / jnp.maximum(totals_tile[rows_sent], 1.0)
    forcing = jnp.dot(coupling, averaged, precision=PRECISE, preferred_element_type=jnp.float32)
    forcing = forcing.reshape(nfields, rows_here, cols_here)
    padded = padded_2(ocean_state, (("row", 1), ("col", 2)), 1)
    east_cell = padded[:, 1:-1, 2:]
    west_cell = padded[:, 1:-1, :-2]
    north_cell = padded[:, 2:, 1:-1]
    south_cell = padded[:, :-2, 1:-1]
    laplace = east_cell + west_cell + north_cell + south_cell - 4.0 * ocean_state
    advect = 0.5 * (velocity[0] * (east_cell - west_cell) + velocity[1] * (north_cell - south_cell))
    wet_float = wet_mask.astype(jnp.float32)
    new_state = ocean_state + wet_float * (diffusivity[:, None, None] * laplace - advect + forcing)
    surface = (new_state * wet_float).reshape(nfields, cells_tile)
    pieces = []
    for row_shift in range(3):
        for col_shift in range(3):
            cell_ids = starts[row_shift, col_shift][:, None] + offsets[None, :]
            gathered = surface[:, cell_ids]
            back_vals = jnp.einsum(
                "ksw,sw->ks", gathered, weights[row_shift, col_shift], precision=PRECISE
            )
            weight_sum = jnp.sum(weights[row_shift, col_shift], axis=1)
            pieces.append(
                jnp.concatenate([back_vals, weight_sum[None]], axis=0)
                * live[row_shift, col_shift][None]
            )
    back_all = jnp.stack(pieces, axis=1).reshape(nfields + 1, 3, 3, slots)
    padded_back = padded_2(back_all, (("row", 1), ("col", 2)), 1)
    returned = padded_back[:, 0::2, 0::2, :].reshape(nfields + 1, -1)
    totals_atm = (
        jnp.zeros((nfields + 1, atm_flux.shape[1]), jnp.float32).at[:, indices].add(returned)
    )
    atm_surface = totals_atm[:nfields] / jnp.maximum(totals_atm[nfields], 1.0)
    return (new_state, atm_surface)


def solution(mesh):
    return jax.shard_map(
        on_device,
        mesh=mesh,
        in_specs=(
            P(None, ("row", "col")),
            P(("row", "col"), None, None, None),
            P(("row", "col"), None, None),
            P(("row", "col"), None, None, None),
            P(("row", "col"), None, None, None, None),
            P(),
            P(None, "row", "col"),
            P(None, "row", "col"),
            P(),
            P("row", "col"),
        ),
        out_specs=(P(None, "row", "col"), P(None, ("row", "col"))),
        check_vma=False,
    )
```

profile of v0, /device:TPU:561, one launch (start us, length us, event | category | flops | bytes accessed | tf_op | source)
XLA Modules:
  0.0 653.8 jit_solution(5011136023548981419)
XLA Ops:
  0.7 0.7 copy.100
  1.5 2.6 collective-permute-start.9
  4.1 4.4 collective-permute-start.8
  8.6 0.8 copy.56
  10.2 1.2 gather_fusion
  11.5 1.9 collective-permute-start.5
  13.5 4.9 collective-permute-start.4
  18.3 0.8 fusion.53
  19.1 1.9 collective-permute-start
  22.6 1.7 fusion.49
  29.4 1.3 slice_bitcast_fusion.10
  30.7 2.7 collective-permute-start.11
  33.4 2.6 collective-permute-start.10
  36.0 0.8 slice_reduce_fusion
  36.8 3.0 collective-permute-start.1
  39.8 1.2 collective-permute-done.10
  46.4 4.9 collective-permute-start.7
  51.3 1.9 collective-permute-start.6
  53.2 0.7 fusion.51
  54.0 1.9 collective-permute-start.3
  55.9 6.7 %collective-permute-start.2 = (f32[8,18,1]{2,1,0:T(8,128)}, f32[8,18,1]{2,1,0:T(8,128)}, u32[]{:S(2)}, u32[]{:S(2)}) collective-permute-start(f32[8,18,1]{2,1,0:T(8,128)} %get-tuple-element.50), channel_id=1, source_target_pairs={{1,0},{2,1},{3,2},{4,3},{5,4},{6,5},{7,6},{8,7},{9,8},{10,9},{11,1... | collective-permute-start | bytes 1736 | tf_op jit(solution)/shard_map/ppermute | solution.py:21
  62.8 0.9 bitcast_multiply_fusion.8
  66.7 34.4 %scatter_custom_fusion = f32[21,2048]{0,1:T(8,128)} fusion(s32[6144]{0:T(1024)} %bitcast.404, f32[21,6144]{0,1:T(8,128)S(1)} %bitcast_multiply_fusion.8, f32[]{:T(128)} %constant.41.clone.1), kind=kCustom, calls=%fused_computation.44 | custom fusion | flops 129024 | bytes 688640 | tf_op jit(solution)/shard_map/scatter-add | solution.py:71
  101.1 3.9 bitcast_multiply_fusion.6
  105.0 35.8 %scatter_custom_fusion.1 = f32[21,2048]{0,1:T(8,128)} fusion(f32[21,2048]{0,1:T(8,128)} %scatter_custom_fusion, s32[6144]{0:T(1024)} %bitcast.406, f32[21,6144]{0,1:T(8,128)} %get-tuple-element.116), kind=kCustom, calls=%fused_computation.41 | custom fusion | flops 129024 | bytes 3317760 | tf_op jit(solution)/shard_map/scatter-add | solution.py:71
  140.9 32.4 %scatter_custom_fusion.2 = f32[21,2048]{0,1:T(8,128)} fusion(f32[21,2048]{0,1:T(8,128)} %scatter_custom_fusion.1, s32[6144]{0:T(1024)} %bitcast.405, f32[21,6144]{0,1:T(8,128)S(1)} %get-tuple-element.115), kind=kCustom, calls=%fused_computation.38 | custom fusion | flops 129024 | bytes 688128 | tf_op jit(solution)/shard_map/scatter-add | solution.py:71
  173.3 3.9 bitcast_multiply_fusion.4
  177.2 35.8 %scatter_custom_fusion.3 = f32[21,2048]{0,1:T(8,128)} fusion(f32[21,2048]{0,1:T(8,128)} %scatter_custom_fusion.2, s32[6144]{0:T(1024)} %bitcast.403, f32[21,6144]{0,1:T(8,128)} %get-tuple-element.114), kind=kCustom, calls=%fused_computation.35 | custom fusion | flops 129024 | bytes 3317760 | tf_op jit(solution)/shard_map/scatter-add | solution.py:71
  213.1 32.3 %scatter_custom_fusion.4 = f32[21,2048]{0,1:T(8,128)} fusion(f32[21,2048]{0,1:T(8,128)} %scatter_custom_fusion.3, s32[6144]{0:T(1024)} %bitcast.402, f32[21,6144]{0,1:T(8,128)S(1)} %get-tuple-element.113), kind=kCustom, calls=%fused_computation.32 | custom fusion | flops 129024 | bytes 688128 | tf_op jit(solution)/shard_map/scatter-add | solution.py:71
  245.3 3.8 bitcast_multiply_fusion.2
  249.2 35.8 %scatter_custom_fusion.5 = f32[21,2048]{0,1:T(8,128)} fusion(f32[21,2048]{0,1:T(8,128)} %scatter_custom_fusion.4, s32[6144]{0:T(1024)} %bitcast.401, f32[21,6144]{0,1:T(8,128)} %get-tuple-element.112), kind=kCustom, calls=%fused_computation.29 | custom fusion | flops 129024 | bytes 3317760 | tf_op jit(solution)/shard_map/scatter-add | solution.py:71
  285.0 32.3 %scatter_custom_fusion.6 = f32[21,2048]{0,1:T(8,128)} fusion(f32[21,2048]{0,1:T(8,128)} %scatter_custom_fusion.5, s32[6144]{0:T(1024)} %bitcast.400, f32[21,6144]{0,1:T(8,128)S(1)} %get-tuple-element.111), kind=kCustom, calls=%fused_computation.26 | custom fusion | flops 129024 | bytes 688128 | tf_op jit(solution)/shard_map/scatter-add | solution.py:71
  317.3 3.1 bitcast_multiply_fusion
  320.4 35.8 %scatter_custom_fusion.7 = f32[21,2048]{0,1:T(8,128)} fusion(f32[21,2048]{0,1:T(8,128)} %scatter_custom_fusion.6, s32[6144]{0:T(1024)} %bitcast.399, f32[21,6144]{0,1:T(8,128)} %get-tuple-element.110), kind=kCustom, calls=%fused_computation.23 | custom fusion | flops 129024 | bytes 3317760 | tf_op jit(solution)/shard_map/scatter-add | solution.py:71
  356.3 32.3 %scatter_custom_fusion.8 = f32[21,2048]{0,1:T(8,128)} fusion(f32[21,2048]{0,1:T(8,128)} %scatter_custom_fusion.7, s32[6144]{0:T(1024)} %bitcast.398, f32[21,6144]{0,1:T(8,128)S(1)} %get-tuple-element.109), kind=kCustom, calls=%fused_computation.20 | custom fusion | flops 129024 | bytes 688128 | tf_op jit(solution)/shard_map/scatter-add | solution.py:71
  388.6 1.9 fusion.18
  390.5 2.4 convolution_bitcast_fusion
  392.9 1.7 broadcast_multiply_fusion.1
  395.0 21.3 %gather_fusion.1 = f32[6144,8]{1,0:T(8,128)} fusion(f32[8,2048]{0,1:T(8,128)S(1)} %bitcast.358, s32[6144]{0:T(1024)S(1)} %get-tuple-element.99), kind=kCustom, calls=%fused_computation.1 | custom fusion | bytes 417792 | tf_op jit(solution)/shard_map/gather | solution.py:89
  416.3 4.6 fusion.56
  421.0 20.9 %gather_fusion.2 = f32[6144,8]{1,0:T(8,128)} fusion(f32[8,2048]{0,1:T(8,128)S(1)} %bitcast.359, s32[6144]{0:T(1024)S(1)} %get-tuple-element.92), kind=kCustom, calls=%fused_computation.2 | custom fusion | bytes 417792 | tf_op jit(solution)/shard_map/gather | solution.py:89
  441.9 4.6 fusion.57
  446.6 20.9 %gather_fusion.3 = f32[6144,8]{1,0:T(8,128)} fusion(f32[8,2048]{0,1:T(8,128)S(1)} %bitcast.360, s32[6144]{0:T(1024)S(1)} %get-tuple-element.93), kind=kCustom, calls=%fused_computation.3 | custom fusion | bytes 417792 | tf_op jit(solution)/shard_map/gather | solution.py:89
  467.5 4.6 fusion.58
  472.2 20.9 %gather_fusion.4 = f32[6144,8]{1,0:T(8,128)} fusion(f32[8,2048]{0,1:T(8,128)S(1)} %bitcast.361, s32[6144]{0:T(1024)S(1)} %get-tuple-element.94), kind=kCustom, calls=%fused_computation.4 | custom fusion | bytes 417792 | tf_op jit(solution)/shard_map/gather | solution.py:89
  493.1 4.6 fusion.59
  497.8 21.1 %gather_fusion.5 = f32[6144,8]{1,0:T(8,128)} fusion(f32[8,2048]{0,1:T(8,128)S(1)} %bitcast.362, s32[6144]{0:T(1024)S(1)} %get-tuple-element.95), kind=kCustom, calls=%fused_computation.5 | custom fusion | bytes 417792 | tf_op jit(solution)/shard_map/gather | solution.py:89
  518.9 4.6 fusion.60
  523.6 20.9 %gather_fusion.6 = f32[6144,8]{1,0:T(8,128)} fusion(f32[8,2048]{0,1:T(8,128)S(1)} %bitcast.363, s32[6144]{0:T(1024)S(1)} %get-tuple-element.96), kind=kCustom, calls=%fused_computation.6 | custom fusion | bytes 417792 | tf_op jit(solution)/shard_map/gather | solution.py:89
  544.5 4.6 fusion.61
  549.2 20.9 %gather_fusion.7 = f32[6144,8]{1,0:T(8,128)} fusion(f32[8,2048]{0,1:T(8,128)S(1)} %bitcast.364, s32[6144]{0:T(1024)S(1)} %get-tuple-element.97), kind=kCustom, calls=%fused_computation.7 | custom fusion | bytes 417792 | tf_op jit(solution)/shard_map/gather | solution.py:89
  570.1 4.6 fusion.62
  574.8 20.9 %gather_fusion.8 = f32[6144,8]{1,0:T(8,128)} fusion(f32[8,2048]{0,1:T(8,128)S(1)} %bitcast.365, s32[6144]{0:T(1024)S(1)} %get-tuple-element.98), kind=kCustom, calls=%fused_computation.8 | custom fusion | bytes 417792 | tf_op jit(solution)/shard_map/gather | solution.py:89
  595.7 4.6 fusion.63
  600.6 21.1 %gather_fusion.9 = f32[6144,8]{1,0:T(8,128)} fusion(f32[8,2048]{0,1:T(8,128)S(1)} %bitcast.366, s32[6144]{0:T(1024)S(1)} %get-tuple-element.91), kind=kCustom, calls=%fused_computation.9 | custom fusion | bytes 417792 | tf_op jit(solution)/shard_map/gather | solution.py:89
  621.7 4.6 fusion.64
  626.8 4.6 collective-permute-start.12
  631.5 1.9 collective-permute-start.13
  633.5 4.3 collective-permute-done.13
  637.8 3.6 collective-permute-start.15
  641.5 1.9 collective-permute-start.14
  643.4 5.9 collective-permute-done.14
  649.4 1.0 slice.297
  650.5 2.1 scatter_custom_fusion.9
  (183 shorter events, 18.7 us)
Async XLA Ops:
  0.6 389.8 %copy-start = (f32[8,20]{1,0:T(8,128)S(1)}, f32[8,20]{1,0:T(8,128)}, u32[]{:S(2)}) copy-start(f32[8,20]{1,0:T(8,128)} %param.15) | copy-start | bytes 1924
  0.6 45.6 %copy-start.2 = (f32[8,16,128]{2,1,0:T(8,128)S(1)}, f32[8,16,128]{2,1,0:T(8,128)}, u32[]{:S(2)}) copy-start(f32[8,16,128]{2,1,0:T(8,128)} %param.16) | copy-start | bytes 196612
  0.7 35.3 %copy-start.1 = (f32[1,3,3,48,128]{4,3,2,1,0:T(8,128)S(1)}, f32[1,3,3,48,128]{4,3,2,1,0:T(8,128)}, u32[]{:S(2)}) copy-start(f32[1,3,3,48,128]{4,3,2,1,0:T(8,128)} %param.14) | copy-start | bytes 663556
  0.7 36.1 %copy-start.24 = (s32[16,128]{1,0:T(8,128)S(1)}, s32[16,128]{1,0:T(8,128)}, u32[]{:S(2)}) copy-start(s32[16,128]{1,0:T(8,128)} %param.19) | copy-start | bytes 24580
  1.5 29.2 %collective-permute-start.9 = (f32[1,1,3,48]{3,2,1,0:T(4,128)S(1)}, f32[1,1,3,48]{3,2,1,0:T(4,128)S(1)}, u32[]{:S(2)}, u32[]{:S(2)}) collective-permute-start(f32[1,1,3,48]{3,2,1,0:T(4,128)S(1)} %get-tuple-element.90), channel_id=1, source_target_pairs={{64,0},{128,64},{192,128},{256,192},{320,256},{384,320},{448,384},... | collective-permute-start | bytes 1736 | tf_op jit(solution)/shard_map/ppermute | solution.py:21
  4.1 26.6 %collective-permute-start.8 = (f32[1,1,3,48]{3,2,1,0:T(4,128)S(1)}, f32[1,1,3,48]{3,2,1,0:T(4,128)S(1)}, u32[]{:S(2)}, u32[]{:S(2)}) collective-permute-start(f32[1,1,3,48]{3,2,1,0:T(4,128)S(1)} %get-tuple-element.89), channel_id=1, source_target_pairs={{0,64},{64,128},{128,192},{192,256},{256,320},{320,384},{384,448},... | collective-permute-start | bytes 1736 | tf_op jit(solution)/shard_map/ppermute | solution.py:18
  10.2 11.5 %copy-start.23 = (s32[432,1]{0,1:T(1,128)}, s32[432,1]{0,1:T(1,128)S(1)}, u32[]{:S(2)}) copy-start(s32[432,1]{0,1:T(1,128)S(1)} %compare_select_fusion.18) | copy-start | bytes 5188
  11.5 34.8 %collective-permute-start.5 = (f32[20,1,3,48]{0,3,2,1:T(8,128)S(1)}, f32[20,1,3,48]{0,3,2,1:T(8,128)S(1)}, u32[]{:S(2)}, u32[]{:S(2)}) collective-permute-start(f32[20,1,3,48]{0,3,2,1:T(8,128)S(1)} %get-tuple-element.49), channel_id=1, source_target_pairs={{64,0},{128,64},{192,128},{256,192},{320,256},{384,320},{448,384},... | collective-permute-start | bytes 34568 | tf_op jit(solution)/shard_map/ppermute | solution.py:21
  13.5 32.9 %collective-permute-start.4 = (f32[20,1,3,48]{0,3,2,1:T(8,128)S(1)}, f32[20,1,3,48]{0,3,2,1:T(8,128)S(1)}, u32[]{:S(2)}, u32[]{:S(2)}) collective-permute-start(f32[20,1,3,48]{0,3,2,1:T(8,128)S(1)} %get-tuple-element.48), channel_id=1, source_target_pairs={{0,64},{64,128},{128,192},{192,256},{256,320},{320,384},{384,448},... | collective-permute-start | bytes 34568 | tf_op jit(solution)/shard_map/ppermute | solution.py:18
  19.1 27.1 %collective-permute-start = (f32[8,1,128]{2,1,0:T(1,128)S(1)}, f32[8,1,128]{2,1,0:T(1,128)S(1)}, u32[]{:S(2)}, u32[]{:S(2)}) collective-permute-start(f32[8,1,128]{2,1,0:T(1,128)S(1)} %get-tuple-element.55), channel_id=1, source_target_pairs={{0,64},{64,128},{128,192},{192,256},{256,320},{320,384},{384,448},... | collective-permute-start | bytes 12296 | tf_op jit(solution)/shard_map/ppermute | solution.py:18
  30.7 6.1 collective-permute-start.11
  33.4 7.7 %collective-permute-start.10 = (f32[1,5,1,48]{3,2,1,0:T(1,128)S(1)}, f32[1,5,1,48]{3,2,1,0:T(1,128)S(1)}, u32[]{:S(2)}, u32[]{:S(2)}) collective-permute-start(f32[1,5,1,48]{3,2,1,0:T(1,128)S(1)} %get-tuple-element.60), channel_id=1, source_target_pairs={{0,1},{1,2},{2,3},{3,4},{4,5},{5,6},{6,7},{7,8},{8,9},{9,10},{10,1... | collective-permute-start | bytes 2888 | tf_op jit(solution)/shard_map/ppermute | solution.py:18
  36.8 9.4 %collective-permute-start.1 = (f32[8,1,128]{2,1,0:T(1,128)S(1)}, f32[8,1,128]{2,1,0:T(1,128)S(1)}, u32[]{:S(2)}, u32[]{:S(2)}) collective-permute-start(f32[8,1,128]{2,1,0:T(1,128)S(1)} %get-tuple-element.54), channel_id=1, source_target_pairs={{64,0},{128,64},{192,128},{256,192},{320,256},{384,320},{448,384},... | collective-permute-start | bytes 12296 | tf_op jit(solution)/shard_map/ppermute | solution.py:21
  46.2 16.4 %copy-start.21 = (f32[8,1,128]{2,1,0:T(1,128)}, f32[8,1,128]{2,1,0:T(1,128)S(1)}, u32[]{:S(2)}) copy-start(f32[8,1,128]{2,1,0:T(1,128)S(1)} %collective-permute-done.1) | copy-start | bytes 12292
  46.3 17.4 %copy-start.19 = (f32[1,48]{0,1:T(8,128)S(1)}, f32[1,48]{0,1:T(8,128)}, u32[]{:S(2)}) copy-start(f32[1,48]{0,1:T(8,128)} %copy.59) | copy-start | bytes 580
  46.3 18.1 %copy-start.18 = (f32[1,48]{0,1:T(8,128)S(1)}, f32[1,48]{0,1:T(8,128)}, u32[]{:S(2)}) copy-start(f32[1,48]{0,1:T(8,128)} %copy.58) | copy-start | bytes 580
  46.3 18.7 %copy-start.17 = (f32[1,48]{0,1:T(8,128)S(1)}, f32[1,48]{0,1:T(8,128)}, u32[]{:S(2)}) copy-start(f32[1,48]{0,1:T(8,128)} %copy.61) | copy-start | bytes 580
  46.4 20.1 %copy-start.16 = (f32[1,48]{0,1:T(8,128)S(1)}, f32[1,48]{0,1:T(8,128)}, u32[]{:S(2)}) copy-start(f32[1,48]{0,1:T(8,128)} %copy.62) | copy-start | bytes 580
  46.4 20.2 %copy-start.15 = (f32[1,48]{0,1:T(8,128)S(1)}, f32[1,48]{0,1:T(8,128)}, u32[]{:S(2)}) copy-start(f32[1,48]{0,1:T(8,128)} %copy.65) | copy-start | bytes 580
  46.4 16.2 %collective-permute-start.7 = (f32[20,5,1,48]{0,3,2,1:T(8,128)S(1)}, f32[20,5,1,48]{0,3,2,1:T(8,128)S(1)}, u32[]{:S(2)}, u32[]{:S(2)}) collective-permute-start(f32[20,5,1,48]{0,3,2,1:T(8,128)S(1)} %get-tuple-element.20), channel_id=1, source_target_pairs={{1,0},{2,1},{3,2},{4,3},{5,4},{6,5},{7,6},{8,7},{9,8},{10,9},{11,1... | collective-permute-start | bytes 57608 | tf_op jit(solution)/shard_map/ppermute | solution.py:21
  51.3 15.3 %copy-start.14 = (f32[1,48]{0,1:T(8,128)S(1)}, f32[1,48]{0,1:T(8,128)}, u32[]{:S(2)}) copy-start(f32[1,48]{0,1:T(8,128)} %copy.64) | copy-start | bytes 580
  51.3 11.3 %collective-permute-start.6 = (f32[20,5,1,48]{0,3,2,1:T(8,128)S(1)}, f32[20,5,1,48]{0,3,2,1:T(8,128)S(1)}, u32[]{:S(2)}, u32[]{:S(2)}) collective-permute-start(f32[20,5,1,48]{0,3,2,1:T(8,128)S(1)} %get-tuple-element.19), channel_id=1, source_target_pairs={{0,1},{1,2},{2,3},{3,4},{4,5},{5,6},{6,7},{7,8},{8,9},{9,10},{10,1... | collective-permute-start | bytes 57608 | tf_op jit(solution)/shard_map/ppermute | solution.py:18
  54.0 338.9 %collective-permute-start.3 = (f32[8,18,1]{2,1,0:T(8,128)}, f32[8,18,1]{2,1,0:T(8,128)}, u32[]{:S(2)}, u32[]{:S(2)}) collective-permute-start(f32[8,18,1]{2,1,0:T(8,128)} %get-tuple-element.51), channel_id=1, source_target_pairs={{0,1},{1,2},{2,3},{3,4},{4,5},{5,6},{6,7},{7,8},{8,9},{9,10},{10,1... | collective-permute-start | bytes 1736 | tf_op jit(solution)/shard_map/ppermute | solution.py:18
  55.9 337.0 %collective-permute-start.2 = (f32[8,18,1]{2,1,0:T(8,128)}, f32[8,18,1]{2,1,0:T(8,128)}, u32[]{:S(2)}, u32[]{:S(2)}) collective-permute-start(f32[8,18,1]{2,1,0:T(8,128)} %get-tuple-element.50), channel_id=1, source_target_pairs={{1,0},{2,1},{3,2},{4,3},{5,4},{6,5},{7,6},{8,7},{9,8},{10,9},{11,1... | collective-permute-start | bytes 1736 | tf_op jit(solution)/shard_map/ppermute | solution.py:21
  285.0 32.3 %copy-start.12 = (f32[6144]{0:T(1024)S(1)}, f32[6144]{0:T(1024)}, u32[]{:S(2)}) copy-start(f32[6144]{0:T(1024)} %get-tuple-element.28) | copy-start | bytes 73732
  285.0 32.3 %copy-start.13 = (f32[6144]{0:T(1024)S(1)}, f32[6144]{0:T(1024)}, u32[]{:S(2)}) copy-start(f32[6144]{0:T(1024)} %get-tuple-element.30) | copy-start | bytes 73732
  388.6 4.3 copy-start.20
  388.6 4.3 copy-start.22
  388.6 4.3 copy-start.43
  390.5 25.8 %copy-start.11 = (f32[1,1,48,128]{3,2,1,0:T(8,128)S(1)}, f32[1,1,48,128]{3,2,1,0:T(8,128)}, u32[]{:S(2)}) copy-start(f32[1,1,48,128]{3,2,1,0:T(8,128)} %get-tuple-element.38) | copy-start | bytes 73732
  395.0 46.9 %copy-start.10 = (f32[1,1,48,128]{3,2,1,0:T(8,128)S(1)}, f32[1,1,48,128]{3,2,1,0:T(8,128)}, u32[]{:S(2)}) copy-start(f32[1,1,48,128]{3,2,1,0:T(8,128)} %get-tuple-element.37) | copy-start | bytes 73732
  421.0 46.5 %copy-start.9 = (f32[1,1,48,128]{3,2,1,0:T(8,128)S(1)}, f32[1,1,48,128]{3,2,1,0:T(8,128)}, u32[]{:S(2)}) copy-start(f32[1,1,48,128]{3,2,1,0:T(8,128)} %get-tuple-element.36) | copy-start | bytes 73732
  446.6 46.5 %copy-start.8 = (f32[1,1,48,128]{3,2,1,0:T(8,128)S(1)}, f32[1,1,48,128]{3,2,1,0:T(8,128)}, u32[]{:S(2)}) copy-start(f32[1,1,48,128]{3,2,1,0:T(8,128)} %get-tuple-element.35) | copy-start | bytes 73732
  472.2 46.7 %copy-start.7 = (f32[1,1,48,128]{3,2,1,0:T(8,128)S(1)}, f32[1,1,48,128]{3,2,1,0:T(8,128)}, u32[]{:S(2)}) copy-start(f32[1,1,48,128]{3,2,1,0:T(8,128)} %get-tuple-element.34) | copy-start | bytes 73732
  497.8 46.7 %copy-start.6 = (f32[1,1,48,128]{3,2,1,0:T(8,128)S(1)}, f32[1,1,48,128]{3,2,1,0:T(8,128)}, u32[]{:S(2)}) copy-start(f32[1,1,48,128]{3,2,1,0:T(8,128)} %get-tuple-element.33) | copy-start | bytes 73732
  523.6 46.5 %copy-start.5 = (f32[1,1,48,128]{3,2,1,0:T(8,128)S(1)}, f32[1,1,48,128]{3,2,1,0:T(8,128)}, u32[]{:S(2)}) copy-start(f32[1,1,48,128]{3,2,1,0:T(8,128)} %get-tuple-element.32) | copy-start | bytes 73732
  549.2 46.5 %copy-start.4 = (f32[1,1,48,128]{3,2,1,0:T(8,128)S(1)}, f32[1,1,48,128]{3,2,1,0:T(8,128)}, u32[]{:S(2)}) copy-start(f32[1,1,48,128]{3,2,1,0:T(8,128)} %get-tuple-element.31) | copy-start | bytes 73732
  574.8 46.9 %copy-start.3 = (f32[1,1,48,128]{3,2,1,0:T(8,128)S(1)}, f32[1,1,48,128]{3,2,1,0:T(8,128)}, u32[]{:S(2)}) copy-start(f32[1,1,48,128]{3,2,1,0:T(8,128)} %get-tuple-element.21) | copy-start | bytes 73732
  600.3 26.0 %copy-start.33 = (f32[48]{0:T(128)S(1)}, f32[48]{0:T(128)}, u32[]{:S(2)}) copy-start(f32[48]{0:T(128)} %get-tuple-element.9) | copy-start | bytes 580
  600.4 26.0 %copy-start.42 = (f32[48]{0:T(128)S(1)}, f32[48]{0:T(128)}, u32[]{:S(2)}) copy-start(f32[48]{0:T(128)} %get-tuple-element.63) | copy-start | bytes 580
  600.4 26.1 %copy-start.32 = (f32[48]{0:T(128)S(1)}, f32[48]{0:T(128)}, u32[]{:S(2)}) copy-start(f32[48]{0:T(128)} %get-tuple-element.10) | copy-start | bytes 580
  600.4 26.1 %copy-start.41 = (f32[48]{0:T(128)S(1)}, f32[48]{0:T(128)}, u32[]{:S(2)}) copy-start(f32[48]{0:T(128)} %get-tuple-element.64) | copy-start | bytes 580
  600.4 26.1 %copy-start.31 = (f32[48]{0:T(128)S(1)}, f32[48]{0:T(128)}, u32[]{:S(2)}) copy-start(f32[48]{0:T(128)} %get-tuple-element.11) | copy-start | bytes 580
  600.4 26.1 %copy-start.40 = (f32[48]{0:T(128)S(1)}, f32[48]{0:T(128)}, u32[]{:S(2)}) copy-start(f32[48]{0:T(128)} %get-tuple-element.65) | copy-start | bytes 580
  600.4 26.1 %copy-start.30 = (f32[48]{0:T(128)S(1)}, f32[48]{0:T(128)}, u32[]{:S(2)}) copy-start(f32[48]{0:T(128)} %get-tuple-element.12) | copy-start | bytes 580
  600.4 26.1 %copy-start.39 = (f32[48]{0:T(128)S(1)}, f32[48]{0:T(128)}, u32[]{:S(2)}) copy-start(f32[48]{0:T(128)} %get-tuple-element.66) | copy-start | bytes 580
  600.4 26.1 %copy-start.29 = (f32[48]{0:T(128)S(1)}, f32[48]{0:T(128)}, u32[]{:S(2)}) copy-start(f32[48]{0:T(128)} %get-tuple-element.13) | copy-start | bytes 580
  600.4 26.1 %copy-start.38 = (f32[48]{0:T(128)S(1)}, f32[48]{0:T(128)}, u32[]{:S(2)}) copy-start(f32[48]{0:T(128)} %get-tuple-element.67) | copy-start | bytes 580
  600.4 26.1 %copy-start.28 = (f32[48]{0:T(128)S(1)}, f32[48]{0:T(128)}, u32[]{:S(2)}) copy-start(f32[48]{0:T(128)} %get-tuple-element.14) | copy-start | bytes 580
  600.4 26.1 %copy-start.37 = (f32[48]{0:T(128)S(1)}, f32[48]{0:T(128)}, u32[]{:S(2)}) copy-start(f32[48]{0:T(128)} %get-tuple-element.68) | copy-start | bytes 580
  600.4 26.1 %copy-start.27 = (f32[48]{0:T(128)S(1)}, f32[48]{0:T(128)}, u32[]{:S(2)}) copy-start(f32[48]{0:T(128)} %get-tuple-element.15) | copy-start | bytes 580
  600.5 26.1 %copy-start.36 = (f32[48]{0:T(128)S(1)}, f32[48]{0:T(128)}, u32[]{:S(2)}) copy-start(f32[48]{0:T(128)} %get-tuple-element.69) | copy-start | bytes 580
  600.5 26.2 %copy-start.26 = (f32[48]{0:T(128)S(1)}, f32[48]{0:T(128)}, u32[]{:S(2)}) copy-start(f32[48]{0:T(128)} %get-tuple-element.16) | copy-start | bytes 580
  600.5 26.2 %copy-start.35 = (f32[48]{0:T(128)S(1)}, f32[48]{0:T(128)}, u32[]{:S(2)}) copy-start(f32[48]{0:T(128)} %get-tuple-element.70) | copy-start | bytes 580
  600.5 26.2 %copy-start.25 = (f32[48]{0:T(128)S(1)}, f32[48]{0:T(128)}, u32[]{:S(2)}) copy-start(f32[48]{0:T(128)} %get-tuple-element.8) | copy-start | bytes 580
  600.5 26.2 %copy-start.34 = (f32[48]{0:T(128)S(1)}, f32[48]{0:T(128)}, u32[]{:S(2)}) copy-start(f32[48]{0:T(128)} %get-tuple-element.62) | copy-start | bytes 580
  626.8 6.6 %collective-permute-start.12 = (f32[9,1,3,48]{3,2,1,0:T(4,128)S(1)}, f32[9,1,3,48]{3,2,1,0:T(4,128)S(1)}, u32[]{:S(2)}, u32[]{:S(2)}) collective-permute-start(f32[9,1,3,48]{3,2,1,0:T(4,128)S(1)} %get-tuple-element.57), channel_id=1, source_target_pairs={{0,64},{64,128},{128,192},{192,256},{256,320},{320,384},{384,448},... | collective-permute-start | bytes 15560 | tf_op jit(solution)/shard_map/ppermute | solution.py:18
  631.5 6.3 collective-permute-start.13
  637.8 5.6 collective-permute-start.15
  641.5 7.9 %collective-permute-start.14 = (f32[9,5,1,48]{3,2,1,0:T(1,128)S(1)}, f32[9,5,1,48]{3,2,1,0:T(1,128)S(1)}, u32[]{:S(2)}, u32[]{:S(2)}) collective-permute-start(f32[9,5,1,48]{3,2,1,0:T(1,128)S(1)} %get-tuple-element.52), channel_id=1, source_target_pairs={{0,1},{1,2},{2,3},{3,4},{4,5},{5,6},{6,7},{7,8},{8,9},{9,10},{10,1... | collective-permute-start | bytes 25928 | tf_op jit(solution)/shard_map/ppermute | solution.py:18
where the time goes:
time: 663 us; the launch traced here: 654 us
  other arithmetic  340 us (51%)
  local copies, waits for them, and re-layouts  205 us (31%)
  starting transfers between devices  51.5 us (8%)
  matrix products  44 us (7%)
  waiting for transfers between devices  11.5 us (2%)
    scatter-add x9, other arithmetic, on_device(): totals_tile = totals_tile.at[:, cell_ids].add(contrib)  307 us
    gather x9, local copies, waits for them, and re-layouts, on_device(): gathered = surface[:, cell_ids]  189 us
    dot_general x9, matrix products, on_device(): jnp.einsum('ksw,sw->ks', gathered, weights[row_shift, col_shift], precisi...  41.7 us
    ppermute x8, starting transfers between devices, padded_2(): lax.ppermute(lax.slice_in_dim(block, 0, width, axis=dim), axis, backward)  27.3 us
    ppermute x8, starting transfers between devices, padded_2(): lax.ppermute(lax.slice_in_dim(block, block.shape[dim] - width, None, axis...  24.2 us
    mul x5, other arithmetic, on_device(): stacked[:, :, None] * weights[row_shift, col_shift][None]  15.7 us
  transfers between devices with their start and end apart: 16, of which 3 were waited for; matrix products, arithmetic and copies ran while one was open for 54% of the time, Pallas kernels for 0%

commit v1 on v0

v1 whole, which is shorter than its diff:
```python
import jax
import jax.numpy as jnp
from jax import lax
from jax.experimental import pallas as pl
from jax.experimental.pallas import tpu as pltpu
from jax.sharding import PartitionSpec as P

WIN_R = 8
WIN_C = 16
OFF = 64
VMEM = pl.BlockSpec(memory_space=pltpu.VMEM)
SMEM = pl.BlockSpec(memory_space=pltpu.SMEM)
F32 = jnp.float32
BF16 = jnp.bfloat16
NT = (((1,), (1,)), ((), ()))


def lanes_of(shape):
    return lax.broadcasted_iota(jnp.int32, shape, 1)


def halves(value):
    high = value.astype(BF16)
    low = (value - high.astype(F32)).astype(BF16)
    return high, low


def pack_kernel(flux, index, count, coupling, state, parity, send1, send2, own, index_scr, flux_scr):
    slots = index.shape[2]
    even = parity[0] == 0
    index_scr[...] = jnp.zeros_like(index_scr)
    for i in range(9):
        index_scr[i : i + 1, 0:slots] = index[i]
    flux_scr[...] = jnp.zeros_like(flux_scr)
    flux_scr[:, 0 : flux.shape[1]] = lax.dot_general(
        coupling[...], flux[...], (((1,), (0,)), ((), ())),
        precision=lax.Precision.HIGHEST, preferred_element_type=F32,
    )
    mapped = flux_scr[...]
    lane = lanes_of(mapped.shape)
    groups = []
    for a in range(3):
        for b in range(3):
            used = count[a, 0, b]
            places = jnp.broadcast_to(index_scr[3 * a + b : 3 * a + b + 1, :], mapped.shape)
            picked = jnp.take_along_axis(mapped, places, axis=1)
            flag = ((lane >= OFF) & (lane < OFF + used)).astype(F32)
            groups.append(jnp.where(lane < used, picked, flag))
    rows = state.shape[0] // 8
    for b in range(3):
        up, down = groups[6 + b], groups[b]
        send1[b] = jnp.where(even, up, down)
        send2[b] = jnp.where(even, down, up)
        own[b] = groups[3 + b]
    first = state[pl.ds(0, 8, stride=rows), :]
    last = state[pl.ds(rows - 1, 8, stride=rows), :]
    send1[3] = jnp.where(even, last, first)
    send2[3] = jnp.where(even, first, last)
    west = jnp.zeros_like(mapped)
    east = jnp.zeros_like(mapped)
    width = state.shape[1]
    for y in range(rows):
        line = state[pl.ds(y, 8, stride=rows), :]
        west = jnp.where(lane == y, jnp.broadcast_to(line[:, 0:1], mapped.shape), west)
        east = jnp.where(lane == y, jnp.broadcast_to(line[:, width - 1 : width], mapped.shape), east)
    own[3] = west
    own[4] = east


def spread_kernel(start, weight, high, low, start_scr):
    slots, width = weight.shape[3], weight.shape[4]
    rows = high.shape[1] // width
    start_scr[...] = jnp.zeros_like(start_scr)
    for i in range(9):
        start_scr[i : i + 1, 0:slots] = start[i].astype(F32)
    turned = start_scr[...].T
    lane = lanes_of((slots, width))
    for p in range(3):
        for q in range(3):
            i = 3 * p + q
            first = turned[0:slots, i : i + 1].astype(jnp.int32)
            top = first // width
            left = jnp.broadcast_to(first - top * width, (slots, width))
            above = jnp.broadcast_to(top * WIN_C, (slots, width))
            across = lane - left
            inside = (across >= 0) & (across < WIN_C)
            place = jnp.where(inside, across - above, -(1 << 20))
            block = weight[0, p, q]
            for y in range(rows):
                at = place + y * WIN_C
                hit = (at >= 0) & (at < WIN_R * WIN_C)
                value = jnp.take_along_axis(block, at & (width - 1), axis=1)
                value = jnp.where(hit, value, 0.0)
                part, rest = halves(value)
                high[i * slots : (i + 1) * slots, y * width : (y + 1) * width] = part
                low[i * slots : (i + 1) * slots, y * width : (y + 1) * width] = rest


def ocean_kernel(
    row1, row2, col1, col2, own, parity, high, low, state, velocity, diffusivity, wet,
    new_state, send1, send2, back_own, surface,
):
    slots = high.shape[0] // 9
    width = state.shape[1]
    rows = state.shape[0] // 8
    even_r = parity[0] == 0
    even_c = parity[1] == 0

    def from_plus(one, two, even, i):
        return jnp.where(even, one[i], two[i])

    def from_minus(one, two, even, i):
        return jnp.where(even, two[i], one[i])

    middle = [from_minus(row1, row2, even_r, 1), own[1], from_plus(row1, row2, even_r, 1)]
    blocks = []
    for p in range(3):
        blocks += [from_minus(col1, col2, even_c, p), middle[p], from_plus(col1, col2, even_c, p)]
    south_edge = from_minus(row1, row2, even_r, 3)
    north_edge = from_plus(row1, row2, even_r, 3)
    west_edge = from_minus(col1, col2, even_c, 3)
    east_edge = from_plus(col1, col2, even_c, 3)

    fields = jnp.concatenate([block[:, 0:slots] for block in blocks], axis=1)
    flags = jnp.concatenate([block[:, OFF : OFF + slots] for block in blocks], axis=1)
    first_row = lax.broadcasted_iota(jnp.int32, flags.shape, 0) == 0
    flags = jnp.where(first_row, flags, 0.0)
    field_high = fields.astype(BF16).astype(F32)
    field_low = fields - field_high
    left_high = jnp.concatenate([field_high, flags], axis=0).astype(BF16)
    left_low = jnp.concatenate([field_low, jnp.zeros_like(flags)], axis=0).astype(BF16)
    left = jnp.concatenate([left_high, left_low], axis=0)

    lane = lanes_of((8, width))
    row_of = lax.broadcasted_iota(jnp.int32, (8, width), 0)
    one_row = jnp.where(row_of == 0, 1.0, 0.0)
    spread = jnp.zeros((8, width), F32)
    for k in range(8):
        spread = jnp.where(row_of == k, diffusivity[k], spread)
    step = 2 * width
    lines = [state[pl.ds(y, 8, stride=rows), :] for y in range(rows)]
    for part in range(rows // 2):
        cells = slice(part * step, (part + 1) * step)
        sums = jnp.dot(left, high[:, cells], preferred_element_type=F32)
        sums = sums[0:16] + sums[16:32] + jnp.dot(left_high, low[:, cells], preferred_element_type=F32)
        for y in (2 * part, 2 * part + 1):
            at = slice((y % 2) * width, (y % 2 + 1) * width)
            cover = sums[8:9, at]
            forcing = sums[0:8, at] / jnp.maximum(jnp.broadcast_to(cover, (8, width)), 1.0)
            here = lines[y]
            north = lines[y + 1] if y + 1 < rows else north_edge
            south = lines[y - 1] if y > 0 else south_edge
            east = pltpu.roll(here, width - 1, 1)
            east = jnp.where(lane == width - 1, jnp.broadcast_to(east_edge[:, y : y + 1], (8, width)), east)
            west = pltpu.roll(here, 1, 1)
            west = jnp.where(lane == 0, jnp.broadcast_to(west_edge[:, y : y + 1], (8, width)), west)
            laplace = east + west + north + south - 4.0 * here
            along = jnp.broadcast_to(velocity[0, y : y + 1, :], (8, width))
            across = jnp.broadcast_to(velocity[1, y : y + 1, :], (8, width))
            advect = 0.5 * (along * (east - west) + across * (north - south))
            mask = jnp.broadcast_to(wet[y : y + 1, :], (8, width)).astype(F32)
            fresh = here + mask * (spread * laplace - advect + forcing)
            new_state[pl.ds(y, 8, stride=rows), :] = fresh
            seen = fresh * mask
            seen_high = seen.astype(BF16).astype(F32)
            column = slice(y * width, (y + 1) * width)
            surface[0:16, column] = jnp.concatenate([seen_high, one_row], axis=0).astype(BF16)
            surface[16:32, column] = jnp.concatenate([seen - seen_high, jnp.zeros_like(seen)], axis=0).astype(BF16)
    back = lax.dot_general(surface[...], high[...], NT, preferred_element_type=F32)
    back = back[0:16] + back[16:32] + lax.dot_general(
        surface[0:16, :], low[...], NT, preferred_element_type=F32
    )
    pad = jnp.zeros((8, OFF - slots), F32)
    out = []
    for i in range(9):
        at = slice(i * slots, (i + 1) * slots)
        out.append(jnp.concatenate([back[0:8, at], pad, back[8:16, at], pad], axis=1))
    for q in range(3):
        up, down = out[6 + q], out[q]
        send1[q] = jnp.where(even_r, up, down)
        send2[q] = jnp.where(even_r, down, up)
        back_own[q] = out[3 + q]


def surface_kernel(row1, row2, col1, col2, own, parity, index, count, result, index_scr):
    slots = index.shape[2]
    cells = result.shape[1]
    even_r = parity[0] == 0
    even_c = parity[1] == 0
    index_scr[...] = jnp.zeros_like(index_scr)
    for i in range(9):
        index_scr[i : i + 1, 0:slots] = index[i]
    middle = [
        jnp.where(even_r, row2[1], row1[1]),
        own[1],
        jnp.where(even_r, row1[1], row2[1]),
    ]
    width = own.shape[2]
    lane = lanes_of((8, width))
    cell = lax.broadcasted_iota(jnp.int32, (cells, width), 0)
    total = jnp.zeros((32, cells), F32)
    for a in range(3):
        group = [
            jnp.where(even_c, col2[a], col1[a]),
            middle[a],
            jnp.where(even_c, col1[a], col2[a]),
        ]
        for b in range(3):
            used = lane < count[a, 0, b]
            block = group[b]
            value = jnp.where(used, block, 0.0)
            weights = jnp.where(used, pltpu.roll(block, OFF, 1), 0.0)
            left = jnp.concatenate([value, weights], axis=0)
            left_high = left.astype(BF16).astype(F32)
            left = jnp.concatenate([left_high, left - left_high], axis=0).astype(BF16)
            places = jnp.broadcast_to(index_scr[3 * a + b : 3 * a + b + 1, :], (cells, width))
            hot = (places == cell).astype(F32).astype(BF16)
            total = total + lax.dot_general(left, hot, NT, preferred_element_type=F32)
    total = total[0:16] + total[16:32]
    cover = jnp.maximum(jnp.broadcast_to(total[8:9], (8, cells)), 1.0)
    result[...] = total[0:8] / cover


def swaps(count):
    near = [(i, i ^ 1) for i in range(count)]
    far = [(i, i + 1) for i in range(1, count - 1, 2)]
    far = far + [(j, i) for i, j in far]
    return near, far


def exchange(send1, send2, axis):
    near, far = swaps(lax.axis_size(axis))
    two = lax.ppermute(send2, axis, far)
    one = lax.ppermute(send1, axis, near)
    return one, two


def column_sends(row1, row2, own, extra, even_r, even_c):
    minus = jnp.where(even_r, row2, row1)
    plus = jnp.where(even_r, row1, row2)
    low = jnp.stack([minus[0], own[0], plus[0]] + [edge for edge in extra[:1]])
    high = jnp.stack([minus[2], own[2], plus[2]] + [edge for edge in extra[1:]])
    return jnp.where(even_c, high, low), jnp.where(even_c, low, high)


def call(kernel, outs, scratch, specs, flops, size, *args, name):
    return pl.pallas_call(
        kernel,
        out_shape=outs,
        in_specs=specs,
        out_specs=[VMEM] * len(outs),
        scratch_shapes=scratch,
        compiler_params=pltpu.CompilerParams(vmem_limit_bytes=24 * 1024 * 1024),
        cost_estimate=pl.CostEstimate(flops=flops, bytes_accessed=size, transcendentals=0),
        name=name,
    )(*args)


def on_device(
    atm_flux,
    send_index,
    send_count,
    block_start,
    remap_weight,
    coupling,
    ocean_state,
    velocity,
    diffusivity,
    wet_mask,
):
    fields, rows, width = ocean_state.shape
    slots = send_index.shape[3]
    cells = rows * width
    parity = jnp.stack([lax.axis_index("row") % 2, lax.axis_index("col") % 2]).astype(jnp.int32)
    even_r = parity[0] == 0
    even_c = parity[1] == 0
    state = ocean_state.reshape(fields * rows, width)
    index = send_index.reshape(9, 1, slots)
    count = send_count.reshape(3, 1, 3)
    start = block_start.reshape(9, 1, slots)

    def shape(*dims, dtype=F32):
        return jax.ShapeDtypeStruct(dims, dtype)

    send1, send2, own = call(
        pack_kernel,
        [shape(4, 8, width), shape(4, 8, width), shape(5, 8, width)],
        [pltpu.VMEM((16, width), jnp.int32), pltpu.VMEM((8, width), F32)],
        [VMEM, VMEM, SMEM, VMEM, VMEM, SMEM],
        100_000, 200_000,
        atm_flux, index, count, coupling, state, parity,
        name="pack",
    )
    row1, row2 = exchange(send1, send2, "row")
    high, low = call(
        spread_kernel,
        [shape(9 * slots, cells, dtype=BF16), shape(9 * slots, cells, dtype=BF16)],
        [pltpu.VMEM((16, width), F32)],
        [VMEM, VMEM],
        20_000_000, 4_000_000,
        start, remap_weight,
        name="spread",
    )
    send1, send2 = column_sends(row1, row2, own, [own[3], own[4]], even_r, even_c)
    col1, col2 = exchange(send1, send2, "col")
    new_state, send1, send2, own = call(
        ocean_kernel,
        [shape(fields * rows, width), shape(3, 8, width), shape(3, 8, width), shape(3, 8, width)],
        [pltpu.VMEM((32, cells), BF16)],
        [VMEM] * 5 + [SMEM] + [VMEM] * 4 + [SMEM, VMEM],
        100_000_000, 4_000_000,
        row1, row2, col1, col2, own, parity, high, low, state, velocity,
        diffusivity, wet_mask,
        name="ocean",
    )
    row1, row2 = exchange(send1, send2, "row")
    send1, send2 = column_sends(row1, row2, own, [], even_r, even_c)
    col1, col2 = exchange(send1, send2, "col")
    (result,) = call(
        surface_kernel,
        [shape(fields, atm_flux.shape[1])],
        [pltpu.VMEM((16, width), jnp.int32)],
        [VMEM, VMEM, VMEM, VMEM, VMEM, SMEM, VMEM, SMEM],
        1_000_000, 200_000,
        row1, row2, col1, col2, own, parity, index, count,
        name="surface",
    )
    return new_state.reshape(ocean_state.shape), result


def solution(mesh):
    return jax.shard_map(
        on_device,
        mesh=mesh,
        in_specs=(
            P(None, ("row", "col")),
            P(("row", "col"), None, None, None),
            P(("row", "col"), None, None),
            P(("row", "col"), None, None, None),
            P(("row", "col"), None, None, None, None),
            P(),
            P(None, "row", "col"),
            P(None, "row", "col"),
            P(),
            P("row", "col"),
        ),
        out_specs=(P(None, "row", "col"), P(None, ("row", "col"))),
        check_vma=False,
    )
```

time: 663 us -> 55 us (0.08)
  the two profiles are of different devices: /device:TPU:561 before, /device:TPU:1 now
where the time goes in v1:
time: 55 us; the launch traced here: 54.3 us
  starting transfers between devices  29.7 us (54%)
  Pallas kernels  8.31 us (15%)
  local copies, waits for them, and re-layouts  8.15 us (15%)
  waiting for transfers between devices  7.23 us (13%)
  between operations  0.84 us (2%)
    ppermute x4, starting transfers between devices, exchange(): one = lax.ppermute(send1, axis, near)  24.5 us
    pallas_call x4, Pallas kernels, call(): pl.pallas_call(kernel, out_shape=outs, in_specs=specs, out_specs=[VMEM] *...  8.31 us
    unnamed x26, local copies, waits for them, and re-layouts  8.13 us
    ppermute x4, waiting for transfers between devices, exchange(): two = lax.ppermute(send2, axis, far)  6.16 us
    ppermute x4, starting transfers between devices, exchange(): two = lax.ppermute(send2, axis, far)  5.17 us
  transfers between devices with their start and end apart: 8, of which 3 were waited for; matrix products, arithmetic and copies ran while one was open for 0% of the time, Pallas kernels for 6%

profile of v1, /device:TPU:1, one launch (start us, length us, event | category | flops | bytes accessed | tf_op | source)
XLA Modules:
  0.0 54.3 jit_solution(9230287178958250128)
XLA Ops:
  0.6 0.1 pad_add_fusion.parity
  0.7 0.0 copy-start
  0.7 0.8 %copy-done = f32[8,16,128]{2,1,0:T(8,128)S(1)} copy-done((f32[8,16,128]{2,1,0:T(8,128)S(1)}, f32[8,16,128]{2,1,0:T(8,128)}, u32[]{:S(2)}) %copy-start) | copy-done | bytes 65560
  1.6 0.0 copy-start.3
  1.6 0.7 %copy-done.3 = s32[1,3,3,48]{3,0,2,1:T(1,128)S(1)} copy-done((s32[1,3,3,48]{3,0,2,1:T(1,128)S(1)}, s32[1,3,3,48]{3,0,2,1:T(1,128)}, u32[]{:S(2)}) %copy-start.3) | copy-done | bytes 1752
  2.3 0.0 copy-start.6
  2.3 0.7 %copy-done.6 = f32[20,96]{1,0:T(8,128)S(1)} copy-done((f32[20,96]{1,0:T(8,128)S(1)}, f32[20,96]{1,0:T(8,128)}, u32[]{:S(2)}) %copy-start.6) | copy-done | bytes 7704
  3.0 0.0 copy-start.8
  3.0 0.7 %copy-done.8 = s32[1,3,3]{2,0,1:T(1,128)S(1)} copy-done((s32[1,3,3]{2,0,1:T(1,128)S(1)}, s32[1,3,3]{2,0,1:T(1,128)}, u32[]{:S(2)}) %copy-start.8) | copy-done | bytes 60
  3.6 0.0 copy-start.11
  3.6 0.7 %copy-done.11 = f32[8,20]{1,0:T(8,128)S(1)} copy-done((f32[8,20]{1,0:T(8,128)S(1)}, f32[8,20]{1,0:T(8,128)}, u32[]{:S(2)}) %copy-start.11) | copy-done | bytes 664
  4.3 0.8 %pack.1 = (f32[4,8,128]{2,1,0:T(8,128)S(1)}, f32[4,8,128]{2,1,0:T(8,128)S(1)}, f32[5,8,128]{2,1,0:T(8,128)S(1)}) custom-call(f32[20,96]{1,0:T(8,128)S(1)} %copy-done.6, s32[9,1,48]{2,1,0:T(1,128)S(1)} %bitcast.9, s32[3,1,3]{2,1,0:T(1,128)S(1)} %bitcast.11, f32[8,20]{1,0:T(8,128)S(1)} %copy-done.11, f32[128,128]{1,0:T(8,128)S(1)} %bitcast.7, ...), custom_call_target="tpu_custom_call" | custom-call | flops 100000 | bytes 200000 | tf_op jit(solution)/shard_map/pack/pallas_call | solution.py:247
  5.1 16.1 %collective-permute-start = (f32[4,8,128]{2,1,0:T(8,128)S(1)}, f32[4,8,128]{2,1,0:T(8,128)S(1)}, u32[]{:S(2)}, u32[]{:S(2)}) collective-permute-start(f32[4,8,128]{2,1,0:T(8,128)S(1)} %get-tuple-element.11), channel_id=1, source_target_pairs={{0,64},{64,0},{128,192},{192,128},{256,320},{320,256},{384,448},{4... | collective-permute-start | bytes 49160 | tf_op jit(solution)/shard_map/ppermute | solution.py:234
  21.2 1.9 %collective-permute-start.1 = (f32[4,8,128]{2,1,0:T(8,128)S(1)}, f32[4,8,128]{2,1,0:T(8,128)S(1)}, u32[]{:S(2)}, u32[]{:S(2)}) collective-permute-start(f32[4,8,128]{2,1,0:T(8,128)S(1)} %get-tuple-element.12), channel_id=1, source_target_pairs={{64,128},{192,256},{320,384},{448,512},{576,640},{704,768},{832,89... | collective-permute-start | bytes 49160 | tf_op jit(solution)/shard_map/ppermute | solution.py:233
  23.1 0.0 collective-permute-done.row1
  23.2 3.1 %collective-permute-done.1.row2 = f32[4,8,128]{2,1,0:T(8,128)S(1)} collective-permute-done((f32[4,8,128]{2,1,0:T(8,128)S(1)}, f32[4,8,128]{2,1,0:T(8,128)S(1)}, u32[]{:S(2)}, u32[]{:S(2)}) %collective-permute-start.1) | collective-permute-done | bytes 16416 | tf_op jit(solution)/shard_map/ppermute | solution.py:233
  26.3 0.7 %collective-permute-start.3 = (f32[4,8,128]{2,1,0:T(8,128)S(1)}, f32[4,8,128]{2,1,0:T(8,128)S(1)}, u32[]{:S(2)}, u32[]{:S(2)}) collective-permute-start(f32[4,8,128]{2,1,0:T(8,128)S(1)} %get-tuple-element.20), channel_id=1, source_target_pairs={{1,2},{3,4},{5,6},{7,8},{9,10},{11,12},{13,14},{15,16},{17,18},{19... | collective-permute-start | bytes 49160 | tf_op jit(solution)/shard_map/ppermute | solution.py:233
  26.9 1.9 %collective-permute-start.2 = (f32[4,8,128]{2,1,0:T(8,128)S(1)}, f32[4,8,128]{2,1,0:T(8,128)S(1)}, u32[]{:S(2)}, u32[]{:S(2)}) collective-permute-start(f32[4,8,128]{2,1,0:T(8,128)S(1)} %get-tuple-element.21), channel_id=1, source_target_pairs={{0,1},{1,0},{2,3},{3,2},{4,5},{5,4},{6,7},{7,6},{8,9},{9,8},{10,11... | collective-permute-start | bytes 49160 | tf_op jit(solution)/shard_map/ppermute | solution.py:234
  28.9 0.0 copy-start.2
  28.9 0.9 %copy-done.2 = f32[1,3,3,48,128]{4,3,2,1,0:T(8,128)S(1)} copy-done((f32[1,3,3,48,128]{4,3,2,1,0:T(8,128)S(1)}, f32[1,3,3,48,128]{4,3,2,1,0:T(8,128)}, u32[]{:S(2)}) %copy-start.2) | copy-done | bytes 221208
  29.8 0.0 copy-start.10
  29.8 0.7 %copy-done.10 = s32[1,3,3,48]{3,0,2,1:T(1,128)S(1)} copy-done((s32[1,3,3,48]{3,0,2,1:T(1,128)S(1)}, s32[1,3,3,48]{3,0,2,1:T(1,128)}, u32[]{:S(2)}) %copy-start.10) | copy-done | bytes 1752
  30.5 3.3 %spread.1 = (bf16[432,2048]{1,0:T(8,128)(2,1)S(1)}, bf16[432,2048]{1,0:T(8,128)(2,1)S(1)}) custom-call(s32[9,1,48]{2,1,0:T(1,128)S(1)} %bitcast.13, f32[1,3,3,48,128]{4,3,2,1,0:T(8,128)S(1)} %copy-done.2), custom_call_target="tpu_custom_call" | custom-call | flops 20000000 | bytes 4000000 | tf_op jit(solution)/shard_map/spread/pallas_call | solution.py:247
  33.8 0.0 collective-permute-done.3.col2
  33.8 0.0 collective-permute-done.2.col1
  33.8 0.0 copy-start.1
  33.8 0.8 %copy-done.1 = f32[8,16,128]{2,1,0:T(8,128)S(1)} copy-done((f32[8,16,128]{2,1,0:T(8,128)S(1)}, f32[8,16,128]{2,1,0:T(8,128)}, u32[]{:S(2)}) %copy-start.1) | copy-done | bytes 65560
  34.7 0.0 copy-start.5
  34.7 0.7 %copy-done.5 = f32[2,16,128]{2,1,0:T(8,128)S(1)} copy-done((f32[2,16,128]{2,1,0:T(8,128)S(1)}, f32[2,16,128]{2,1,0:T(8,128)}, u32[]{:S(2)}) %copy-start.5) | copy-done | bytes 16408
  35.4 0.0 copy-start.7
  35.4 0.7 %copy-done.7 = s32[16,128]{1,0:T(8,128)S(1)} copy-done((s32[16,128]{1,0:T(8,128)S(1)}, s32[16,128]{1,0:T(8,128)}, u32[]{:S(2)}) %copy-start.7) | copy-done | bytes 8216
  36.1 0.0 copy-start.12
  36.1 0.7 %copy-done.12 = f32[8]{0:T(128)S(1)} copy-done((f32[8]{0:T(128)S(1)}, f32[8]{0:T(128)}, u32[]{:S(2)}) %copy-start.12) | copy-done | bytes 56
  36.7 0.0 copy-start.4
  36.7 0.0 copy-start.9
  36.7 2.8 %ocean.1 = (f32[128,128]{1,0:T(8,128)}, f32[3,8,128]{2,1,0:T(8,128)S(1)}, f32[3,8,128]{2,1,0:T(8,128)S(1)}, f32[3,8,128]{2,1,0:T(8,128)S(1)}) custom-call(f32[4,8,128]{2,1,0:T(8,128)S(1)} %collective-permute-done.row1, f32[4,8,128]{2,1,0:T(8,128)S(1)} %collective-permute-done.1.row2, f32[4,8,128]{2,1,0:T(8,128)S(1)} %collective-permute-done.2.col1, ...), custom_call_target="tpu_custom_call" | custom-call | flops 100000000 | bytes 4000000 | tf_op jit(solution)/shard_map/ocean/pallas_call | solution.py:247
  39.5 1.9 %collective-permute-start.4 = (f32[3,8,128]{2,1,0:T(8,128)S(1)}, f32[3,8,128]{2,1,0:T(8,128)S(1)}, u32[]{:S(2)}, u32[]{:S(2)}) collective-permute-start(f32[3,8,128]{2,1,0:T(8,128)S(1)} %get-tuple-element.17), channel_id=1, source_target_pairs={{0,64},{64,0},{128,192},{192,128},{256,320},{320,256},{384,448},{4... | collective-permute-start | bytes 36872 | tf_op jit(solution)/shard_map/ppermute | solution.py:234
  41.4 1.9 %collective-permute-start.5 = (f32[3,8,128]{2,1,0:T(8,128)S(1)}, f32[3,8,128]{2,1,0:T(8,128)S(1)}, u32[]{:S(2)}, u32[]{:S(2)}) collective-permute-start(f32[3,8,128]{2,1,0:T(8,128)S(1)} %get-tuple-element.18), channel_id=1, source_target_pairs={{64,128},{192,256},{320,384},{448,512},{576,640},{704,768},{832,89... | collective-permute-start | bytes 36872 | tf_op jit(solution)/shard_map/ppermute | solution.py:233
  43.4 0.0 collective-permute-done.4.row1
  43.4 3.1 %collective-permute-done.5.row2 = f32[3,8,128]{2,1,0:T(8,128)S(1)} collective-permute-done((f32[3,8,128]{2,1,0:T(8,128)S(1)}, f32[3,8,128]{2,1,0:T(8,128)S(1)}, u32[]{:S(2)}, u32[]{:S(2)}) %collective-permute-start.5) | collective-permute-done | bytes 12320 | tf_op jit(solution)/shard_map/ppermute | solution.py:233
  46.5 0.7 %collective-permute-start.7 = (f32[3,8,128]{2,1,0:T(8,128)S(1)}, f32[3,8,128]{2,1,0:T(8,128)S(1)}, u32[]{:S(2)}, u32[]{:S(2)}) collective-permute-start(f32[3,8,128]{2,1,0:T(8,128)S(1)} %get-tuple-element.24), channel_id=1, source_target_pairs={{1,2},{3,4},{5,6},{7,8},{9,10},{11,12},{13,14},{15,16},{17,18},{19... | collective-permute-start | bytes 36872 | tf_op jit(solution)/shard_map/ppermute | solution.py:233
  47.1 4.6 %collective-permute-start.6 = (f32[3,8,128]{2,1,0:T(8,128)S(1)}, f32[3,8,128]{2,1,0:T(8,128)S(1)}, u32[]{:S(2)}, u32[]{:S(2)}) collective-permute-start(f32[3,8,128]{2,1,0:T(8,128)S(1)} %get-tuple-element.25), channel_id=1, source_target_pairs={{0,1},{1,0},{2,3},{3,2},{4,5},{5,4},{6,7},{7,6},{8,9},{9,8},{10,11... | collective-permute-start | bytes 36872 | tf_op jit(solution)/shard_map/ppermute | solution.py:234
  51.8 0.0 collective-permute-done.7.col2
  51.8 1.1 %collective-permute-done.6.col1 = f32[3,8,128]{2,1,0:T(8,128)S(1)} collective-permute-done((f32[3,8,128]{2,1,0:T(8,128)S(1)}, f32[3,8,128]{2,1,0:T(8,128)S(1)}, u32[]{:S(2)}, u32[]{:S(2)}) %collective-permute-start.6) | collective-permute-done | bytes 12320 | tf_op jit(solution)/shard_map/ppermute | solution.py:234
  52.8 0.0 copy-done.4
  52.8 0.0 copy-done.9
  52.8 1.5 %surface.1 = f32[8,96]{1,0:T(8,128)} custom-call(f32[3,8,128]{2,1,0:T(8,128)S(1)} %collective-permute-done.4.row1, f32[3,8,128]{2,1,0:T(8,128)S(1)} %collective-permute-done.5.row2, f32[3,8,128]{2,1,0:T(8,128)S(1)} %collective-permute-done.6.col1, f32[3,8,128]{2,1,0:T(8,128)S(1)} %collective-permute-done.7.col2, f32[3,8,128]{2,1,0:T(8,128)S(1)} %get-tuple-element.19.own, ...), custom_call_target="tpu_custom_call" | custom-call | flops 1000000 | bytes 200000 | tf_op jit(solution)/shard_map/surface/pallas_call | solution.py:247
  (9 shorter events, 0.0 us)
Async XLA Ops:
  0.7 0.8 %copy-start = (f32[8,16,128]{2,1,0:T(8,128)S(1)}, f32[8,16,128]{2,1,0:T(8,128)}, u32[]{:S(2)}) copy-start(f32[8,16,128]{2,1,0:T(8,128)} %param.16) | copy-start | bytes 196612
  1.6 0.7 %copy-start.3 = (s32[1,3,3,48]{3,0,2,1:T(1,128)S(1)}, s32[1,3,3,48]{3,0,2,1:T(1,128)}, u32[]{:S(2)}) copy-start(s32[1,3,3,48]{3,0,2,1:T(1,128)} %param.11) | copy-start | bytes 5188
  2.3 0.7 %copy-start.6 = (f32[20,96]{1,0:T(8,128)S(1)}, f32[20,96]{1,0:T(8,128)}, u32[]{:S(2)}) copy-start(f32[20,96]{1,0:T(8,128)} %flux.1) | copy-start | bytes 23044
  3.0 0.7 %copy-start.8 = (s32[1,3,3]{2,0,1:T(1,128)S(1)}, s32[1,3,3]{2,0,1:T(1,128)}, u32[]{:S(2)}) copy-start(s32[1,3,3]{2,0,1:T(1,128)} %param.12) | copy-start | bytes 112
  3.6 0.7 %copy-start.11 = (f32[8,20]{1,0:T(8,128)S(1)}, f32[8,20]{1,0:T(8,128)}, u32[]{:S(2)}) copy-start(f32[8,20]{1,0:T(8,128)} %coupling.1) | copy-start | bytes 1924
  5.1 18.0 %collective-permute-start = (f32[4,8,128]{2,1,0:T(8,128)S(1)}, f32[4,8,128]{2,1,0:T(8,128)S(1)}, u32[]{:S(2)}, u32[]{:S(2)}) collective-permute-start(f32[4,8,128]{2,1,0:T(8,128)S(1)} %get-tuple-element.11), channel_id=1, source_target_pairs={{0,64},{64,0},{128,192},{192,128},{256,320},{320,256},{384,448},{4... | collective-permute-start | bytes 49160 | tf_op jit(solution)/shard_map/ppermute | solution.py:234
  21.2 5.1 %collective-permute-start.1 = (f32[4,8,128]{2,1,0:T(8,128)S(1)}, f32[4,8,128]{2,1,0:T(8,128)S(1)}, u32[]{:S(2)}, u32[]{:S(2)}) collective-permute-start(f32[4,8,128]{2,1,0:T(8,128)S(1)} %get-tuple-element.12), channel_id=1, source_target_pairs={{64,128},{192,256},{320,384},{448,512},{576,640},{704,768},{832,89... | collective-permute-start | bytes 49160 | tf_op jit(solution)/shard_map/ppermute | solution.py:233
  26.3 7.5 %collective-permute-start.3 = (f32[4,8,128]{2,1,0:T(8,128)S(1)}, f32[4,8,128]{2,1,0:T(8,128)S(1)}, u32[]{:S(2)}, u32[]{:S(2)}) collective-permute-start(f32[4,8,128]{2,1,0:T(8,128)S(1)} %get-tuple-element.20), channel_id=1, source_target_pairs={{1,2},{3,4},{5,6},{7,8},{9,10},{11,12},{13,14},{15,16},{17,18},{19... | collective-permute-start | bytes 49160 | tf_op jit(solution)/shard_map/ppermute | solution.py:233
  26.9 6.9 %collective-permute-start.2 = (f32[4,8,128]{2,1,0:T(8,128)S(1)}, f32[4,8,128]{2,1,0:T(8,128)S(1)}, u32[]{:S(2)}, u32[]{:S(2)}) collective-permute-start(f32[4,8,128]{2,1,0:T(8,128)S(1)} %get-tuple-element.21), channel_id=1, source_target_pairs={{0,1},{1,0},{2,3},{3,2},{4,5},{5,4},{6,7},{7,6},{8,9},{9,8},{10,11... | collective-permute-start | bytes 49160 | tf_op jit(solution)/shard_map/ppermute | solution.py:234
  28.9 0.9 %copy-start.2 = (f32[1,3,3,48,128]{4,3,2,1,0:T(8,128)S(1)}, f32[1,3,3,48,128]{4,3,2,1,0:T(8,128)}, u32[]{:S(2)}) copy-start(f32[1,3,3,48,128]{4,3,2,1,0:T(8,128)} %weight.1) | copy-start | bytes 663556
  29.8 0.7 %copy-start.10 = (s32[1,3,3,48]{3,0,2,1:T(1,128)S(1)}, s32[1,3,3,48]{3,0,2,1:T(1,128)}, u32[]{:S(2)}) copy-start(s32[1,3,3,48]{3,0,2,1:T(1,128)} %param.13) | copy-start | bytes 5188
  33.8 0.8 %copy-start.1 = (f32[8,16,128]{2,1,0:T(8,128)S(1)}, f32[8,16,128]{2,1,0:T(8,128)}, u32[]{:S(2)}) copy-start(f32[8,16,128]{2,1,0:T(8,128)} %param.16) | copy-start | bytes 196612
  34.7 0.7 %copy-start.5 = (f32[2,16,128]{2,1,0:T(8,128)S(1)}, f32[2,16,128]{2,1,0:T(8,128)}, u32[]{:S(2)}) copy-start(f32[2,16,128]{2,1,0:T(8,128)} %velocity.1) | copy-start | bytes 49156
  35.4 0.7 %copy-start.7 = (s32[16,128]{1,0:T(8,128)S(1)}, s32[16,128]{1,0:T(8,128)}, u32[]{:S(2)}) copy-start(s32[16,128]{1,0:T(8,128)} %wet.1) | copy-start | bytes 24580
  36.1 0.7 %copy-start.12 = (f32[8]{0:T(128)S(1)}, f32[8]{0:T(128)}, u32[]{:S(2)}) copy-start(f32[8]{0:T(128)} %diffusivity.1) | copy-start | bytes 100
  36.7 16.1 %copy-start.4 = (s32[1,3,3,48]{3,0,2,1:T(1,128)S(1)}, s32[1,3,3,48]{3,0,2,1:T(1,128)}, u32[]{:S(2)}) copy-start(s32[1,3,3,48]{3,0,2,1:T(1,128)} %param.11) | copy-start | bytes 5188
  36.7 16.1 %copy-start.9 = (s32[1,3,3]{2,0,1:T(1,128)S(1)}, s32[1,3,3]{2,0,1:T(1,128)}, u32[]{:S(2)}) copy-start(s32[1,3,3]{2,0,1:T(1,128)} %param.12) | copy-start | bytes 112
  39.5 3.9 %collective-permute-start.4 = (f32[3,8,128]{2,1,0:T(8,128)S(1)}, f32[3,8,128]{2,1,0:T(8,128)S(1)}, u32[]{:S(2)}, u32[]{:S(2)}) collective-permute-start(f32[3,8,128]{2,1,0:T(8,128)S(1)} %get-tuple-element.17), channel_id=1, source_target_pairs={{0,64},{64,0},{128,192},{192,128},{256,320},{320,256},{384,448},{4... | collective-permute-start | bytes 36872 | tf_op jit(solution)/shard_map/ppermute | solution.py:234
  41.4 5.0 %collective-permute-start.5 = (f32[3,8,128]{2,1,0:T(8,128)S(1)}, f32[3,8,128]{2,1,0:T(8,128)S(1)}, u32[]{:S(2)}, u32[]{:S(2)}) collective-permute-start(f32[3,8,128]{2,1,0:T(8,128)S(1)} %get-tuple-element.18), channel_id=1, source_target_pairs={{64,128},{192,256},{320,384},{448,512},{576,640},{704,768},{832,89... | collective-permute-start | bytes 36872 | tf_op jit(solution)/shard_map/ppermute | solution.py:233
  46.5 5.3 %collective-permute-start.7 = (f32[3,8,128]{2,1,0:T(8,128)S(1)}, f32[3,8,128]{2,1,0:T(8,128)S(1)}, u32[]{:S(2)}, u32[]{:S(2)}) collective-permute-start(f32[3,8,128]{2,1,0:T(8,128)S(1)} %get-tuple-element.24), channel_id=1, source_target_pairs={{1,2},{3,4},{5,6},{7,8},{9,10},{11,12},{13,14},{15,16},{17,18},{19... | collective-permute-start | bytes 36872 | tf_op jit(solution)/shard_map/ppermute | solution.py:233
  47.1 5.7 %collective-permute-start.6 = (f32[3,8,128]{2,1,0:T(8,128)S(1)}, f32[3,8,128]{2,1,0:T(8,128)S(1)}, u32[]{:S(2)}, u32[]{:S(2)}) collective-permute-start(f32[3,8,128]{2,1,0:T(8,128)S(1)} %get-tuple-element.25), channel_id=1, source_target_pairs={{0,1},{1,0},{2,3},{3,2},{4,5},{5,4},{6,7},{7,6},{8,9},{9,8},{10,11... | collective-permute-start | bytes 36872 | tf_op jit(solution)/shard_map/ppermute | solution.py:234

commit v2 on v1

v2 whole, which is shorter than its diff:
```python
import functools

import jax
import jax.numpy as jnp
from jax import lax
from jax.experimental import pallas as pl
from jax.experimental.pallas import tpu as pltpu
from jax.sharding import PartitionSpec as P

WIN_R = 8
WIN_C = 16
OFF = 64
SPLIT = 5
VMEM = pl.BlockSpec(memory_space=pltpu.VMEM)
HBM = pl.BlockSpec(memory_space=pltpu.HBM)
F32 = jnp.float32
BF16 = jnp.bfloat16
NT = (((1,), (1,)), ((), ()))


def lanes_of(shape):
    return lax.broadcasted_iota(jnp.int32, shape, 1)


def halves(value):
    high = value.astype(BF16)
    low = (value - high.astype(F32)).astype(BF16)
    return high, low


def is_even(axis):
    return lax.axis_index(axis) % 2 == 0


def pack_kernel(
    flux, index, count, coupling, state, start, weight, velocity, diffusivity, wet,
    send1, send2, own, index_kept, count_kept, state_kept, start_kept, weight_kept, velocity_kept,
    diffusivity_kept, wet_kept,
    flux_in, coupling_in, index_scr, flux_scr, sems,
):
    pairs = [
        (flux, flux_in), (coupling, coupling_in), (index, index_kept), (count, count_kept), (state, state_kept),
        (start, start_kept), (weight, weight_kept), (velocity, velocity_kept),
        (diffusivity, diffusivity_kept), (wet, wet_kept),
    ]
    copies = [pltpu.make_async_copy(source, target, sems.at[i]) for i, (source, target) in enumerate(pairs)]
    for copy in copies:
        copy.start()
    slots = index.shape[2]
    even = is_even("row")
    index_scr[...] = jnp.zeros_like(index_scr)
    flux_scr[...] = jnp.zeros_like(flux_scr)
    for copy in copies[:5]:
        copy.wait()
    for i in range(9):
        index_scr[i : i + 1, 0:slots] = index_kept[i]
    flux_scr[:, 0 : flux.shape[1]] = lax.dot_general(
        coupling_in[...], flux_in[...], (((1,), (0,)), ((), ())),
        precision=lax.Precision.HIGHEST, preferred_element_type=F32,
    )
    rows = state.shape[0] // 8
    mapped = flux_scr[...]
    lane = lanes_of(mapped.shape)
    west = jnp.zeros_like(mapped)
    east = jnp.zeros_like(mapped)
    width = state.shape[1]
    for y in range(rows):
        line = state_kept[pl.ds(y, 8, stride=rows), :]
        west = jnp.where(lane == y, jnp.broadcast_to(line[:, 0:1], mapped.shape), west)
        east = jnp.where(lane == y, jnp.broadcast_to(line[:, width - 1 : width], mapped.shape), east)
    own[3] = west
    own[4] = east
    groups = []
    for a in range(3):
        for b in range(3):
            used = jnp.broadcast_to(count_kept[a][:, b : b + 1], mapped.shape)
            places = jnp.broadcast_to(index_scr[3 * a + b : 3 * a + b + 1, :], mapped.shape)
            picked = jnp.take_along_axis(mapped, places, axis=1)
            flag = ((lane >= OFF) & (lane < OFF + used)).astype(F32)
            groups.append(jnp.where(lane < used, picked, flag))
    for b in range(3):
        up, down = groups[6 + b], groups[b]
        send1[b] = jnp.where(even, up, down)
        send2[b] = jnp.where(even, down, up)
        own[b] = groups[3 + b]
    first = state_kept[pl.ds(0, 8, stride=rows), :]
    last = state_kept[pl.ds(rows - 1, 8, stride=rows), :]
    send1[3] = jnp.where(even, last, first)
    send2[3] = jnp.where(even, first, last)
    for copy in copies[5:]:
        copy.wait()


def spread_kernel(begin, end, start, weight, after, high, low, start_scr):
    slots, width = weight.shape[3], weight.shape[4]
    rows = high.shape[1] // width
    start_scr[...] = jnp.zeros_like(start_scr)
    for i in range(begin, end):
        start_scr[i : i + 1, 0:slots] = start[i].astype(F32)
    turned = start_scr[...].T
    lane = lanes_of((slots, width))
    for i in range(begin, end):
        first = turned[0:slots, i : i + 1].astype(jnp.int32)
        top = first // width
        left = jnp.broadcast_to(first - top * width, (slots, width))
        above = jnp.broadcast_to(top * WIN_C, (slots, width))
        across = lane - left
        inside = (across >= 0) & (across < WIN_C)
        place = jnp.where(inside, across - above, -(1 << 20))
        block = weight[0, i // 3, i % 3]
        at_rows = slice((i - begin) * slots, (i - begin + 1) * slots)
        for y in range(rows):
            at = place + y * WIN_C
            hit = (at >= 0) & (at < WIN_R * WIN_C)
            value = jnp.take_along_axis(block, at & (width - 1), axis=1)
            value = jnp.where(hit, value, 0.0)
            part, rest = halves(value)
            high[at_rows, y * width : (y + 1) * width] = part
            low[at_rows, y * width : (y + 1) * width] = rest


def hot_kernel(index, count, after, hot, index_scr):
    slots = index.shape[2]
    cells, width = hot.shape[0], index_scr.shape[1]
    index_scr[...] = jnp.zeros_like(index_scr)
    for i in range(9):
        index_scr[i : i + 1, 0:slots] = index[i]
    lane = lanes_of((1, width))
    cell = lax.broadcasted_iota(jnp.int32, (cells, width), 0)
    for i in range(9):
        used = lane < jnp.broadcast_to(count[i // 3][:, i % 3 : i % 3 + 1], (1, width))
        places = jnp.where(used, index_scr[i : i + 1, :], -1)
        here = jnp.broadcast_to(places, (cells, width)) == cell
        hot[:, i * width : (i + 1) * width] = here.astype(F32).astype(BF16)


def ocean_kernel(
    row1, row2, col1, col2, own, high1, low1, high2, low2, state, velocity, diffusivity, wet,
    new_state, send1, send2, back_own, surface,
):
    split = high1.shape[0]
    slots = (split + high2.shape[0]) // 9
    width = state.shape[1]
    rows = state.shape[0] // 8
    even_r = is_even("row")
    even_c = is_even("col")

    def from_plus(one, two, even, i):
        return jnp.where(even, one[i], two[i])

    def from_minus(one, two, even, i):
        return jnp.where(even, two[i], one[i])

    middle = [from_minus(row1, row2, even_r, 1), own[1], from_plus(row1, row2, even_r, 1)]
    blocks = []
    for p in range(3):
        blocks += [from_minus(col1, col2, even_c, p), middle[p], from_plus(col1, col2, even_c, p)]
    south_edge = from_minus(row1, row2, even_r, 3)
    north_edge = from_plus(row1, row2, even_r, 3)
    west_edge = from_minus(col1, col2, even_c, 3)
    east_edge = from_plus(col1, col2, even_c, 3)

    def left_of(group):
        fields = jnp.concatenate([block[:, 0:slots] for block in group], axis=1)
        flags = jnp.concatenate([block[:, OFF : OFF + slots] for block in group], axis=1)
        first_row = lax.broadcasted_iota(jnp.int32, flags.shape, 0) == 0
        flags = jnp.where(first_row, flags, 0.0)
        field_high = fields.astype(BF16).astype(F32)
        field_low = fields - field_high
        parts = [field_high, flags, field_low, jnp.zeros_like(flags)]
        return jnp.concatenate(parts, axis=0).astype(BF16)

    left1 = left_of(blocks[: split // slots])
    left2 = left_of(blocks[split // slots :])

    lane = lanes_of((8, width))
    row_of = lax.broadcasted_iota(jnp.int32, (8, width), 0)
    one_row = jnp.where(row_of == 0, 1.0, 0.0)
    spread = jnp.zeros((8, width), F32)
    for k in range(8):
        spread = jnp.where(row_of == k, jnp.broadcast_to(diffusivity[:, k : k + 1], (8, width)), spread)
    step = 2 * width
    lines = [state[pl.ds(y, 8, stride=rows), :] for y in range(rows)]
    for part in range(rows // 2):
        cells = slice(part * step, (part + 1) * step)
        sums = jnp.dot(left1, high1[:, cells], preferred_element_type=F32)
        sums = sums + jnp.dot(left2, high2[:, cells], preferred_element_type=F32)
        rest = jnp.dot(left1[0:16], low1[:, cells], preferred_element_type=F32)
        rest = rest + jnp.dot(left2[0:16], low2[:, cells], preferred_element_type=F32)
        sums = sums[0:16] + sums[16:32] + rest
        for y in (2 * part, 2 * part + 1):
            at = slice((y % 2) * width, (y % 2 + 1) * width)
            cover = sums[8:9, at]
            forcing = sums[0:8, at] / jnp.maximum(jnp.broadcast_to(cover, (8, width)), 1.0)
            here = lines[y]
            north = lines[y + 1] if y + 1 < rows else north_edge
            south = lines[y - 1] if y > 0 else south_edge
            east = pltpu.roll(here, width - 1, 1)
            east = jnp.where(lane == width - 1, jnp.broadcast_to(east_edge[:, y : y + 1], (8, width)), east)
            west = pltpu.roll(here, 1, 1)
            west = jnp.where(lane == 0, jnp.broadcast_to(west_edge[:, y : y + 1], (8, width)), west)
            laplace = east + west + north + south - 4.0 * here
            along = jnp.broadcast_to(velocity[0, y : y + 1, :], (8, width))
            across = jnp.broadcast_to(velocity[1, y : y + 1, :], (8, width))
            advect = 0.5 * (along * (east - west) + across * (north - south))
            mask = jnp.broadcast_to(wet[y : y + 1, :], (8, width)).astype(F32)
            fresh = here + mask * (spread * laplace - advect + forcing)
            new_state[pl.ds(y, 8, stride=rows), :] = fresh
            seen = fresh * mask
            seen_high = seen.astype(BF16).astype(F32)
            column = slice(y * width, (y + 1) * width)
            surface[0:16, column] = jnp.concatenate([seen_high, one_row], axis=0).astype(BF16)
            surface[16:32, column] = jnp.concatenate([seen - seen_high, jnp.zeros_like(seen)], axis=0).astype(BF16)
    pad = jnp.zeros((8, OFF - slots), F32)
    out = []
    for high, low in ((high1, low1), (high2, low2)):
        back = lax.dot_general(surface[...], high[...], NT, preferred_element_type=F32)
        back = back[0:16] + back[16:32] + lax.dot_general(
            surface[0:16, :], low[...], NT, preferred_element_type=F32
        )
        for i in range(high.shape[0] // slots):
            at = slice(i * slots, (i + 1) * slots)
            out.append(jnp.concatenate([back[0:8, at], pad, back[8:16, at], pad], axis=1))
    for q in range(3):
        up, down = out[6 + q], out[q]
        send1[q] = jnp.where(even_r, up, down)
        send2[q] = jnp.where(even_r, down, up)
        back_own[q] = out[3 + q]


def surface_kernel(row1, row2, col1, col2, own, hot, result):
    cells = result.shape[1]
    even_r = is_even("row")
    even_c = is_even("col")
    middle = [
        jnp.where(even_r, row2[1], row1[1]),
        own[1],
        jnp.where(even_r, row1[1], row2[1]),
    ]
    blocks = []
    for a in range(3):
        blocks += [
            jnp.where(even_c, col2[a], col1[a]),
            middle[a],
            jnp.where(even_c, col1[a], col2[a]),
        ]
    values = jnp.concatenate(blocks, axis=1)
    weights = jnp.concatenate([pltpu.roll(block, OFF, 1) for block in blocks], axis=1)
    value_high = values.astype(BF16).astype(F32)
    weight_high = weights.astype(BF16).astype(F32)
    left = jnp.concatenate([value_high, weight_high, values - value_high, weights - weight_high], axis=0)
    total = lax.dot_general(left.astype(BF16), hot[...], NT, preferred_element_type=F32)
    total = total[0:16] + total[16:32]
    cover = jnp.maximum(jnp.broadcast_to(total[8:9], (8, cells)), 1.0)
    result[...] = total[0:8] / cover


def swaps(count):
    near = [(i, i ^ 1) for i in range(count)]
    far = [(i, i + 1) for i in range(1, count - 1, 2)]
    far = far + [(j, i) for i, j in far]
    return near, far


def exchange(send1, send2, axis):
    near, far = swaps(lax.axis_size(axis))
    two = lax.ppermute(send2, axis, far)
    one = lax.ppermute(send1, axis, near)
    return one, two


def column_sends(row1, row2, own, extra, even_r, even_c):
    minus = jnp.where(even_r, row2, row1)
    plus = jnp.where(even_r, row1, row2)
    low = jnp.stack([minus[0], own[0], plus[0]] + [edge for edge in extra[:1]])
    high = jnp.stack([minus[2], own[2], plus[2]] + [edge for edge in extra[1:]])
    return jnp.where(even_c, high, low), jnp.where(even_c, low, high)


def in_hbm(array):
    return pltpu.with_memory_space_constraint(array, pltpu.HBM)


def call(kernel, outs, scratch, specs, flops, size, *args, name):
    return pl.pallas_call(
        kernel,
        out_shape=outs,
        in_specs=specs,
        out_specs=[VMEM] * len(outs),
        scratch_shapes=scratch,
        compiler_params=pltpu.CompilerParams(vmem_limit_bytes=24 * 1024 * 1024),
        cost_estimate=pl.CostEstimate(flops=flops, bytes_accessed=size, transcendentals=0),
        name=name,
    )(*args)


def on_device(
    atm_flux,
    send_index,
    send_count,
    block_start,
    remap_weight,
    coupling,
    ocean_state,
    velocity,
    diffusivity,
    wet_mask,
):
    fields, rows, width = ocean_state.shape
    slots = send_index.shape[3]
    cells = rows * width
    atm_cells = atm_flux.shape[1]
    even_r = is_even("row")
    even_c = is_even("col")
    state = ocean_state.reshape(fields * rows, width)
    index = send_index.reshape(9, 1, slots)
    count = send_count.reshape(3, 1, 3)
    start = block_start.reshape(9, 1, slots)

    def shape(*dims, dtype=F32):
        return jax.ShapeDtypeStruct(dims, dtype)

    kept = [index, count, state, start, remap_weight, velocity, diffusivity.reshape(1, -1), wet_mask]
    send1, send2, own, index, count, state, start, weight, velocity, diffusivity, wet = call(
        pack_kernel,
        [shape(4, 8, width), shape(4, 8, width), shape(5, 8, width)]
        + [shape(*array.shape, dtype=array.dtype) for array in kept],
        [
            pltpu.VMEM(atm_flux.shape, F32),
            pltpu.VMEM(coupling.shape, F32),
            pltpu.VMEM((16, width), jnp.int32),
            pltpu.VMEM((8, width), F32),
            pltpu.SemaphoreType.DMA((10,)),
        ],
        [HBM] * 10,
        100_000, 1_000_000,
        *(in_hbm(array) for array in (atm_flux, index, count, coupling)),
        *(in_hbm(array) for array in kept[2:]),
        name="pack",
    )

    def spread(begin, end, after, name):
        return call(
            functools.partial(spread_kernel, begin, end),
            [shape((end - begin) * slots, cells, dtype=BF16)] * 2,
            [pltpu.VMEM((16, width), F32)],
            [VMEM, VMEM, VMEM],
            20_000_000, 4_000_000,
            start, weight, after,
            name=name,
        )

    row1, row2 = exchange(send1, send2, "row")
    high1, low1 = spread(0, SPLIT, own, "spread_one")
    row1, row2, high1, low1 = lax.optimization_barrier((row1, row2, high1, low1))
    send1, send2 = column_sends(row1, row2, own, [own[3], own[4]], even_r, even_c)
    col1, col2 = exchange(send1, send2, "col")
    high2, low2 = spread(SPLIT, 9, send1, "spread_two")
    new_state, send1, send2, own = call(
        ocean_kernel,
        [shape(fields * rows, width), shape(3, 8, width), shape(3, 8, width), shape(3, 8, width)],
        [pltpu.VMEM((32, cells), BF16)],
        [VMEM] * 13,
        100_000_000, 4_000_000,
        row1, row2, col1, col2, own, high1, low1, high2, low2, state, velocity, diffusivity, wet,
        name="ocean",
    )
    row1, row2 = exchange(send1, send2, "row")
    (hot,) = call(
        hot_kernel,
        [shape(atm_cells, 9 * width, dtype=BF16)],
        [pltpu.VMEM((16, width), jnp.int32)],
        [VMEM] * 3,
        1_000_000, 200_000,
        index, count, own,
        name="hot",
    )
    row1, row2, hot = lax.optimization_barrier((row1, row2, hot))
    send1, send2 = column_sends(row1, row2, own, [], even_r, even_c)
    col1, col2 = exchange(send1, send2, "col")
    (result,) = call(
        surface_kernel,
        [shape(fields, atm_cells)],
        [],
        [VMEM] * 6,
        1_000_000, 200_000,
        row1, row2, col1, col2, own, hot,
        name="surface",
    )
    return new_state.reshape(ocean_state.shape), result


def solution(mesh):
    return jax.shard_map(
        on_device,
        mesh=mesh,
        in_specs=(
            P(None, ("row", "col")),
            P(("row", "col"), None, None, None),
            P(("row", "col"), None, None),
            P(("row", "col"), None, None, None),
            P(("row", "col"), None, None, None, None),
            P(),
            P(None, "row", "col"),
            P(None, "row", "col"),
            P(),
            P("row", "col"),
        ),
        out_specs=(P(None, "row", "col"), P(None, ("row", "col"))),
        check_vma=False,
    )
```

time: 55 us -> 47.2 us (0.86)
  the two profiles are of different devices: /device:TPU:1 before, /device:TPU:22 now
where the time goes in v2:
time: 47.2 us; the launch traced here: 46.8 us
  starting transfers between devices  28.8 us (61%)
  waiting for transfers between devices  9.15 us (19%)
  Pallas kernels  7.96 us (17%)
  between operations  0.81 us (2%)
    ppermute x4, starting transfers between devices, exchange(): one = lax.ppermute(send1, axis, near)  17.9 us
    ppermute x4, starting transfers between devices, exchange(): two = lax.ppermute(send2, axis, far)  10.9 us
    ppermute x4, waiting for transfers between devices, exchange(): two = lax.ppermute(send2, axis, far)  9.14 us
    pallas_call x6, Pallas kernels, call(): pl.pallas_call(kernel, out_shape=outs, in_specs=specs, out_specs=[VMEM] *...  7.96 us
  transfers between devices with their start and end apart: 8, of which 4 were waited for; matrix products, arithmetic and copies ran while one was open for 0% of the time, Pallas kernels for 8%

profile of v2, /device:TPU:22, one launch (start us, length us, event | category | flops | bytes accessed | tf_op | source)
XLA Modules:
  0.0 46.8 jit_solution(14259165766940762298)
XLA Ops:
  0.6 1.2 %pack.1 = (f32[4,8,128]{2,1,0:T(8,128)S(1)}, f32[4,8,128]{2,1,0:T(8,128)S(1)}, f32[5,8,128]{2,1,0:T(8,128)S(1)}, s32[9,1,48]{2,1,0:T(1,128)S(1)}, s32[3,1,3]{2,1...) custom-call(f32[20,96]{1,0:T(8,128)} %flux.1, ...), custom_call_target="tpu_custom_call" | custom-call | flops 100000 | bytes 1000000 | tf_op jit(solution)/shard_map/pack/pallas_call | solution.py:285
  1.9 1.9 %collective-permute-start = (f32[4,8,128]{2,1,0:T(8,128)S(1)}, f32[4,8,128]{2,1,0:T(8,128)S(1)}, u32[]{:S(2)}, u32[]{:S(2)}) collective-permute-start(f32[4,8,128]{2,1,0:T(8,128)S(1)} %get-tuple-element.28), channel_id=1, source_target_pairs={{0,64},{64,0},{128,192},{192,128},{256,320},{320,256},{384,448},{4... | collective-permute-start | bytes 49160 | tf_op jit(solution)/shard_map/ppermute | solution.py:268
  3.8 2.3 %collective-permute-start.1 = (f32[4,8,128]{2,1,0:T(8,128)S(1)}, f32[4,8,128]{2,1,0:T(8,128)S(1)}, u32[]{:S(2)}, u32[]{:S(2)}) collective-permute-start(f32[4,8,128]{2,1,0:T(8,128)S(1)} %get-tuple-element.29), channel_id=1, source_target_pairs={{64,128},{192,256},{320,384},{448,512},{576,640},{704,768},{832,89... | collective-permute-start | bytes 49160 | tf_op jit(solution)/shard_map/ppermute | solution.py:267
  6.2 1.9 %spread_one.1 = (bf16[240,2048]{1,0:T(8,128)(2,1)S(1)}, bf16[240,2048]{1,0:T(8,128)(2,1)S(1)}) custom-call(s32[9,1,48]{2,1,0:T(1,128)S(1)} %get-tuple-element.30.start, f32[1,3,3,48,128]{4,3,2,1,0:T(8,128)S(1)} %get-tuple-element.31.weight, f32[5,8,128]{2,1,0:T(8,128)S(1)} %get-tuple-element.32.after.own), custom_call_target="tpu_custom_call" | custom-call | flops 20000000 | bytes 4000000 | tf_op jit(solution)/shard_map/spread_one/pallas_call | solution.py:285
  8.1 0.0 collective-permute-done.row1
  8.1 0.7 %collective-permute-done.1.row2 = f32[4,8,128]{2,1,0:T(8,128)S(1)} collective-permute-done((f32[4,8,128]{2,1,0:T(8,128)S(1)}, f32[4,8,128]{2,1,0:T(8,128)S(1)}, u32[]{:S(2)}, u32[]{:S(2)}) %collective-permute-start.1) | collective-permute-done | bytes 16416 | tf_op jit(solution)/shard_map/ppermute | solution.py:267
  8.9 2.4 %collective-permute-start.2 = (f32[4,8,128]{2,1,0:T(8,128)S(1)}, f32[4,8,128]{2,1,0:T(8,128)S(1)}, u32[]{:S(2)}, u32[]{:S(2)}) collective-permute-start(f32[4,8,128]{2,1,0:T(8,128)S(1)} %get-tuple-element.55.after), channel_id=1, source_target_pairs={{0,1},{1,0},{2,3},{3,2},{4,5},{5,4},{6,7},{7,6},{8,9},{9,8},{10,11... | collective-permute-start | bytes 49160 | tf_op jit(solution)/shard_map/ppermute | solution.py:268
  11.3 4.7 %collective-permute-start.3 = (f32[4,8,128]{2,1,0:T(8,128)S(1)}, f32[4,8,128]{2,1,0:T(8,128)S(1)}, u32[]{:S(2)}, u32[]{:S(2)}) collective-permute-start(f32[4,8,128]{2,1,0:T(8,128)S(1)} %get-tuple-element.54), channel_id=1, source_target_pairs={{1,2},{3,4},{5,6},{7,8},{9,10},{11,12},{13,14},{15,16},{17,18},{19... | collective-permute-start | bytes 49160 | tf_op jit(solution)/shard_map/ppermute | solution.py:267
  16.0 1.6 %spread_two.1 = (bf16[192,2048]{1,0:T(8,128)(2,1)S(1)}, bf16[192,2048]{1,0:T(8,128)(2,1)S(1)}) custom-call(s32[9,1,48]{2,1,0:T(1,128)S(1)} %get-tuple-element.30.start, f32[1,3,3,48,128]{4,3,2,1,0:T(8,128)S(1)} %get-tuple-element.31.weight, f32[4,8,128]{2,1,0:T(8,128)S(1)} %get-tuple-element.55.after), custom_call_target="tpu_custom_call" | custom-call | flops 20000000 | bytes 4000000 | tf_op jit(solution)/shard_map/spread_two/pallas_call | solution.py:285
  17.6 0.0 collective-permute-done.2.col1
  17.6 0.6 %collective-permute-done.3.col2 = f32[4,8,128]{2,1,0:T(8,128)S(1)} collective-permute-done((f32[4,8,128]{2,1,0:T(8,128)S(1)}, f32[4,8,128]{2,1,0:T(8,128)S(1)}, u32[]{:S(2)}, u32[]{:S(2)}) %collective-permute-start.3) | collective-permute-done | bytes 16416 | tf_op jit(solution)/shard_map/ppermute | solution.py:267
  18.2 2.3 %ocean.1 = (f32[128,128]{1,0:T(8,128)}, f32[3,8,128]{2,1,0:T(8,128)S(1)}, f32[3,8,128]{2,1,0:T(8,128)S(1)}, f32[3,8,128]{2,1,0:T(8,128)S(1)}) custom-call(f32[4,8,128]{2,1,0:T(8,128)S(1)} %collective-permute-done.row1, f32[4,8,128]{2,1,0:T(8,128)S(1)} %collective-permute-done.1.row2, f32[4,8,128]{2,1,0:T(8,128)S(1)} %collective-permute-done.2.col1, ...), custom_call_target="tpu_custom_call" | custom-call | flops 100000000 | bytes 4000000 | tf_op jit(solution)/shard_map/ocean/pallas_call | solution.py:285
  20.5 1.9 %collective-permute-start.4 = (f32[3,8,128]{2,1,0:T(8,128)S(1)}, f32[3,8,128]{2,1,0:T(8,128)S(1)}, u32[]{:S(2)}, u32[]{:S(2)}) collective-permute-start(f32[3,8,128]{2,1,0:T(8,128)S(1)} %get-tuple-element.46), channel_id=1, source_target_pairs={{0,64},{64,0},{128,192},{192,128},{256,320},{320,256},{384,448},{4... | collective-permute-start | bytes 36872 | tf_op jit(solution)/shard_map/ppermute | solution.py:268
  22.4 1.9 %collective-permute-start.5 = (f32[3,8,128]{2,1,0:T(8,128)S(1)}, f32[3,8,128]{2,1,0:T(8,128)S(1)}, u32[]{:S(2)}, u32[]{:S(2)}) collective-permute-start(f32[3,8,128]{2,1,0:T(8,128)S(1)} %get-tuple-element.47), channel_id=1, source_target_pairs={{64,128},{192,256},{320,384},{448,512},{576,640},{704,768},{832,89... | collective-permute-start | bytes 36872 | tf_op jit(solution)/shard_map/ppermute | solution.py:267
  24.3 0.1 hot.1
  24.5 0.0 collective-permute-done.4.row1
  24.5 2.9 %collective-permute-done.5.row2 = f32[3,8,128]{2,1,0:T(8,128)S(1)} collective-permute-done((f32[3,8,128]{2,1,0:T(8,128)S(1)}, f32[3,8,128]{2,1,0:T(8,128)S(1)}, u32[]{:S(2)}, u32[]{:S(2)}) %collective-permute-start.5) | collective-permute-done | bytes 12320 | tf_op jit(solution)/shard_map/ppermute | solution.py:267
  27.4 11.7 %collective-permute-start.6 = (f32[3,8,128]{2,1,0:T(8,128)S(1)}, f32[3,8,128]{2,1,0:T(8,128)S(1)}, u32[]{:S(2)}, u32[]{:S(2)}) collective-permute-start(f32[3,8,128]{2,1,0:T(8,128)S(1)} %get-tuple-element.59), channel_id=1, source_target_pairs={{0,1},{1,0},{2,3},{3,2},{4,5},{5,4},{6,7},{7,6},{8,9},{9,8},{10,11... | collective-permute-start | bytes 36872 | tf_op jit(solution)/shard_map/ppermute | solution.py:268
  39.1 1.9 %collective-permute-start.7 = (f32[3,8,128]{2,1,0:T(8,128)S(1)}, f32[3,8,128]{2,1,0:T(8,128)S(1)}, u32[]{:S(2)}, u32[]{:S(2)}) collective-permute-start(f32[3,8,128]{2,1,0:T(8,128)S(1)} %get-tuple-element.58), channel_id=1, source_target_pairs={{1,2},{3,4},{5,6},{7,8},{9,10},{11,12},{13,14},{15,16},{17,18},{19... | collective-permute-start | bytes 36872 | tf_op jit(solution)/shard_map/ppermute | solution.py:267
  41.0 0.0 collective-permute-done.6.col1
  41.0 4.9 %collective-permute-done.7.col2 = f32[3,8,128]{2,1,0:T(8,128)S(1)} collective-permute-done((f32[3,8,128]{2,1,0:T(8,128)S(1)}, f32[3,8,128]{2,1,0:T(8,128)S(1)}, u32[]{:S(2)}, u32[]{:S(2)}) %collective-permute-start.7) | collective-permute-done | bytes 12320 | tf_op jit(solution)/shard_map/ppermute | solution.py:267
  45.9 0.9 %surface.1 = f32[8,96]{1,0:T(8,128)} custom-call(f32[3,8,128]{2,1,0:T(8,128)S(1)} %collective-permute-done.4.row1, f32[3,8,128]{2,1,0:T(8,128)S(1)} %collective-permute-done.5.row2, f32[3,8,128]{2,1,0:T(8,128)S(1)} %collective-permute-done.6.col1, f32[3,8,128]{2,1,0:T(8,128)S(1)} %collective-permute-done.7.col2, ...), custom_call_target="tpu_custom_call" | custom-call | flops 1000000 | bytes 200000 | tf_op jit(solution)/shard_map/surface/pallas_call | solution.py:285
  (9 shorter events, 0.0 us)
Async XLA Ops:
  1.9 6.2 %collective-permute-start = (f32[4,8,128]{2,1,0:T(8,128)S(1)}, f32[4,8,128]{2,1,0:T(8,128)S(1)}, u32[]{:S(2)}, u32[]{:S(2)}) collective-permute-start(f32[4,8,128]{2,1,0:T(8,128)S(1)} %get-tuple-element.28), channel_id=1, source_target_pairs={{0,64},{64,0},{128,192},{192,128},{256,320},{320,256},{384,448},{4... | collective-permute-start | bytes 49160 | tf_op jit(solution)/shard_map/ppermute | solution.py:268
  3.8 5.1 %collective-permute-start.1 = (f32[4,8,128]{2,1,0:T(8,128)S(1)}, f32[4,8,128]{2,1,0:T(8,128)S(1)}, u32[]{:S(2)}, u32[]{:S(2)}) collective-permute-start(f32[4,8,128]{2,1,0:T(8,128)S(1)} %get-tuple-element.29), channel_id=1, source_target_pairs={{64,128},{192,256},{320,384},{448,512},{576,640},{704,768},{832,89... | collective-permute-start | bytes 49160 | tf_op jit(solution)/shard_map/ppermute | solution.py:267
  8.9 8.7 %collective-permute-start.2 = (f32[4,8,128]{2,1,0:T(8,128)S(1)}, f32[4,8,128]{2,1,0:T(8,128)S(1)}, u32[]{:S(2)}, u32[]{:S(2)}) collective-permute-start(f32[4,8,128]{2,1,0:T(8,128)S(1)} %get-tuple-element.55.after), channel_id=1, source_target_pairs={{0,1},{1,0},{2,3},{3,2},{4,5},{5,4},{6,7},{7,6},{8,9},{9,8},{10,11... | collective-permute-start | bytes 49160 | tf_op jit(solution)/shard_map/ppermute | solution.py:268
  11.3 6.9 %collective-permute-start.3 = (f32[4,8,128]{2,1,0:T(8,128)S(1)}, f32[4,8,128]{2,1,0:T(8,128)S(1)}, u32[]{:S(2)}, u32[]{:S(2)}) collective-permute-start(f32[4,8,128]{2,1,0:T(8,128)S(1)} %get-tuple-element.54), channel_id=1, source_target_pairs={{1,2},{3,4},{5,6},{7,8},{9,10},{11,12},{13,14},{15,16},{17,18},{19... | collective-permute-start | bytes 49160 | tf_op jit(solution)/shard_map/ppermute | solution.py:267
  20.5 4.0 %collective-permute-start.4 = (f32[3,8,128]{2,1,0:T(8,128)S(1)}, f32[3,8,128]{2,1,0:T(8,128)S(1)}, u32[]{:S(2)}, u32[]{:S(2)}) collective-permute-start(f32[3,8,128]{2,1,0:T(8,128)S(1)} %get-tuple-element.46), channel_id=1, source_target_pairs={{0,64},{64,0},{128,192},{192,128},{256,320},{320,256},{384,448},{4... | collective-permute-start | bytes 36872 | tf_op jit(solution)/shard_map/ppermute | solution.py:268
  22.4 5.0 %collective-permute-start.5 = (f32[3,8,128]{2,1,0:T(8,128)S(1)}, f32[3,8,128]{2,1,0:T(8,128)S(1)}, u32[]{:S(2)}, u32[]{:S(2)}) collective-permute-start(f32[3,8,128]{2,1,0:T(8,128)S(1)} %get-tuple-element.47), channel_id=1, source_target_pairs={{64,128},{192,256},{320,384},{448,512},{576,640},{704,768},{832,89... | collective-permute-start | bytes 36872 | tf_op jit(solution)/shard_map/ppermute | solution.py:267
  27.4 13.6 %collective-permute-start.6 = (f32[3,8,128]{2,1,0:T(8,128)S(1)}, f32[3,8,128]{2,1,0:T(8,128)S(1)}, u32[]{:S(2)}, u32[]{:S(2)}) collective-permute-start(f32[3,8,128]{2,1,0:T(8,128)S(1)} %get-tuple-element.59), channel_id=1, source_target_pairs={{0,1},{1,0},{2,3},{3,2},{4,5},{5,4},{6,7},{7,6},{8,9},{9,8},{10,11... | collective-permute-start | bytes 36872 | tf_op jit(solution)/shard_map/ppermute | solution.py:268
  39.1 6.8 %collective-permute-start.7 = (f32[3,8,128]{2,1,0:T(8,128)S(1)}, f32[3,8,128]{2,1,0:T(8,128)S(1)}, u32[]{:S(2)}, u32[]{:S(2)}) collective-permute-start(f32[3,8,128]{2,1,0:T(8,128)S(1)} %get-tuple-element.58), channel_id=1, source_target_pairs={{1,2},{3,4},{5,6},{7,8},{9,10},{11,12},{13,14},{15,16},{17,18},{19... | collective-permute-start | bytes 36872 | tf_op jit(solution)/shard_map/ppermute | solution.py:267

commit v3 on v2

--- a/solution.py
+++ b/solution.py
@@ -10,7 +10,7 @@
 WIN_R = 8
 WIN_C = 16
 OFF = 64
-SPLIT = 5
+SPLIT = 4
 VMEM = pl.BlockSpec(memory_space=pltpu.VMEM)
 HBM = pl.BlockSpec(memory_space=pltpu.HBM)
 F32 = jnp.float32
@@ -28,8 +28,8 @@
     return high, low
 
 
-def is_even(axis):
-    return lax.axis_index(axis) % 2 == 0
+def far_is_plus(axis):
+    return lax.axis_index(axis) % 2 == 1
 
 
 def pack_kernel(
@@ -47,17 +47,21 @@
     for copy in copies:
         copy.start()
     slots = index.shape[2]
-    even = is_even("row")
+    plus = far_is_plus("row")
     index_scr[...] = jnp.zeros_like(index_scr)
     flux_scr[...] = jnp.zeros_like(flux_scr)
     for copy in copies[:5]:
         copy.wait()
     for i in range(9):
         index_scr[i : i + 1, 0:slots] = index_kept[i]
-    flux_scr[:, 0 : flux.shape[1]] = lax.dot_general(
-        coupling_in[...], flux_in[...], (((1,), (0,)), ((), ())),
-        precision=lax.Precision.HIGHEST, preferred_element_type=F32,
-    )
+    size = (8, flux.shape[1])
+    terms = [
+        jnp.broadcast_to(coupling_in[:, f : f + 1], size) * jnp.broadcast_to(flux_in[f : f + 1, :], size)
+        for f in range(flux.shape[0])
+    ]
+    while len(terms) > 1:
+        terms = [sum(terms[i : i + 2]) for i in range(0, len(terms), 2)]
+    flux_scr[:, 0 : flux.shape[1]] = terms[0]
     rows = state.shape[0] // 8
     mapped = flux_scr[...]
     lane = lanes_of(mapped.shape)
@@ -75,20 +79,24 @@
         for b in range(3):
             used = jnp.broadcast_to(count_kept[a][:, b : b + 1], mapped.shape)
             places = jnp.broadcast_to(index_scr[3 * a + b : 3 * a + b + 1, :], mapped.shape)
-            picked = jnp.take_along_axis(mapped, places, axis=1)
+            picked = pick(mapped, places)
             flag = ((lane >= OFF) & (lane < OFF + used)).astype(F32)
             groups.append(jnp.where(lane < used, picked, flag))
     for b in range(3):
         up, down = groups[6 + b], groups[b]
-        send1[b] = jnp.where(even, up, down)
-        send2[b] = jnp.where(even, down, up)
+        send1[b] = jnp.where(plus, up, down)
+        send2[b] = jnp.where(plus, down, up)
         own[b] = groups[3 + b]
     first = state_kept[pl.ds(0, 8, stride=rows), :]
     last = state_kept[pl.ds(rows - 1, 8, stride=rows), :]
-    send1[3] = jnp.where(even, last, first)
-    send2[3] = jnp.where(even, first, last)
+    send1[3] = jnp.where(plus, last, first)
+    send2[3] = jnp.where(plus, first, last)
     for copy in copies[5:]:
         copy.wait()
+
+
+def pick(table, lanes):
+    return jnp.take_along_axis(table, lanes, axis=1, mode="promise_in_bounds", wrap_negative_indices=False)
 
 
 def spread_kernel(begin, end, start, weight, after, high, low, start_scr):
@@ -99,6 +107,10 @@
         start_scr[i : i + 1, 0:slots] = start[i].astype(F32)
     turned = start_scr[...].T
     lane = lanes_of((slots, width))
+    source = lax.broadcasted_iota(jnp.int32, (width, WIN_R * width), 0)
+    target = lax.broadcasted_iota(jnp.int32, (width, WIN_R * width), 1)
+    wanted = (target // width) * WIN_C + (target & (WIN_C - 1))
+    copies = (source == wanted).astype(F32).astype(BF16)
     for i in range(begin, end):
         first = turned[0:slots, i : i + 1].astype(jnp.int32)
         top = first // width
@@ -106,32 +118,41 @@
         above = jnp.broadcast_to(top * WIN_C, (slots, width))
         across = lane - left
         inside = (across >= 0) & (across < WIN_C)
-        place = jnp.where(inside, across - above, -(1 << 20))
-        block = weight[0, i // 3, i % 3]
+        turn = (lane - left) & (WIN_C - 1)
+        group = (lane - above) & (WIN_R * WIN_C - WIN_C)
+        block = pick(weight[0, i // 3, i % 3], group + turn)
+        top = jnp.broadcast_to(top, (slots, width))
+        part = block.astype(BF16).astype(F32)
+        both = jnp.concatenate([part, block - part], axis=0).astype(BF16)
+        both = jnp.dot(both, copies, preferred_element_type=F32)
         at_rows = slice((i - begin) * slots, (i - begin + 1) * slots)
-        for y in range(rows):
-            at = place + y * WIN_C
-            hit = (at >= 0) & (at < WIN_R * WIN_C)
-            value = jnp.take_along_axis(block, at & (width - 1), axis=1)
-            value = jnp.where(hit, value, 0.0)
-            part, rest = halves(value)
-            high[at_rows, y * width : (y + 1) * width] = part
-            low[at_rows, y * width : (y + 1) * width] = rest
-
-
-def hot_kernel(index, count, after, hot, index_scr):
+        for y in range(WIN_R):
+            part = jnp.where(inside, both[:slots, y * width : (y + 1) * width], 0.0)
+            rest = jnp.where(inside, both[slots:, y * width : (y + 1) * width], 0.0)
+            late = top > y
+            for to, keep in ((y, ~late), (y + WIN_R, late)):
+                columns = slice(to * width, (to + 1) * width)
+                high[at_rows, columns] = jnp.where(keep, part, 0.0).astype(BF16)
+                low[at_rows, columns] = jnp.where(keep, rest, 0.0).astype(BF16)
+
+
+def hot_kernel(index, count, fresh, hot, new_state, index_scr, sem):
+    store = pltpu.make_async_copy(fresh, new_state, sem)
+    store.start()
     slots = index.shape[2]
-    cells, width = hot.shape[0], index_scr.shape[1]
+    cells, width = hot.shape[1], index_scr.shape[1]
     index_scr[...] = jnp.zeros_like(index_scr)
     for i in range(9):
         index_scr[i : i + 1, 0:slots] = index[i]
     lane = lanes_of((1, width))
-    cell = lax.broadcasted_iota(jnp.int32, (cells, width), 0)
+    used = [lane < jnp.broadcast_to(count[i // 3][:, i % 3 : i % 3 + 1], (1, width)) for i in range(9)]
+    places = [jnp.where(used[i], index_scr[i : i + 1, :], -1) for i in range(9)]
+    turned = jnp.concatenate(places + [places[0]] * 7, axis=0).astype(F32).T.astype(jnp.int32)
+    cell = lanes_of((width, cells))
     for i in range(9):
-        used = lane < jnp.broadcast_to(count[i // 3][:, i % 3 : i % 3 + 1], (1, width))
-        places = jnp.where(used, index_scr[i : i + 1, :], -1)
-        here = jnp.broadcast_to(places, (cells, width)) == cell
-        hot[:, i * width : (i + 1) * width] = here.astype(F32).astype(BF16)
+        here = jnp.broadcast_to(turned[:, i : i + 1], (width, cells)) == cell
+        hot[i * width : (i + 1) * width, :] = here.astype(F32).astype(BF16)
+    store.wait()
 
 
 def ocean_kernel(
@@ -142,23 +163,23 @@
     slots = (split + high2.shape[0]) // 9
     width = state.shape[1]
     rows = state.shape[0] // 8
-    even_r = is_even("row")
-    even_c = is_even("col")
-
-    def from_plus(one, two, even, i):
-        return jnp.where(even, one[i], two[i])
-
-    def from_minus(one, two, even, i):
-        return jnp.where(even, two[i], one[i])
-
-    middle = [from_minus(row1, row2, even_r, 1), own[1], from_plus(row1, row2, even_r, 1)]
+    plus_r = far_is_plus("row")
+    plus_c = far_is_plus("col")
+
+    def from_plus(one, two, plus, i):
+        return jnp.where(plus, one[i], two[i])
+
+    def from_minus(one, two, plus, i):
+        return jnp.where(plus, two[i], one[i])
+
+    middle = [from_minus(row1, row2, plus_r, 1), own[1], from_plus(row1, row2, plus_r, 1)]
     blocks = []
     for p in range(3):
-        blocks += [from_minus(col1, col2, even_c, p), middle[p], from_plus(col1, col2, even_c, p)]
-    south_edge = from_minus(row1, row2, even_r, 3)
-    north_edge = from_plus(row1, row2, even_r, 3)
-    west_edge = from_minus(col1, col2, even_c, 3)
-    east_edge = from_plus(col1, col2, even_c, 3)
+        blocks += [from_minus(col1, col2, plus_c, p), middle[p], from_plus(col1, col2, plus_c, p)]
+    south_edge = from_minus(row1, row2, plus_r, 3)
+    north_edge = from_plus(row1, row2, plus_r, 3)
+    west_edge = from_minus(col1, col2, plus_c, 3)
+    east_edge = from_plus(col1, col2, plus_c, 3)
 
     def left_of(group):
         fields = jnp.concatenate([block[:, 0:slots] for block in group], axis=1)
@@ -223,33 +244,33 @@
             out.append(jnp.concatenate([back[0:8, at], pad, back[8:16, at], pad], axis=1))
     for q in range(3):
         up, down = out[6 + q], out[q]
-        send1[q] = jnp.where(even_r, up, down)
-        send2[q] = jnp.where(even_r, down, up)
+        send1[q] = jnp.where(plus_r, up, down)
+        send2[q] = jnp.where(plus_r, down, up)
         back_own[q] = out[3 + q]
 
 
 def surface_kernel(row1, row2, col1, col2, own, hot, result):
     cells = result.shape[1]
-    even_r = is_even("row")
-    even_c = is_even("col")
+    plus_r = far_is_plus("row")
+    plus_c = far_is_plus("col")
     middle = [
-        jnp.where(even_r, row2[1], row1[1]),
+        jnp.where(plus_r, row2[1], row1[1]),
         own[1],
-        jnp.where(even_r, row1[1], row2[1]),
+        jnp.where(plus_r, row1[1], row2[1]),
     ]
     blocks = []
     for a in range(3):
         blocks += [
-            jnp.where(even_c, col2[a], col1[a]),
+            jnp.where(plus_c, col2[a], col1[a]),
             middle[a],
-            jnp.where(even_c, col1[a], col2[a]),
+            jnp.where(plus_c, col1[a], col2[a]),
         ]
     values = jnp.concatenate(blocks, axis=1)
     weights = jnp.concatenate([pltpu.roll(block, OFF, 1) for block in blocks], axis=1)
     value_high = values.astype(BF16).astype(F32)
     weight_high = weights.astype(BF16).astype(F32)
     left = jnp.concatenate([value_high, weight_high, values - value_high, weights - weight_high], axis=0)
-    total = lax.dot_general(left.astype(BF16), hot[...], NT, preferred_element_type=F32)
+    total = jnp.dot(left.astype(BF16), hot[...], preferred_element_type=F32)
     total = total[0:16] + total[16:32]
     cover = jnp.maximum(jnp.broadcast_to(total[8:9], (8, cells)), 1.0)
     result[...] = total[0:8] / cover
@@ -264,29 +285,29 @@
 
 def exchange(send1, send2, axis):
     near, far = swaps(lax.axis_size(axis))
-    two = lax.ppermute(send2, axis, far)
-    one = lax.ppermute(send1, axis, near)
+    one = lax.ppermute(send1, axis, far)
+    two = lax.ppermute(send2, axis, near)
     return one, two
 
 
-def column_sends(row1, row2, own, extra, even_r, even_c):
-    minus = jnp.where(even_r, row2, row1)
-    plus = jnp.where(even_r, row1, row2)
+def column_sends(row1, row2, own, extra, plus_r, plus_c):
+    minus = jnp.where(plus_r, row2, row1)
+    plus = jnp.where(plus_r, row1, row2)
     low = jnp.stack([minus[0], own[0], plus[0]] + [edge for edge in extra[:1]])
     high = jnp.stack([minus[2], own[2], plus[2]] + [edge for edge in extra[1:]])
-    return jnp.where(even_c, high, low), jnp.where(even_c, low, high)
+    return jnp.where(plus_c, high, low), jnp.where(plus_c, low, high)
 
 
 def in_hbm(array):
     return pltpu.with_memory_space_constraint(array, pltpu.HBM)
 
 
-def call(kernel, outs, scratch, specs, flops, size, *args, name):
+def call(kernel, outs, scratch, specs, flops, size, *args, name, out_specs=None):
     return pl.pallas_call(
         kernel,
         out_shape=outs,
         in_specs=specs,
-        out_specs=[VMEM] * len(outs),
+        out_specs=out_specs or [VMEM] * len(outs),
         scratch_shapes=scratch,
         compiler_params=pltpu.CompilerParams(vmem_limit_bytes=24 * 1024 * 1024),
         cost_estimate=pl.CostEstimate(flops=flops, bytes_accessed=size, transcendentals=0),
@@ -310,8 +331,8 @@
     slots = send_index.shape[3]
     cells = rows * width
     atm_cells = atm_flux.shape[1]
-    even_r = is_even("row")
-    even_c = is_even("col")
+    plus_r = far_is_plus("row")
+    plus_c = far_is_plus("col")
     state = ocean_state.reshape(fields * rows, width)
     index = send_index.reshape(9, 1, slots)
     count = send_count.reshape(3, 1, 3)
@@ -353,10 +374,10 @@
     row1, row2 = exchange(send1, send2, "row")
     high1, low1 = spread(0, SPLIT, own, "spread_one")
     row1, row2, high1, low1 = lax.optimization_barrier((row1, row2, high1, low1))
-    send1, send2 = column_sends(row1, row2, own, [own[3], own[4]], even_r, even_c)
+    send1, send2 = column_sends(row1, row2, own, [own[3], own[4]], plus_r, plus_c)
     col1, col2 = exchange(send1, send2, "col")
     high2, low2 = spread(SPLIT, 9, send1, "spread_two")
-    new_state, send1, send2, own = call(
+    fresh, send1, send2, own = call(
         ocean_kernel,
         [shape(fields * rows, width), shape(3, 8, width), shape(3, 8, width), shape(3, 8, width)],
         [pltpu.VMEM((32, cells), BF16)],
@@ -366,17 +387,18 @@
         name="ocean",
     )
     row1, row2 = exchange(send1, send2, "row")
-    (hot,) = call(
+    hot, new_state = call(
         hot_kernel,
-        [shape(atm_cells, 9 * width, dtype=BF16)],
-        [pltpu.VMEM((16, width), jnp.int32)],
+        [shape(9 * width, atm_cells, dtype=BF16), shape(fields * rows, width)],
+        [pltpu.VMEM((16, width), jnp.int32), pltpu.SemaphoreType.DMA],
         [VMEM] * 3,
         1_000_000, 200_000,
-        index, count, own,
+        index, count, fresh,
+        out_specs=[VMEM, HBM],
         name="hot",
     )
     row1, row2, hot = lax.optimization_barrier((row1, row2, hot))
-    send1, send2 = column_sends(row1, row2, own, [], even_r, even_c)
+    send1, send2 = column_sends(row1, row2, own, [], plus_r, plus_c)
     col1, col2 = exchange(send1, send2, "col")
     (result,) = call(
         surface_kernel,

time: 47.2 us -> 39.9 us (0.85)
  the two profiles are of different devices: /device:TPU:22 before, /device:TPU:430 now
where the time goes in v3:
time: 39.9 us; the launch traced here: 39.6 us
  starting transfers between devices  25.8 us (65%)
  Pallas kernels  6.44 us (16%)
  waiting for transfers between devices  6.41 us (16%)
  between operations  0.84 us (2%)
    ppermute x4, starting transfers between devices, exchange(): one = lax.ppermute(send1, axis, far)  13.4 us
    ppermute x4, starting transfers between devices, exchange(): two = lax.ppermute(send2, axis, near)  12.5 us
    pallas_call x6, Pallas kernels, call(): pl.pallas_call(kernel, out_shape=outs, in_specs=specs, out_specs=out_spec...  6.44 us
    ppermute x4, waiting for transfers between devices, exchange(): one = lax.ppermute(send1, axis, far)  3.66 us
    ppermute x4, waiting for transfers between devices, exchange(): two = lax.ppermute(send2, axis, near)  2.74 us
  transfers between devices with their start and end apart: 8, of which 3 were waited for; matrix products, arithmetic and copies ran while one was open for 0% of the time, Pallas kernels for 7%

profile of v3, /device:TPU:430, one launch (start us, length us, event | category | flops | bytes accessed | tf_op | source)
XLA Modules:
  0.0 39.6 jit_solution(5373497974243389485)
XLA Ops:
  0.6 1.2 %pack.1 = (f32[4,8,128]{2,1,0:T(8,128)S(1)}, f32[4,8,128]{2,1,0:T(8,128)S(1)}, f32[5,8,128]{2,1,0:T(8,128)S(1)}, s32[9,1,48]{2,1,0:T(1,128)S(1)}, s32[3,1,3]{2,1...) custom-call(f32[20,96]{1,0:T(8,128)} %flux.1, ...), custom_call_target="tpu_custom_call" | custom-call | flops 100000 | bytes 1000000 | tf_op jit(solution)/shard_map/pack/pallas_call | solution.py:306
  1.8 1.9 %collective-permute-start = (f32[4,8,128]{2,1,0:T(8,128)S(1)}, f32[4,8,128]{2,1,0:T(8,128)S(1)}, u32[]{:S(2)}, u32[]{:S(2)}) collective-permute-start(f32[4,8,128]{2,1,0:T(8,128)S(1)} %get-tuple-element.32), channel_id=1, source_target_pairs={{64,128},{192,256},{320,384},{448,512},{576,640},{704,768},{832,89... | collective-permute-start | bytes 49160 | tf_op jit(solution)/shard_map/ppermute | solution.py:288
  3.8 3.7 %collective-permute-start.1 = (f32[4,8,128]{2,1,0:T(8,128)S(1)}, f32[4,8,128]{2,1,0:T(8,128)S(1)}, u32[]{:S(2)}, u32[]{:S(2)}) collective-permute-start(f32[4,8,128]{2,1,0:T(8,128)S(1)} %get-tuple-element.33), channel_id=1, source_target_pairs={{0,64},{64,0},{128,192},{192,128},{256,320},{320,256},{384,448},{4... | collective-permute-start | bytes 49160 | tf_op jit(solution)/shard_map/ppermute | solution.py:289
  7.5 0.9 %spread_one.1 = (bf16[192,2048]{1,0:T(8,128)(2,1)S(1)}, bf16[192,2048]{1,0:T(8,128)(2,1)S(1)}) custom-call(s32[9,1,48]{2,1,0:T(1,128)S(1)} %get-tuple-element.34.start, f32[1,3,3,48,128]{4,3,2,1,0:T(8,128)S(1)} %get-tuple-element.35.weight, f32[5,8,128]{2,1,0:T(8,128)S(1)} %get-tuple-element.36.after.own), custom_call_target="tpu_custom_call" | custom-call | flops 20000000 | bytes 4000000 | tf_op jit(solution)/shard_map/spread_one/pallas_call | solution.py:306
  8.5 0.0 collective-permute-done.row1
  8.5 0.0 collective-permute-done.1.row2
  8.5 6.2 %collective-permute-start.2 = (f32[4,8,128]{2,1,0:T(8,128)S(1)}, f32[4,8,128]{2,1,0:T(8,128)S(1)}, u32[]{:S(2)}, u32[]{:S(2)}) collective-permute-start(f32[4,8,128]{2,1,0:T(8,128)S(1)} %get-tuple-element.59.after), channel_id=1, source_target_pairs={{1,2},{3,4},{5,6},{7,8},{9,10},{11,12},{13,14},{15,16},{17,18},{19... | collective-permute-start | bytes 49160 | tf_op jit(solution)/shard_map/ppermute | solution.py:288
  14.7 1.9 %collective-permute-start.3 = (f32[4,8,128]{2,1,0:T(8,128)S(1)}, f32[4,8,128]{2,1,0:T(8,128)S(1)}, u32[]{:S(2)}, u32[]{:S(2)}) collective-permute-start(f32[4,8,128]{2,1,0:T(8,128)S(1)} %get-tuple-element.58), channel_id=1, source_target_pairs={{0,1},{1,0},{2,3},{3,2},{4,5},{5,4},{6,7},{7,6},{8,9},{9,8},{10,11... | collective-permute-start | bytes 49160 | tf_op jit(solution)/shard_map/ppermute | solution.py:289
  16.7 1.1 %spread_two.1 = (bf16[240,2048]{1,0:T(8,128)(2,1)S(1)}, bf16[240,2048]{1,0:T(8,128)(2,1)S(1)}) custom-call(s32[9,1,48]{2,1,0:T(1,128)S(1)} %get-tuple-element.34.start, f32[1,3,3,48,128]{4,3,2,1,0:T(8,128)S(1)} %get-tuple-element.35.weight, f32[4,8,128]{2,1,0:T(8,128)S(1)} %get-tuple-element.59.after), custom_call_target="tpu_custom_call" | custom-call | flops 20000000 | bytes 4000000 | tf_op jit(solution)/shard_map/spread_two/pallas_call | solution.py:306
  17.8 0.0 collective-permute-done.2.col1
  17.8 2.6 %collective-permute-done.3.col2 = f32[4,8,128]{2,1,0:T(8,128)S(1)} collective-permute-done((f32[4,8,128]{2,1,0:T(8,128)S(1)}, f32[4,8,128]{2,1,0:T(8,128)S(1)}, u32[]{:S(2)}, u32[]{:S(2)}) %collective-permute-start.3) | collective-permute-done | bytes 16416 | tf_op jit(solution)/shard_map/ppermute | solution.py:289
  20.4 1.7 %ocean.1 = (f32[128,128]{1,0:T(8,128)S(1)}, f32[3,8,128]{2,1,0:T(8,128)S(1)}, f32[3,8,128]{2,1,0:T(8,128)S(1)}, f32[3,8,128]{2,1,0:T(8,128)S(1)}) custom-call(f32[4,8,128]{2,1,0:T(8,128)S(1)} %collective-permute-done.row1, f32[4,8,128]{2,1,0:T(8,128)S(1)} %collective-permute-done.1.row2, f32[4,8,128]{2,1,0:T(8,128)S(1)} %collective-permute-done.2.col1, ...), custom_call_target="tpu_custom_call" | custom-call | flops 100000000 | bytes 4000000 | tf_op jit(solution)/shard_map/ocean/pallas_call | solution.py:306
  22.1 1.9 %collective-permute-start.4 = (f32[3,8,128]{2,1,0:T(8,128)S(1)}, f32[3,8,128]{2,1,0:T(8,128)S(1)}, u32[]{:S(2)}, u32[]{:S(2)}) collective-permute-start(f32[3,8,128]{2,1,0:T(8,128)S(1)} %get-tuple-element.51), channel_id=1, source_target_pairs={{64,128},{192,256},{320,384},{448,512},{576,640},{704,768},{832,89... | collective-permute-start | bytes 36872 | tf_op jit(solution)/shard_map/ppermute | solution.py:288
  24.0 4.9 %collective-permute-start.5 = (f32[3,8,128]{2,1,0:T(8,128)S(1)}, f32[3,8,128]{2,1,0:T(8,128)S(1)}, u32[]{:S(2)}, u32[]{:S(2)}) collective-permute-start(f32[3,8,128]{2,1,0:T(8,128)S(1)} %get-tuple-element.52), channel_id=1, source_target_pairs={{0,64},{64,0},{128,192},{192,128},{256,320},{320,256},{384,448},{4... | collective-permute-start | bytes 36872 | tf_op jit(solution)/shard_map/ppermute | solution.py:289
  29.0 0.6 %hot.1 = (bf16[1152,96]{1,0:T(8,128)(2,1)S(1)}, f32[128,128]{1,0:T(8,128)}) custom-call(s32[9,1,48]{2,1,0:T(1,128)S(1)} %get-tuple-element.30.index, s32[3,1,3]{2,1,0:T(1,128)S(1)} %get-tuple-element.31.count, f32[128,128]{1,0:T(8,128)S(1)} %get-tuple-element.49.fresh), custom_call_target="tpu_custom_call" | custom-call | flops 1000000 | bytes 200000 | tf_op jit(solution)/shard_map/hot/pallas_call | solution.py:306
  29.6 0.0 collective-permute-done.4.row1
  29.6 0.1 collective-permute-done.5.row2
  29.8 3.3 %collective-permute-start.6 = (f32[3,8,128]{2,1,0:T(8,128)S(1)}, f32[3,8,128]{2,1,0:T(8,128)S(1)}, u32[]{:S(2)}, u32[]{:S(2)}) collective-permute-start(f32[3,8,128]{2,1,0:T(8,128)S(1)} %get-tuple-element.63), channel_id=1, source_target_pairs={{1,2},{3,4},{5,6},{7,8},{9,10},{11,12},{13,14},{15,16},{17,18},{19... | collective-permute-start | bytes 36872 | tf_op jit(solution)/shard_map/ppermute | solution.py:288
  33.1 1.9 %collective-permute-start.7 = (f32[3,8,128]{2,1,0:T(8,128)S(1)}, f32[3,8,128]{2,1,0:T(8,128)S(1)}, u32[]{:S(2)}, u32[]{:S(2)}) collective-permute-start(f32[3,8,128]{2,1,0:T(8,128)S(1)} %get-tuple-element.62), channel_id=1, source_target_pairs={{0,1},{1,0},{2,3},{3,2},{4,5},{5,4},{6,7},{7,6},{8,9},{9,8},{10,11... | collective-permute-start | bytes 36872 | tf_op jit(solution)/shard_map/ppermute | solution.py:289
  35.0 3.7 %collective-permute-done.6.col1 = f32[3,8,128]{2,1,0:T(8,128)S(1)} collective-permute-done((f32[3,8,128]{2,1,0:T(8,128)S(1)}, f32[3,8,128]{2,1,0:T(8,128)S(1)}, u32[]{:S(2)}, u32[]{:S(2)}) %collective-permute-start.6) | collective-permute-done | bytes 12320 | tf_op jit(solution)/shard_map/ppermute | solution.py:288
  38.7 0.0 collective-permute-done.7.col2
  38.7 0.9 %surface.1 = f32[8,96]{1,0:T(8,128)} custom-call(f32[3,8,128]{2,1,0:T(8,128)S(1)} %collective-permute-done.4.row1, f32[3,8,128]{2,1,0:T(8,128)S(1)} %collective-permute-done.5.row2, f32[3,8,128]{2,1,0:T(8,128)S(1)} %collective-permute-done.6.col1, f32[3,8,128]{2,1,0:T(8,128)S(1)} %collective-permute-done.7.col2, f32[3,8,128]{2,1,0:T(8,128)S(1)} %get-tuple-element.56.own, ...), custom_call_target="tpu_custom_call" | custom-call | flops 1000000 | bytes 200000 | tf_op jit(solution)/shard_map/surface/pallas_call | solution.py:306
  (9 shorter events, 0.0 us)
Async XLA Ops:
  1.8 6.6 %collective-permute-start = (f32[4,8,128]{2,1,0:T(8,128)S(1)}, f32[4,8,128]{2,1,0:T(8,128)S(1)}, u32[]{:S(2)}, u32[]{:S(2)}) collective-permute-start(f32[4,8,128]{2,1,0:T(8,128)S(1)} %get-tuple-element.32), channel_id=1, source_target_pairs={{64,128},{192,256},{320,384},{448,512},{576,640},{704,768},{832,89... | collective-permute-start | bytes 49160 | tf_op jit(solution)/shard_map/ppermute | solution.py:288
  3.8 4.7 %collective-permute-start.1 = (f32[4,8,128]{2,1,0:T(8,128)S(1)}, f32[4,8,128]{2,1,0:T(8,128)S(1)}, u32[]{:S(2)}, u32[]{:S(2)}) collective-permute-start(f32[4,8,128]{2,1,0:T(8,128)S(1)} %get-tuple-element.33), channel_id=1, source_target_pairs={{0,64},{64,0},{128,192},{192,128},{256,320},{320,256},{384,448},{4... | collective-permute-start | bytes 49160 | tf_op jit(solution)/shard_map/ppermute | solution.py:289
  8.5 9.2 %collective-permute-start.2 = (f32[4,8,128]{2,1,0:T(8,128)S(1)}, f32[4,8,128]{2,1,0:T(8,128)S(1)}, u32[]{:S(2)}, u32[]{:S(2)}) collective-permute-start(f32[4,8,128]{2,1,0:T(8,128)S(1)} %get-tuple-element.59.after), channel_id=1, source_target_pairs={{1,2},{3,4},{5,6},{7,8},{9,10},{11,12},{13,14},{15,16},{17,18},{19... | collective-permute-start | bytes 49160 | tf_op jit(solution)/shard_map/ppermute | solution.py:288
  14.7 5.6 %collective-permute-start.3 = (f32[4,8,128]{2,1,0:T(8,128)S(1)}, f32[4,8,128]{2,1,0:T(8,128)S(1)}, u32[]{:S(2)}, u32[]{:S(2)}) collective-permute-start(f32[4,8,128]{2,1,0:T(8,128)S(1)} %get-tuple-element.58), channel_id=1, source_target_pairs={{0,1},{1,0},{2,3},{3,2},{4,5},{5,4},{6,7},{7,6},{8,9},{9,8},{10,11... | collective-permute-start | bytes 49160 | tf_op jit(solution)/shard_map/ppermute | solution.py:289
  22.1 7.5 %collective-permute-start.4 = (f32[3,8,128]{2,1,0:T(8,128)S(1)}, f32[3,8,128]{2,1,0:T(8,128)S(1)}, u32[]{:S(2)}, u32[]{:S(2)}) collective-permute-start(f32[3,8,128]{2,1,0:T(8,128)S(1)} %get-tuple-element.51), channel_id=1, source_target_pairs={{64,128},{192,256},{320,384},{448,512},{576,640},{704,768},{832,89... | collective-permute-start | bytes 36872 | tf_op jit(solution)/shard_map/ppermute | solution.py:288
  24.0 5.7 %collective-permute-start.5 = (f32[3,8,128]{2,1,0:T(8,128)S(1)}, f32[3,8,128]{2,1,0:T(8,128)S(1)}, u32[]{:S(2)}, u32[]{:S(2)}) collective-permute-start(f32[3,8,128]{2,1,0:T(8,128)S(1)} %get-tuple-element.52), channel_id=1, source_target_pairs={{0,64},{64,0},{128,192},{192,128},{256,320},{320,256},{384,448},{4... | collective-permute-start | bytes 36872 | tf_op jit(solution)/shard_map/ppermute | solution.py:289
  29.8 8.9 %collective-permute-start.6 = (f32[3,8,128]{2,1,0:T(8,128)S(1)}, f32[3,8,128]{2,1,0:T(8,128)S(1)}, u32[]{:S(2)}, u32[]{:S(2)}) collective-permute-start(f32[3,8,128]{2,1,0:T(8,128)S(1)} %get-tuple-element.63), channel_id=1, source_target_pairs={{1,2},{3,4},{5,6},{7,8},{9,10},{11,12},{13,14},{15,16},{17,18},{19... | collective-permute-start | bytes 36872 | tf_op jit(solution)/shard_map/ppermute | solution.py:288
  33.1 5.6 %collective-permute-start.7 = (f32[3,8,128]{2,1,0:T(8,128)S(1)}, f32[3,8,128]{2,1,0:T(8,128)S(1)}, u32[]{:S(2)}, u32[]{:S(2)}) collective-permute-start(f32[3,8,128]{2,1,0:T(8,128)S(1)} %get-tuple-element.62), channel_id=1, source_target_pairs={{0,1},{1,0},{2,3},{3,2},{4,5},{5,4},{6,7},{7,6},{8,9},{9,8},{10,11... | collective-permute-start | bytes 36872 | tf_op jit(solution)/shard_map/ppermute | solution.py:289

commit v4 on v3

--- a/solution.py
+++ b/solution.py
@@ -10,7 +10,6 @@
 WIN_R = 8
 WIN_C = 16
 OFF = 64
-SPLIT = 4
 VMEM = pl.BlockSpec(memory_space=pltpu.VMEM)
 HBM = pl.BlockSpec(memory_space=pltpu.HBM)
 F32 = jnp.float32
@@ -136,7 +135,7 @@
                 low[at_rows, columns] = jnp.where(keep, rest, 0.0).astype(BF16)
 
 
-def hot_kernel(index, count, fresh, hot, new_state, index_scr, sem):
+def hot_kernel(index, count, fresh, after, hot, new_state, index_scr, sem):
     store = pltpu.make_async_copy(fresh, new_state, sem)
     store.start()
     slots = index.shape[2]
@@ -156,11 +155,10 @@
 
 
 def ocean_kernel(
-    row1, row2, col1, col2, own, high1, low1, high2, low2, state, velocity, diffusivity, wet,
+    row1, row2, col1, col2, own, high, low, state, velocity, diffusivity, wet,
     new_state, send1, send2, back_own, surface,
 ):
-    split = high1.shape[0]
-    slots = (split + high2.shape[0]) // 9
+    slots = high.shape[0] // 9
     width = state.shape[1]
     rows = state.shape[0] // 8
     plus_r = far_is_plus("row")
@@ -191,8 +189,7 @@
         parts = [field_high, flags, field_low, jnp.zeros_like(flags)]
         return jnp.concatenate(parts, axis=0).astype(BF16)
 
-    left1 = left_of(blocks[: split // slots])
-    left2 = left_of(blocks[split // slots :])
+    left = left_of(blocks)
 
     lane = lanes_of((8, width))
     row_of = lax.broadcasted_iota(jnp.int32, (8, width), 0)
@@ -204,10 +201,8 @@
     lines = [state[pl.ds(y, 8, stride=rows), :] for y in range(rows)]
     for part in range(rows // 2):
         cells = slice(part * step, (part + 1) * step)
-        sums = jnp.dot(left1, high1[:, cells], preferred_element_type=F32)
-        sums = sums + jnp.dot(left2, high2[:, cells], preferred_element_type=F32)
-        rest = jnp.dot(left1[0:16], low1[:, cells], preferred_element_type=F32)
-        rest = rest + jnp.dot(left2[0:16], low2[:, cells], preferred_element_type=F32)
+        sums = jnp.dot(left, high[:, cells], preferred_element_type=F32)
+        rest = jnp.dot(left[0:16], low[:, cells], preferred_element_type=F32)
         sums = sums[0:16] + sums[16:32] + rest
         for y in (2 * part, 2 * part + 1):
             at = slice((y % 2) * width, (y % 2 + 1) * width)
@@ -234,14 +229,13 @@
             surface[16:32, column] = jnp.concatenate([seen - seen_high, jnp.zeros_like(seen)], axis=0).astype(BF16)
     pad = jnp.zeros((8, OFF - slots), F32)
     out = []
-    for high, low in ((high1, low1), (high2, low2)):
-        back = lax.dot_general(surface[...], high[...], NT, preferred_element_type=F32)
-        back = back[0:16] + back[16:32] + lax.dot_general(
-            surface[0:16, :], low[...], NT, preferred_element_type=F32
-        )
-        for i in range(high.shape[0] // slots):
-            at = slice(i * slots, (i + 1) * slots)
-            out.append(jnp.concatenate([back[0:8, at], pad, back[8:16, at], pad], axis=1))
+    back = lax.dot_general(surface[...], high[...], NT, preferred_element_type=F32)
+    back = back[0:16] + back[16:32] + lax.dot_general(
+        surface[0:16, :], low[...], NT, preferred_element_type=F32
+    )
+    for i in range(9):
+        at = slice(i * slots, (i + 1) * slots)
+        out.append(jnp.concatenate([back[0:8, at], pad, back[8:16, at], pad], axis=1))
     for q in range(3):
         up, down = out[6 + q], out[q]
         send1[q] = jnp.where(plus_r, up, down)
@@ -286,6 +280,7 @@
 def exchange(send1, send2, axis):
     near, far = swaps(lax.axis_size(axis))
     one = lax.ppermute(send1, axis, far)
+    send2, _ = lax.optimization_barrier((send2, send1))
     two = lax.ppermute(send2, axis, near)
     return one, two
 
@@ -360,46 +355,43 @@
         name="pack",
     )
 
-    def spread(begin, end, after, name):
+    def spread(after):
         return call(
-            functools.partial(spread_kernel, begin, end),
-            [shape((end - begin) * slots, cells, dtype=BF16)] * 2,
+            functools.partial(spread_kernel, 0, 9),
+            [shape(9 * slots, cells, dtype=BF16)] * 2,
             [pltpu.VMEM((16, width), F32)],
             [VMEM, VMEM, VMEM],
             20_000_000, 4_000_000,
             start, weight, after,
-            name=name,
+            name="spread",
         )
 
     row1, row2 = exchange(send1, send2, "row")
-    high1, low1 = spread(0, SPLIT, own, "spread_one")
-    row1, row2, high1, low1 = lax.optimization_barrier((row1, row2, high1, low1))
     send1, send2 = column_sends(row1, row2, own, [own[3], own[4]], plus_r, plus_c)
     col1, col2 = exchange(send1, send2, "col")
-    high2, low2 = spread(SPLIT, 9, send1, "spread_two")
+    high, low = spread(send1)
     fresh, send1, send2, own = call(
         ocean_kernel,
         [shape(fields * rows, width), shape(3, 8, width), shape(3, 8, width), shape(3, 8, width)],
         [pltpu.VMEM((32, cells), BF16)],
-        [VMEM] * 13,
+        [VMEM] * 11,
         100_000_000, 4_000_000,
-        row1, row2, col1, col2, own, high1, low1, high2, low2, state, velocity, diffusivity, wet,
+        row1, row2, col1, col2, own, high, low, state, velocity, diffusivity, wet,
         name="ocean",
     )
     row1, row2 = exchange(send1, send2, "row")
+    send1, send2 = column_sends(row1, row2, own, [], plus_r, plus_c)
+    col1, col2 = exchange(send1, send2, "col")
     hot, new_state = call(
         hot_kernel,
         [shape(9 * width, atm_cells, dtype=BF16), shape(fields * rows, width)],
         [pltpu.VMEM((16, width), jnp.int32), pltpu.SemaphoreType.DMA],
-        [VMEM] * 3,
+        [VMEM] * 4,
         1_000_000, 200_000,
-        index, count, fresh,
+        index, count, fresh, send1,
         out_specs=[VMEM, HBM],
         name="hot",
     )
-    row1, row2, hot = lax.optimization_barrier((row1, row2, hot))
-    send1, send2 = column_sends(row1, row2, own, [], plus_r, plus_c)
-    col1, col2 = exchange(send1, send2, "col")
     (result,) = call(
         surface_kernel,
         [shape(fields, atm_cells)],

time: 39.9 us -> 39.7 us (level)
    ppermute x4, waiting for transfers between devices: 2.74 us -> 3.47 us  [exchange(): two = lax.ppermute(send2, axis, near)]
    ppermute x4, waiting for transfers between devices: 3.66 us -> 3.01 us  [exchange(): one = lax.ppermute(send1, axis, far)]
    pallas_call x6 -> x5, Pallas kernels: 6.44 us -> 6.2 us  [call(): pl.pallas_call(kernel, out_shape=outs, in_specs=specs, out_specs=out_spec...]
  transfers between devices with their start and end apart: 8 -> 8, of which waited for: 3 -> 4; matrix products, arithmetic and copies ran while one was open for 0% -> 0% of each run, Pallas kernels for 7% -> 6%
where the time goes in v4:
time: 39.7 us; the launch traced here: 39.4 us
  starting transfers between devices  25.8 us (65%)
  waiting for transfers between devices  6.48 us (16%)
  Pallas kernels  6.2 us (16%)
  between operations  0.81 us (2%)
    ppermute x4, starting transfers between devices, exchange(): one = lax.ppermute(send1, axis, far)  13.4 us
    ppermute x4, starting transfers between devices, exchange(): two = lax.ppermute(send2, axis, near)  12.5 us
    pallas_call x5, Pallas kernels, call(): pl.pallas_call(kernel, out_shape=outs, in_specs=specs, out_specs=out_spec...  6.2 us
    ppermute x4, waiting for transfers between devices, exchange(): two = lax.ppermute(send2, axis, near)  3.47 us
    ppermute x4, waiting for transfers between devices, exchange(): one = lax.ppermute(send1, axis, far)  3.01 us
  transfers between devices with their start and end apart: 8, of which 4 were waited for; matrix products, arithmetic and copies ran while one was open for 0% of the time, Pallas kernels for 6%

profile of v4, /device:TPU:430, one launch (start us, length us, event | category | flops | bytes accessed | tf_op | source)
XLA Modules:
  0.0 39.4 jit_solution(17895871670293990727)
XLA Ops:
  0.6 1.2 %pack.1 = (f32[4,8,128]{2,1,0:T(8,128)S(1)}, f32[4,8,128]{2,1,0:T(8,128)S(1)}, f32[5,8,128]{2,1,0:T(8,128)S(1)}, s32[9,1,48]{2,1,0:T(1,128)S(1)}, s32[3,1,3]{2,1...) custom-call(f32[20,96]{1,0:T(8,128)} %flux.1, ...), custom_call_target="tpu_custom_call" | custom-call | flops 100000 | bytes 1000000 | tf_op jit(solution)/shard_map/pack/pallas_call | solution.py:301
  1.8 1.9 %collective-permute-start = (f32[4,8,128]{2,1,0:T(8,128)S(1)}, f32[4,8,128]{2,1,0:T(8,128)S(1)}, u32[]{:S(2)}, u32[]{:S(2)}) collective-permute-start(f32[4,8,128]{2,1,0:T(8,128)S(1)} %get-tuple-element.27), channel_id=1, source_target_pairs={{64,128},{192,256},{320,384},{448,512},{576,640},{704,768},{832,89... | collective-permute-start | bytes 49160 | tf_op jit(solution)/shard_map/ppermute | solution.py:282
  3.8 3.7 %collective-permute-start.1 = (f32[4,8,128]{2,1,0:T(8,128)S(1)}, f32[4,8,128]{2,1,0:T(8,128)S(1)}, u32[]{:S(2)}, u32[]{:S(2)}) collective-permute-start(f32[4,8,128]{2,1,0:T(8,128)S(1)} %get-tuple-element.29), channel_id=1, source_target_pairs={{0,64},{64,0},{128,192},{192,128},{256,320},{320,256},{384,448},{4... | collective-permute-start | bytes 49160 | tf_op jit(solution)/shard_map/ppermute | solution.py:284
  7.5 0.8 %collective-permute-done.1.row2 = f32[4,8,128]{2,1,0:T(8,128)S(1)} collective-permute-done((f32[4,8,128]{2,1,0:T(8,128)S(1)}, f32[4,8,128]{2,1,0:T(8,128)S(1)}, u32[]{:S(2)}, u32[]{:S(2)}) %collective-permute-start.1) | collective-permute-done | bytes 16416 | tf_op jit(solution)/shard_map/ppermute | solution.py:284
  8.3 0.0 collective-permute-done.row1
  8.3 6.2 %collective-permute-start.2 = (f32[4,8,128]{2,1,0:T(8,128)S(1)}, f32[4,8,128]{2,1,0:T(8,128)S(1)}, u32[]{:S(2)}, u32[]{:S(2)}) collective-permute-start(f32[4,8,128]{2,1,0:T(8,128)S(1)} %get-tuple-element.49.after), channel_id=1, source_target_pairs={{1,2},{3,4},{5,6},{7,8},{9,10},{11,12},{13,14},{15,16},{17,18},{19... | collective-permute-start | bytes 49160 | tf_op jit(solution)/shard_map/ppermute | solution.py:282
  14.6 1.9 %collective-permute-start.3 = (f32[4,8,128]{2,1,0:T(8,128)S(1)}, f32[4,8,128]{2,1,0:T(8,128)S(1)}, u32[]{:S(2)}, u32[]{:S(2)}) collective-permute-start(f32[4,8,128]{2,1,0:T(8,128)S(1)} %get-tuple-element.31), channel_id=1, source_target_pairs={{0,1},{1,0},{2,3},{3,2},{4,5},{5,4},{6,7},{7,6},{8,9},{9,8},{10,11... | collective-permute-start | bytes 49160 | tf_op jit(solution)/shard_map/ppermute | solution.py:284
  16.5 1.8 %spread.1 = (bf16[432,2048]{1,0:T(8,128)(2,1)S(1)}, bf16[432,2048]{1,0:T(8,128)(2,1)S(1)}) custom-call(s32[9,1,48]{2,1,0:T(1,128)S(1)} %get-tuple-element.32.start, f32[1,3,3,48,128]{4,3,2,1,0:T(8,128)S(1)} %get-tuple-element.33.weight, f32[4,8,128]{2,1,0:T(8,128)S(1)} %get-tuple-element.49.after), custom_call_target="tpu_custom_call" | custom-call | flops 20000000 | bytes 4000000 | tf_op jit(solution)/shard_map/spread/pallas_call | solution.py:301
  18.3 0.0 collective-permute-done.2.col1
  18.3 1.9 %collective-permute-done.3.col2 = f32[4,8,128]{2,1,0:T(8,128)S(1)} collective-permute-done((f32[4,8,128]{2,1,0:T(8,128)S(1)}, f32[4,8,128]{2,1,0:T(8,128)S(1)}, u32[]{:S(2)}, u32[]{:S(2)}) %collective-permute-start.3) | collective-permute-done | bytes 16416 | tf_op jit(solution)/shard_map/ppermute | solution.py:284
  20.2 1.7 %ocean.1 = (f32[128,128]{1,0:T(8,128)S(1)}, f32[3,8,128]{2,1,0:T(8,128)S(1)}, f32[3,8,128]{2,1,0:T(8,128)S(1)}, f32[3,8,128]{2,1,0:T(8,128)S(1)}) custom-call(f32[4,8,128]{2,1,0:T(8,128)S(1)} %collective-permute-done.row1, f32[4,8,128]{2,1,0:T(8,128)S(1)} %collective-permute-done.1.row2, f32[4,8,128]{2,1,0:T(8,128)S(1)} %collective-permute-done.2.col1, ...), custom_call_target="tpu_custom_call" | custom-call | flops 100000000 | bytes 4000000 | tf_op jit(solution)/shard_map/ocean/pallas_call | solution.py:301
  21.9 1.9 %collective-permute-start.5 = (f32[3,8,128]{2,1,0:T(8,128)S(1)}, f32[3,8,128]{2,1,0:T(8,128)S(1)}, u32[]{:S(2)}, u32[]{:S(2)}) collective-permute-start(f32[3,8,128]{2,1,0:T(8,128)S(1)} %get-tuple-element.42), channel_id=1, source_target_pairs={{64,128},{192,256},{320,384},{448,512},{576,640},{704,768},{832,89... | collective-permute-start | bytes 36872 | tf_op jit(solution)/shard_map/ppermute | solution.py:282
  23.8 4.9 %collective-permute-start.4 = (f32[3,8,128]{2,1,0:T(8,128)S(1)}, f32[3,8,128]{2,1,0:T(8,128)S(1)}, u32[]{:S(2)}, u32[]{:S(2)}) collective-permute-start(f32[3,8,128]{2,1,0:T(8,128)S(1)} %get-tuple-element.43), channel_id=1, source_target_pairs={{0,64},{64,0},{128,192},{192,128},{256,320},{320,256},{384,448},{4... | collective-permute-start | bytes 36872 | tf_op jit(solution)/shard_map/ppermute | solution.py:284
  28.8 0.8 %collective-permute-done.4.row2 = f32[3,8,128]{2,1,0:T(8,128)S(1)} collective-permute-done((f32[3,8,128]{2,1,0:T(8,128)S(1)}, f32[3,8,128]{2,1,0:T(8,128)S(1)}, u32[]{:S(2)}, u32[]{:S(2)}) %collective-permute-start.4) | collective-permute-done | bytes 12320 | tf_op jit(solution)/shard_map/ppermute | solution.py:284
  29.6 0.0 collective-permute-done.5.row1
  29.6 3.3 %collective-permute-start.6 = (f32[3,8,128]{2,1,0:T(8,128)S(1)}, f32[3,8,128]{2,1,0:T(8,128)S(1)}, u32[]{:S(2)}, u32[]{:S(2)}) collective-permute-start(f32[3,8,128]{2,1,0:T(8,128)S(1)} %get-tuple-element.53.after), channel_id=1, source_target_pairs={{1,2},{3,4},{5,6},{7,8},{9,10},{11,12},{13,14},{15,16},{17,18},{19... | collective-permute-start | bytes 36872 | tf_op jit(solution)/shard_map/ppermute | solution.py:282
  32.9 1.9 %collective-permute-start.7 = (f32[3,8,128]{2,1,0:T(8,128)S(1)}, f32[3,8,128]{2,1,0:T(8,128)S(1)}, u32[]{:S(2)}, u32[]{:S(2)}) collective-permute-start(f32[3,8,128]{2,1,0:T(8,128)S(1)} %get-tuple-element.46), channel_id=1, source_target_pairs={{0,1},{1,0},{2,3},{3,2},{4,5},{5,4},{6,7},{7,6},{8,9},{9,8},{10,11... | collective-permute-start | bytes 36872 | tf_op jit(solution)/shard_map/ppermute | solution.py:284
  34.8 0.6 %hot.1 = (bf16[1152,96]{1,0:T(8,128)(2,1)S(1)}, f32[128,128]{1,0:T(8,128)}) custom-call(s32[9,1,48]{2,1,0:T(1,128)S(1)} %get-tuple-element.25.index, s32[3,1,3]{2,1,0:T(1,128)S(1)} %get-tuple-element.26.count, f32[128,128]{1,0:T(8,128)S(1)} %get-tuple-element.40.fresh, f32[3,8,128]{2,1,0:T(8,128)S(1)} %get-tuple-element.53.after), custom_call_target="tpu_custom_call" | custom-call | flops 1000000 | bytes 200000 | tf_op jit(solution)/shard_map/hot/pallas_call | solution.py:301
  35.5 3.0 %collective-permute-done.6.col1 = f32[3,8,128]{2,1,0:T(8,128)S(1)} collective-permute-done((f32[3,8,128]{2,1,0:T(8,128)S(1)}, f32[3,8,128]{2,1,0:T(8,128)S(1)}, u32[]{:S(2)}, u32[]{:S(2)}) %collective-permute-start.6) | collective-permute-done | bytes 12320 | tf_op jit(solution)/shard_map/ppermute | solution.py:282
  38.5 0.0 collective-permute-done.7.col2
  38.5 0.8 %surface.1 = f32[8,96]{1,0:T(8,128)} custom-call(f32[3,8,128]{2,1,0:T(8,128)S(1)} %collective-permute-done.5.row1, f32[3,8,128]{2,1,0:T(8,128)S(1)} %collective-permute-done.4.row2, f32[3,8,128]{2,1,0:T(8,128)S(1)} %collective-permute-done.6.col1, f32[3,8,128]{2,1,0:T(8,128)S(1)} %collective-permute-done.7.col2, f32[3,8,128]{2,1,0:T(8,128)S(1)} %get-tuple-element.44.own, ...), custom_call_target="tpu_custom_call" | custom-call | flops 1000000 | bytes 200000 | tf_op jit(solution)/shard_map/surface/pallas_call | solution.py:301
  (9 shorter events, 0.0 us)
Async XLA Ops:
  1.8 6.5 %collective-permute-start = (f32[4,8,128]{2,1,0:T(8,128)S(1)}, f32[4,8,128]{2,1,0:T(8,128)S(1)}, u32[]{:S(2)}, u32[]{:S(2)}) collective-permute-start(f32[4,8,128]{2,1,0:T(8,128)S(1)} %get-tuple-element.27), channel_id=1, source_target_pairs={{64,128},{192,256},{320,384},{448,512},{576,640},{704,768},{832,89... | collective-permute-start | bytes 49160 | tf_op jit(solution)/shard_map/ppermute | solution.py:282
  3.8 4.5 %collective-permute-start.1 = (f32[4,8,128]{2,1,0:T(8,128)S(1)}, f32[4,8,128]{2,1,0:T(8,128)S(1)}, u32[]{:S(2)}, u32[]{:S(2)}) collective-permute-start(f32[4,8,128]{2,1,0:T(8,128)S(1)} %get-tuple-element.29), channel_id=1, source_target_pairs={{0,64},{64,0},{128,192},{192,128},{256,320},{320,256},{384,448},{4... | collective-permute-start | bytes 49160 | tf_op jit(solution)/shard_map/ppermute | solution.py:284
  8.3 9.9 %collective-permute-start.2 = (f32[4,8,128]{2,1,0:T(8,128)S(1)}, f32[4,8,128]{2,1,0:T(8,128)S(1)}, u32[]{:S(2)}, u32[]{:S(2)}) collective-permute-start(f32[4,8,128]{2,1,0:T(8,128)S(1)} %get-tuple-element.49.after), channel_id=1, source_target_pairs={{1,2},{3,4},{5,6},{7,8},{9,10},{11,12},{13,14},{15,16},{17,18},{19... | collective-permute-start | bytes 49160 | tf_op jit(solution)/shard_map/ppermute | solution.py:282
  14.6 5.6 %collective-permute-start.3 = (f32[4,8,128]{2,1,0:T(8,128)S(1)}, f32[4,8,128]{2,1,0:T(8,128)S(1)}, u32[]{:S(2)}, u32[]{:S(2)}) collective-permute-start(f32[4,8,128]{2,1,0:T(8,128)S(1)} %get-tuple-element.31), channel_id=1, source_target_pairs={{0,1},{1,0},{2,3},{3,2},{4,5},{5,4},{6,7},{7,6},{8,9},{9,8},{10,11... | collective-permute-start | bytes 49160 | tf_op jit(solution)/shard_map/ppermute | solution.py:284
  21.9 7.7 %collective-permute-start.5 = (f32[3,8,128]{2,1,0:T(8,128)S(1)}, f32[3,8,128]{2,1,0:T(8,128)S(1)}, u32[]{:S(2)}, u32[]{:S(2)}) collective-permute-start(f32[3,8,128]{2,1,0:T(8,128)S(1)} %get-tuple-element.42), channel_id=1, source_target_pairs={{64,128},{192,256},{320,384},{448,512},{576,640},{704,768},{832,89... | collective-permute-start | bytes 36872 | tf_op jit(solution)/shard_map/ppermute | solution.py:282
  23.8 5.7 %collective-permute-start.4 = (f32[3,8,128]{2,1,0:T(8,128)S(1)}, f32[3,8,128]{2,1,0:T(8,128)S(1)}, u32[]{:S(2)}, u32[]{:S(2)}) collective-permute-start(f32[3,8,128]{2,1,0:T(8,128)S(1)} %get-tuple-element.43), channel_id=1, source_target_pairs={{0,64},{64,0},{128,192},{192,128},{256,320},{320,256},{384,448},{4... | collective-permute-start | bytes 36872 | tf_op jit(solution)/shard_map/ppermute | solution.py:284
  29.6 8.9 %collective-permute-start.6 = (f32[3,8,128]{2,1,0:T(8,128)S(1)}, f32[3,8,128]{2,1,0:T(8,128)S(1)}, u32[]{:S(2)}, u32[]{:S(2)}) collective-permute-start(f32[3,8,128]{2,1,0:T(8,128)S(1)} %get-tuple-element.53.after), channel_id=1, source_target_pairs={{1,2},{3,4},{5,6},{7,8},{9,10},{11,12},{13,14},{15,16},{17,18},{19... | collective-permute-start | bytes 36872 | tf_op jit(solution)/shard_map/ppermute | solution.py:282
  32.9 5.6 %collective-permute-start.7 = (f32[3,8,128]{2,1,0:T(8,128)S(1)}, f32[3,8,128]{2,1,0:T(8,128)S(1)}, u32[]{:S(2)}, u32[]{:S(2)}) collective-permute-start(f32[3,8,128]{2,1,0:T(8,128)S(1)} %get-tuple-element.46), channel_id=1, source_target_pairs={{0,1},{1,0},{2,3},{3,2},{4,5},{5,4},{6,7},{7,6},{8,9},{9,8},{10,11... | collective-permute-start | bytes 36872 | tf_op jit(solution)/shard_map/ppermute | solution.py:284

commit v5 on v4

--- a/solution.py
+++ b/solution.py
@@ -135,7 +135,7 @@
                 low[at_rows, columns] = jnp.where(keep, rest, 0.0).astype(BF16)
 
 
-def hot_kernel(index, count, fresh, after, hot, new_state, index_scr, sem):
+def hot_kernel(index, count, fresh, hot, new_state, index_scr, sem):
     store = pltpu.make_async_copy(fresh, new_state, sem)
     store.start()
     slots = index.shape[2]
@@ -236,11 +236,11 @@
     for i in range(9):
         at = slice(i * slots, (i + 1) * slots)
         out.append(jnp.concatenate([back[0:8, at], pad, back[8:16, at], pad], axis=1))
-    for q in range(3):
-        up, down = out[6 + q], out[q]
-        send1[q] = jnp.where(plus_r, up, down)
-        send2[q] = jnp.where(plus_r, down, up)
-        back_own[q] = out[3 + q]
+    for p in range(3):
+        up, down = out[3 * p + 2], out[3 * p]
+        send1[p] = jnp.where(plus_c, up, down)
+        send2[p] = jnp.where(plus_c, down, up)
+        back_own[p] = out[3 * p + 1]
 
 
 def surface_kernel(row1, row2, col1, col2, own, hot, result):
@@ -248,17 +248,13 @@
     plus_r = far_is_plus("row")
     plus_c = far_is_plus("col")
     middle = [
-        jnp.where(plus_r, row2[1], row1[1]),
+        jnp.where(plus_c, col2[1], col1[1]),
         own[1],
-        jnp.where(plus_r, row1[1], row2[1]),
+        jnp.where(plus_c, col1[1], col2[1]),
     ]
-    blocks = []
-    for a in range(3):
-        blocks += [
-            jnp.where(plus_c, col2[a], col1[a]),
-            middle[a],
-            jnp.where(plus_c, col1[a], col2[a]),
-        ]
+    blocks = [jnp.where(plus_r, row2[b], row1[b]) for b in range(3)]
+    blocks += middle
+    blocks += [jnp.where(plus_r, row1[b], row2[b]) for b in range(3)]
     values = jnp.concatenate(blocks, axis=1)
     weights = jnp.concatenate([pltpu.roll(block, OFF, 1) for block in blocks], axis=1)
     value_high = values.astype(BF16).astype(F32)
@@ -285,12 +281,12 @@
     return one, two
 
 
-def column_sends(row1, row2, own, extra, plus_r, plus_c):
-    minus = jnp.where(plus_r, row2, row1)
-    plus = jnp.where(plus_r, row1, row2)
-    low = jnp.stack([minus[0], own[0], plus[0]] + [edge for edge in extra[:1]])
-    high = jnp.stack([minus[2], own[2], plus[2]] + [edge for edge in extra[1:]])
-    return jnp.where(plus_c, high, low), jnp.where(plus_c, low, high)
+def forward_sends(one, two, own, extra, plus_before, plus_next):
+    minus = jnp.where(plus_before, two, one)
+    plus = jnp.where(plus_before, one, two)
+    low = jnp.stack([minus[0], own[0], plus[0]] + extra[:1])
+    high = jnp.stack([minus[2], own[2], plus[2]] + extra[1:])
+    return jnp.where(plus_next, high, low), jnp.where(plus_next, low, high)
 
 
 def in_hbm(array):
@@ -367,7 +363,7 @@
         )
 
     row1, row2 = exchange(send1, send2, "row")
-    send1, send2 = column_sends(row1, row2, own, [own[3], own[4]], plus_r, plus_c)
+    send1, send2 = forward_sends(row1, row2, own, [own[3], own[4]], plus_r, plus_c)
     col1, col2 = exchange(send1, send2, "col")
     high, low = spread(send1)
     fresh, send1, send2, own = call(
@@ -379,19 +375,20 @@
         row1, row2, col1, col2, own, high, low, state, velocity, diffusivity, wet,
         name="ocean",
     )
-    row1, row2 = exchange(send1, send2, "row")
-    send1, send2 = column_sends(row1, row2, own, [], plus_r, plus_c)
     col1, col2 = exchange(send1, send2, "col")
     hot, new_state = call(
         hot_kernel,
         [shape(9 * width, atm_cells, dtype=BF16), shape(fields * rows, width)],
         [pltpu.VMEM((16, width), jnp.int32), pltpu.SemaphoreType.DMA],
-        [VMEM] * 4,
+        [VMEM] * 3,
         1_000_000, 200_000,
-        index, count, fresh, send1,
+        index, count, fresh,
         out_specs=[VMEM, HBM],
         name="hot",
     )
+    col1, col2, hot = lax.optimization_barrier((col1, col2, hot))
+    send1, send2 = forward_sends(col1, col2, own, [], plus_c, plus_r)
+    row1, row2 = exchange(send1, send2, "row")
     (result,) = call(
         surface_kernel,
         [shape(fields, atm_cells)],

time: 39.7 us -> 40.3 us (1.015)
  the two profiles are of different devices: /device:TPU:430 before, /device:TPU:431 now
where the time goes in v5:
time: 40.3 us; the launch traced here: 39.9 us
  starting transfers between devices  28 us (69%)
  Pallas kernels  6.2 us (15%)
  waiting for transfers between devices  4.84 us (12%)
  between operations  0.83 us (2%)
    ppermute x4, starting transfers between devices, exchange(): one = lax.ppermute(send1, axis, far)  20.3 us
    ppermute x4, starting transfers between devices, exchange(): two = lax.ppermute(send2, axis, near)  7.68 us
    pallas_call x5, Pallas kernels, call(): pl.pallas_call(kernel, out_shape=outs, in_specs=specs, out_specs=out_spec...  6.2 us
    ppermute x4, waiting for transfers between devices, exchange(): two = lax.ppermute(send2, axis, near)  4.83 us
  transfers between devices with their start and end apart: 8, of which 4 were waited for; matrix products, arithmetic and copies ran while one was open for 0% of the time, Pallas kernels for 6%

profile of v5, /device:TPU:431, one launch (start us, length us, event | category | flops | bytes accessed | tf_op | source)
XLA Modules:
  0.0 39.9 jit_solution(9983249902231245761)
XLA Ops:
  0.6 1.2 %pack.1 = (f32[4,8,128]{2,1,0:T(8,128)S(1)}, f32[4,8,128]{2,1,0:T(8,128)S(1)}, f32[5,8,128]{2,1,0:T(8,128)S(1)}, s32[9,1,48]{2,1,0:T(1,128)S(1)}, s32[3,1,3]{2,1...) custom-call(f32[20,96]{1,0:T(8,128)} %flux.1, ...), custom_call_target="tpu_custom_call" | custom-call | flops 100000 | bytes 1000000 | tf_op jit(solution)/shard_map/pack/pallas_call | solution.py:297
  1.8 3.9 %collective-permute-start = (f32[4,8,128]{2,1,0:T(8,128)S(1)}, f32[4,8,128]{2,1,0:T(8,128)S(1)}, u32[]{:S(2)}, u32[]{:S(2)}) collective-permute-start(f32[4,8,128]{2,1,0:T(8,128)S(1)} %get-tuple-element.30), channel_id=1, source_target_pairs={{64,128},{192,256},{320,384},{448,512},{576,640},{704,768},{832,89... | collective-permute-start | bytes 49160 | tf_op jit(solution)/shard_map/ppermute | solution.py:278
  5.7 1.9 %collective-permute-start.1 = (f32[4,8,128]{2,1,0:T(8,128)S(1)}, f32[4,8,128]{2,1,0:T(8,128)S(1)}, u32[]{:S(2)}, u32[]{:S(2)}) collective-permute-start(f32[4,8,128]{2,1,0:T(8,128)S(1)} %get-tuple-element.32), channel_id=1, source_target_pairs={{0,64},{64,0},{128,192},{192,128},{256,320},{320,256},{384,448},{4... | collective-permute-start | bytes 49160 | tf_op jit(solution)/shard_map/ppermute | solution.py:280
  7.7 1.1 %collective-permute-done.1.row2 = f32[4,8,128]{2,1,0:T(8,128)S(1)} collective-permute-done((f32[4,8,128]{2,1,0:T(8,128)S(1)}, f32[4,8,128]{2,1,0:T(8,128)S(1)}, u32[]{:S(2)}, u32[]{:S(2)}) %collective-permute-start.1) | collective-permute-done | bytes 16416 | tf_op jit(solution)/shard_map/ppermute | solution.py:280
  8.8 0.0 collective-permute-done.row1
  8.9 5.9 %collective-permute-start.2 = (f32[4,8,128]{2,1,0:T(8,128)S(1)}, f32[4,8,128]{2,1,0:T(8,128)S(1)}, u32[]{:S(2)}, u32[]{:S(2)}) collective-permute-start(f32[4,8,128]{2,1,0:T(8,128)S(1)} %get-tuple-element.55.after), channel_id=1, source_target_pairs={{1,2},{3,4},{5,6},{7,8},{9,10},{11,12},{13,14},{15,16},{17,18},{19... | collective-permute-start | bytes 49160 | tf_op jit(solution)/shard_map/ppermute | solution.py:278
  14.8 1.9 %collective-permute-start.3 = (f32[4,8,128]{2,1,0:T(8,128)S(1)}, f32[4,8,128]{2,1,0:T(8,128)S(1)}, u32[]{:S(2)}, u32[]{:S(2)}) collective-permute-start(f32[4,8,128]{2,1,0:T(8,128)S(1)} %get-tuple-element.34), channel_id=1, source_target_pairs={{0,1},{1,0},{2,3},{3,2},{4,5},{5,4},{6,7},{7,6},{8,9},{9,8},{10,11... | collective-permute-start | bytes 49160 | tf_op jit(solution)/shard_map/ppermute | solution.py:280
  16.7 1.8 %spread.1 = (bf16[432,2048]{1,0:T(8,128)(2,1)S(1)}, bf16[432,2048]{1,0:T(8,128)(2,1)S(1)}) custom-call(s32[9,1,48]{2,1,0:T(1,128)S(1)} %get-tuple-element.35.start, f32[1,3,3,48,128]{4,3,2,1,0:T(8,128)S(1)} %get-tuple-element.36.weight, f32[4,8,128]{2,1,0:T(8,128)S(1)} %get-tuple-element.55.after), custom_call_target="tpu_custom_call" | custom-call | flops 20000000 | bytes 4000000 | tf_op jit(solution)/shard_map/spread/pallas_call | solution.py:297
  18.5 0.0 collective-permute-done.2.col1
  18.5 0.7 %collective-permute-done.3.col2 = f32[4,8,128]{2,1,0:T(8,128)S(1)} collective-permute-done((f32[4,8,128]{2,1,0:T(8,128)S(1)}, f32[4,8,128]{2,1,0:T(8,128)S(1)}, u32[]{:S(2)}, u32[]{:S(2)}) %collective-permute-start.3) | collective-permute-done | bytes 16416 | tf_op jit(solution)/shard_map/ppermute | solution.py:280
  19.3 1.7 %ocean.1 = (f32[128,128]{1,0:T(8,128)S(1)}, f32[3,8,128]{2,1,0:T(8,128)S(1)}, f32[3,8,128]{2,1,0:T(8,128)S(1)}, f32[3,8,128]{2,1,0:T(8,128)S(1)}) custom-call(f32[4,8,128]{2,1,0:T(8,128)S(1)} %collective-permute-done.row1, f32[4,8,128]{2,1,0:T(8,128)S(1)} %collective-permute-done.1.row2, f32[4,8,128]{2,1,0:T(8,128)S(1)} %collective-permute-done.2.col1, ...), custom_call_target="tpu_custom_call" | custom-call | flops 100000000 | bytes 4000000 | tf_op jit(solution)/shard_map/ocean/pallas_call | solution.py:297
  21.0 3.6 %collective-permute-start.4 = (f32[3,8,128]{2,1,0:T(8,128)S(1)}, f32[3,8,128]{2,1,0:T(8,128)S(1)}, u32[]{:S(2)}, u32[]{:S(2)}) collective-permute-start(f32[3,8,128]{2,1,0:T(8,128)S(1)} %get-tuple-element.45), channel_id=1, source_target_pairs={{1,2},{3,4},{5,6},{7,8},{9,10},{11,12},{13,14},{15,16},{17,18},{19... | collective-permute-start | bytes 36872 | tf_op jit(solution)/shard_map/ppermute | solution.py:278
  24.6 1.9 %collective-permute-start.5 = (f32[3,8,128]{2,1,0:T(8,128)S(1)}, f32[3,8,128]{2,1,0:T(8,128)S(1)}, u32[]{:S(2)}, u32[]{:S(2)}) collective-permute-start(f32[3,8,128]{2,1,0:T(8,128)S(1)} %get-tuple-element.47), channel_id=1, source_target_pairs={{0,1},{1,0},{2,3},{3,2},{4,5},{5,4},{6,7},{7,6},{8,9},{9,8},{10,11... | collective-permute-start | bytes 36872 | tf_op jit(solution)/shard_map/ppermute | solution.py:280
  26.5 0.6 %hot.1 = (bf16[1152,96]{1,0:T(8,128)(2,1)S(1)}, f32[128,128]{1,0:T(8,128)}) custom-call(s32[9,1,48]{2,1,0:T(1,128)S(1)} %get-tuple-element.28.index, s32[3,1,3]{2,1,0:T(1,128)S(1)} %get-tuple-element.29.count, f32[128,128]{1,0:T(8,128)S(1)} %get-tuple-element.43.fresh), custom_call_target="tpu_custom_call" | custom-call | flops 1000000 | bytes 200000 | tf_op jit(solution)/shard_map/hot/pallas_call | solution.py:297
  27.2 1.8 %collective-permute-done.5.col2 = f32[3,8,128]{2,1,0:T(8,128)S(1)} collective-permute-done((f32[3,8,128]{2,1,0:T(8,128)S(1)}, f32[3,8,128]{2,1,0:T(8,128)S(1)}, u32[]{:S(2)}, u32[]{:S(2)}) %collective-permute-start.5) | collective-permute-done | bytes 12320 | tf_op jit(solution)/shard_map/ppermute | solution.py:280
  29.0 0.0 collective-permute-done.4.col1
  29.1 6.9 %collective-permute-start.6 = (f32[3,8,128]{2,1,0:T(8,128)S(1)}, f32[3,8,128]{2,1,0:T(8,128)S(1)}, u32[]{:S(2)}, u32[]{:S(2)}) collective-permute-start(f32[3,8,128]{2,1,0:T(8,128)S(1)} %get-tuple-element.59), channel_id=1, source_target_pairs={{64,128},{192,256},{320,384},{448,512},{576,640},{704,768},{832,89... | collective-permute-start | bytes 36872 | tf_op jit(solution)/shard_map/ppermute | solution.py:278
  36.0 1.9 %collective-permute-start.7 = (f32[3,8,128]{2,1,0:T(8,128)S(1)}, f32[3,8,128]{2,1,0:T(8,128)S(1)}, u32[]{:S(2)}, u32[]{:S(2)}) collective-permute-start(f32[3,8,128]{2,1,0:T(8,128)S(1)} %get-tuple-element.52), channel_id=1, source_target_pairs={{0,64},{64,0},{128,192},{192,128},{256,320},{320,256},{384,448},{4... | collective-permute-start | bytes 36872 | tf_op jit(solution)/shard_map/ppermute | solution.py:280
  37.9 0.0 collective-permute-done.6.row1
  37.9 1.1 %collective-permute-done.7.row2 = f32[3,8,128]{2,1,0:T(8,128)S(1)} collective-permute-done((f32[3,8,128]{2,1,0:T(8,128)S(1)}, f32[3,8,128]{2,1,0:T(8,128)S(1)}, u32[]{:S(2)}, u32[]{:S(2)}) %collective-permute-start.7) | collective-permute-done | bytes 12320 | tf_op jit(solution)/shard_map/ppermute | solution.py:280
  39.0 0.9 %surface.1 = f32[8,96]{1,0:T(8,128)} custom-call(f32[3,8,128]{2,1,0:T(8,128)S(1)} %collective-permute-done.6.row1, f32[3,8,128]{2,1,0:T(8,128)S(1)} %collective-permute-done.7.row2, f32[3,8,128]{2,1,0:T(8,128)S(1)} %collective-permute-done.4.col1, f32[3,8,128]{2,1,0:T(8,128)S(1)} %collective-permute-done.5.col2, f32[3,8,128]{2,1,0:T(8,128)S(1)} %get-tuple-element.51.own, ...), custom_call_target="tpu_custom_call" | custom-call | flops 1000000 | bytes 200000 | tf_op jit(solution)/shard_map/surface/pallas_call | solution.py:297
  (9 shorter events, 0.0 us)
Async XLA Ops:
  1.8 7.0 %collective-permute-start = (f32[4,8,128]{2,1,0:T(8,128)S(1)}, f32[4,8,128]{2,1,0:T(8,128)S(1)}, u32[]{:S(2)}, u32[]{:S(2)}) collective-permute-start(f32[4,8,128]{2,1,0:T(8,128)S(1)} %get-tuple-element.30), channel_id=1, source_target_pairs={{64,128},{192,256},{320,384},{448,512},{576,640},{704,768},{832,89... | collective-permute-start | bytes 49160 | tf_op jit(solution)/shard_map/ppermute | solution.py:278
  5.7 3.1 %collective-permute-start.1 = (f32[4,8,128]{2,1,0:T(8,128)S(1)}, f32[4,8,128]{2,1,0:T(8,128)S(1)}, u32[]{:S(2)}, u32[]{:S(2)}) collective-permute-start(f32[4,8,128]{2,1,0:T(8,128)S(1)} %get-tuple-element.32), channel_id=1, source_target_pairs={{0,64},{64,0},{128,192},{192,128},{256,320},{320,256},{384,448},{4... | collective-permute-start | bytes 49160 | tf_op jit(solution)/shard_map/ppermute | solution.py:280
  8.9 9.7 %collective-permute-start.2 = (f32[4,8,128]{2,1,0:T(8,128)S(1)}, f32[4,8,128]{2,1,0:T(8,128)S(1)}, u32[]{:S(2)}, u32[]{:S(2)}) collective-permute-start(f32[4,8,128]{2,1,0:T(8,128)S(1)} %get-tuple-element.55.after), channel_id=1, source_target_pairs={{1,2},{3,4},{5,6},{7,8},{9,10},{11,12},{13,14},{15,16},{17,18},{19... | collective-permute-start | bytes 49160 | tf_op jit(solution)/shard_map/ppermute | solution.py:278
  14.8 4.5 %collective-permute-start.3 = (f32[4,8,128]{2,1,0:T(8,128)S(1)}, f32[4,8,128]{2,1,0:T(8,128)S(1)}, u32[]{:S(2)}, u32[]{:S(2)}) collective-permute-start(f32[4,8,128]{2,1,0:T(8,128)S(1)} %get-tuple-element.34), channel_id=1, source_target_pairs={{0,1},{1,0},{2,3},{3,2},{4,5},{5,4},{6,7},{7,6},{8,9},{9,8},{10,11... | collective-permute-start | bytes 49160 | tf_op jit(solution)/shard_map/ppermute | solution.py:280
  21.0 8.0 %collective-permute-start.4 = (f32[3,8,128]{2,1,0:T(8,128)S(1)}, f32[3,8,128]{2,1,0:T(8,128)S(1)}, u32[]{:S(2)}, u32[]{:S(2)}) collective-permute-start(f32[3,8,128]{2,1,0:T(8,128)S(1)} %get-tuple-element.45), channel_id=1, source_target_pairs={{1,2},{3,4},{5,6},{7,8},{9,10},{11,12},{13,14},{15,16},{17,18},{19... | collective-permute-start | bytes 36872 | tf_op jit(solution)/shard_map/ppermute | solution.py:278
  24.6 4.4 %collective-permute-start.5 = (f32[3,8,128]{2,1,0:T(8,128)S(1)}, f32[3,8,128]{2,1,0:T(8,128)S(1)}, u32[]{:S(2)}, u32[]{:S(2)}) collective-permute-start(f32[3,8,128]{2,1,0:T(8,128)S(1)} %get-tuple-element.47), channel_id=1, source_target_pairs={{0,1},{1,0},{2,3},{3,2},{4,5},{5,4},{6,7},{7,6},{8,9},{9,8},{10,11... | collective-permute-start | bytes 36872 | tf_op jit(solution)/shard_map/ppermute | solution.py:280
  29.1 8.8 %collective-permute-start.6 = (f32[3,8,128]{2,1,0:T(8,128)S(1)}, f32[3,8,128]{2,1,0:T(8,128)S(1)}, u32[]{:S(2)}, u32[]{:S(2)}) collective-permute-start(f32[3,8,128]{2,1,0:T(8,128)S(1)} %get-tuple-element.59), channel_id=1, source_target_pairs={{64,128},{192,256},{320,384},{448,512},{576,640},{704,768},{832,89... | collective-permute-start | bytes 36872 | tf_op jit(solution)/shard_map/ppermute | solution.py:278
  36.0 3.1 %collective-permute-start.7 = (f32[3,8,128]{2,1,0:T(8,128)S(1)}, f32[3,8,128]{2,1,0:T(8,128)S(1)}, u32[]{:S(2)}, u32[]{:S(2)}) collective-permute-start(f32[3,8,128]{2,1,0:T(8,128)S(1)} %get-tuple-element.52), channel_id=1, source_target_pairs={{0,64},{64,0},{128,192},{192,128},{256,320},{320,256},{384,448},{4... | collective-permute-start | bytes 36872 | tf_op jit(solution)/shard_map/ppermute | solution.py:280

commit v6 on v4

--- a/solution.py
+++ b/solution.py
@@ -1,5 +1,3 @@
-import functools
-
 import jax
 import jax.numpy as jnp
 from jax import lax
@@ -19,12 +17,6 @@
 
 def lanes_of(shape):
     return lax.broadcasted_iota(jnp.int32, shape, 1)
-
-
-def halves(value):
-    high = value.astype(BF16)
-    low = (value - high.astype(F32)).astype(BF16)
-    return high, low
 
 
 def far_is_plus(axis):
@@ -98,11 +90,10 @@
     return jnp.take_along_axis(table, lanes, axis=1, mode="promise_in_bounds", wrap_negative_indices=False)
 
 
-def spread_kernel(begin, end, start, weight, after, high, low, start_scr):
+def spread_kernel(start, weight, after, matrix, late, start_scr):
     slots, width = weight.shape[3], weight.shape[4]
-    rows = high.shape[1] // width
     start_scr[...] = jnp.zeros_like(start_scr)
-    for i in range(begin, end):
+    for i in range(9):
         start_scr[i : i + 1, 0:slots] = start[i].astype(F32)
     turned = start_scr[...].T
     lane = lanes_of((slots, width))
@@ -110,29 +101,29 @@
     target = lax.broadcasted_iota(jnp.int32, (width, WIN_R * width), 1)
     wanted = (target // width) * WIN_C + (target & (WIN_C - 1))
     copies = (source == wanted).astype(F32).astype(BF16)
-    for i in range(begin, end):
+    tops = jnp.concatenate([start[i] // width for i in range(9)], axis=1)
+    tops = jnp.broadcast_to(tops, late.shape)
+    late[...] = (tops > lax.broadcasted_iota(jnp.int32, late.shape, 0)).astype(F32)
+    for i in range(9):
         first = turned[0:slots, i : i + 1].astype(jnp.int32)
         top = first // width
         left = jnp.broadcast_to(first - top * width, (slots, width))
         above = jnp.broadcast_to(top * WIN_C, (slots, width))
         across = lane - left
         inside = (across >= 0) & (across < WIN_C)
-        turn = (lane - left) & (WIN_C - 1)
+        turn = across & (WIN_C - 1)
         group = (lane - above) & (WIN_R * WIN_C - WIN_C)
         block = pick(weight[0, i // 3, i % 3], group + turn)
-        top = jnp.broadcast_to(top, (slots, width))
         part = block.astype(BF16).astype(F32)
         both = jnp.concatenate([part, block - part], axis=0).astype(BF16)
         both = jnp.dot(both, copies, preferred_element_type=F32)
-        at_rows = slice((i - begin) * slots, (i - begin + 1) * slots)
+        at_rows = slice(i * slots, (i + 1) * slots)
         for y in range(WIN_R):
-            part = jnp.where(inside, both[:slots, y * width : (y + 1) * width], 0.0)
-            rest = jnp.where(inside, both[slots:, y * width : (y + 1) * width], 0.0)
-            late = top > y
-            for to, keep in ((y, ~late), (y + WIN_R, late)):
-                columns = slice(to * width, (to + 1) * width)
-                high[at_rows, columns] = jnp.where(keep, part, 0.0).astype(BF16)
-                low[at_rows, columns] = jnp.where(keep, rest, 0.0).astype(BF16)
+            columns = slice(y * width, (y + 1) * width)
+            part = jnp.where(inside, both[:slots, columns], 0.0)
+            rest = jnp.where(inside, both[slots:, columns], 0.0)
+            pair = jnp.concatenate([part, rest], axis=1).astype(BF16)
+            matrix[at_rows, 2 * y * width : 2 * (y + 1) * width] = pair
 
 
 def hot_kernel(index, count, fresh, after, hot, new_state, index_scr, sem):
@@ -155,10 +146,10 @@
 
 
 def ocean_kernel(
-    row1, row2, col1, col2, own, high, low, state, velocity, diffusivity, wet,
-    new_state, send1, send2, back_own, surface,
+    row1, row2, col1, col2, own, matrix, late, state, velocity, diffusivity, wet,
+    new_state, send1, send2, back_own,
 ):
-    slots = high.shape[0] // 9
+    slots = matrix.shape[0] // 9
     width = state.shape[1]
     rows = state.shape[0] // 8
     plus_r = far_is_plus("row")
@@ -179,60 +170,63 @@
     west_edge = from_minus(col1, col2, plus_c, 3)
     east_edge = from_plus(col1, col2, plus_c, 3)
 
-    def left_of(group):
-        fields = jnp.concatenate([block[:, 0:slots] for block in group], axis=1)
-        flags = jnp.concatenate([block[:, OFF : OFF + slots] for block in group], axis=1)
-        first_row = lax.broadcasted_iota(jnp.int32, flags.shape, 0) == 0
-        flags = jnp.where(first_row, flags, 0.0)
-        field_high = fields.astype(BF16).astype(F32)
-        field_low = fields - field_high
-        parts = [field_high, flags, field_low, jnp.zeros_like(flags)]
-        return jnp.concatenate(parts, axis=0).astype(BF16)
-
-    left = left_of(blocks)
+    fields = jnp.concatenate([block[:, 0:slots] for block in blocks], axis=1)
+    flags = jnp.concatenate([block[:, OFF : OFF + slots] for block in blocks], axis=1)
+    first_row = lax.broadcasted_iota(jnp.int32, flags.shape, 0) == 0
+    flags = jnp.where(first_row, flags, 0.0)
+    field_high = fields.astype(BF16).astype(F32)
+    left = jnp.concatenate([field_high, flags, fields - field_high, jnp.zeros_like(flags)], axis=0)
 
     lane = lanes_of((8, width))
     row_of = lax.broadcasted_iota(jnp.int32, (8, width), 0)
     one_row = jnp.where(row_of == 0, 1.0, 0.0)
-    spread = jnp.zeros((8, width), F32)
+    none = jnp.zeros((8, width), F32)
+    spread = none
     for k in range(8):
         spread = jnp.where(row_of == k, jnp.broadcast_to(diffusivity[:, k : k + 1], (8, width)), spread)
-    step = 2 * width
     lines = [state[pl.ds(y, 8, stride=rows), :] for y in range(rows)]
-    for part in range(rows // 2):
-        cells = slice(part * step, (part + 1) * step)
-        sums = jnp.dot(left, high[:, cells], preferred_element_type=F32)
-        rest = jnp.dot(left[0:16], low[:, cells], preferred_element_type=F32)
-        sums = sums[0:16] + sums[16:32] + rest
-        for y in (2 * part, 2 * part + 1):
-            at = slice((y % 2) * width, (y % 2 + 1) * width)
-            cover = sums[8:9, at]
-            forcing = sums[0:8, at] / jnp.maximum(jnp.broadcast_to(cover, (8, width)), 1.0)
-            here = lines[y]
-            north = lines[y + 1] if y + 1 < rows else north_edge
-            south = lines[y - 1] if y > 0 else south_edge
-            east = pltpu.roll(here, width - 1, 1)
-            east = jnp.where(lane == width - 1, jnp.broadcast_to(east_edge[:, y : y + 1], (8, width)), east)
-            west = pltpu.roll(here, 1, 1)
-            west = jnp.where(lane == 0, jnp.broadcast_to(west_edge[:, y : y + 1], (8, width)), west)
-            laplace = east + west + north + south - 4.0 * here
-            along = jnp.broadcast_to(velocity[0, y : y + 1, :], (8, width))
-            across = jnp.broadcast_to(velocity[1, y : y + 1, :], (8, width))
-            advect = 0.5 * (along * (east - west) + across * (north - south))
-            mask = jnp.broadcast_to(wet[y : y + 1, :], (8, width)).astype(F32)
-            fresh = here + mask * (spread * laplace - advect + forcing)
-            new_state[pl.ds(y, 8, stride=rows), :] = fresh
-            seen = fresh * mask
-            seen_high = seen.astype(BF16).astype(F32)
-            column = slice(y * width, (y + 1) * width)
-            surface[0:16, column] = jnp.concatenate([seen_high, one_row], axis=0).astype(BF16)
-            surface[16:32, column] = jnp.concatenate([seen - seen_high, jnp.zeros_like(seen)], axis=0).astype(BF16)
+
+    def advance(y, sums):
+        forcing = sums[0:8] / jnp.maximum(jnp.broadcast_to(sums[8:9], (8, width)), 1.0)
+        here = lines[y]
+        north = lines[y + 1] if y + 1 < rows else north_edge
+        south = lines[y - 1] if y > 0 else south_edge
+        east = pltpu.roll(here, width - 1, 1)
+        east = jnp.where(lane == width - 1, jnp.broadcast_to(east_edge[:, y : y + 1], (8, width)), east)
+        west = pltpu.roll(here, 1, 1)
+        west = jnp.where(lane == 0, jnp.broadcast_to(west_edge[:, y : y + 1], (8, width)), west)
+        laplace = east + west + north + south - 4.0 * here
+        along = jnp.broadcast_to(velocity[0, y : y + 1, :], (8, width))
+        across = jnp.broadcast_to(velocity[1, y : y + 1, :], (8, width))
+        advect = 0.5 * (along * (east - west) + across * (north - south))
+        mask = jnp.broadcast_to(wet[y : y + 1, :], (8, width)).astype(F32)
+        fresh = here + mask * (spread * laplace - advect + forcing)
+        new_state[pl.ds(y, 8, stride=rows), :] = fresh
+        seen = fresh * mask
+        seen_high = seen.astype(BF16).astype(F32)
+        return [seen_high, one_row, seen - seen_high, none]
+
+    seen = []
+    for y in range(WIN_R):
+        moved = jnp.broadcast_to(late[y : y + 1, :], left.shape) > 0
+        both = jnp.concatenate([jnp.where(moved, 0.0, left), jnp.where(moved, left, 0.0)], axis=0)
+        sums = jnp.dot(
+            both.astype(BF16), matrix[:, 2 * y * width : 2 * (y + 1) * width], preferred_element_type=F32
+        )
+        sums = sums[:, 0:width] + sums[:, width:]
+        lines_seen = advance(y, sums[0:16] + sums[16:32])
+        lines_seen += advance(y + WIN_R, sums[32:48] + sums[48:64])
+        seen.append(jnp.concatenate(lines_seen, axis=0).astype(BF16))
+    back = jnp.zeros((16, matrix.shape[0]), F32)
+    for y in range(WIN_R):
+        moved = jnp.broadcast_to(late[y : y + 1, :], back.shape) > 0
+        part = lax.dot_general(
+            jnp.concatenate([seen[y], seen[y]], axis=1), matrix[:, 2 * y * width : 2 * (y + 1) * width],
+            NT, preferred_element_type=F32,
+        )
+        back = back + jnp.where(moved, part[32:48] + part[48:64], part[0:16] + part[16:32])
     pad = jnp.zeros((8, OFF - slots), F32)
     out = []
-    back = lax.dot_general(surface[...], high[...], NT, preferred_element_type=F32)
-    back = back[0:16] + back[16:32] + lax.dot_general(
-        surface[0:16, :], low[...], NT, preferred_element_type=F32
-    )
     for i in range(9):
         at = slice(i * slots, (i + 1) * slots)
         out.append(jnp.concatenate([back[0:8, at], pad, back[8:16, at], pad], axis=1))
@@ -357,8 +351,8 @@
 
     def spread(after):
         return call(
-            functools.partial(spread_kernel, 0, 9),
-            [shape(9 * slots, cells, dtype=BF16)] * 2,
+            spread_kernel,
+            [shape(9 * slots, cells, dtype=BF16), shape(WIN_R, 9 * slots)],
             [pltpu.VMEM((16, width), F32)],
             [VMEM, VMEM, VMEM],
             20_000_000, 4_000_000,
@@ -369,14 +363,14 @@
     row1, row2 = exchange(send1, send2, "row")
     send1, send2 = column_sends(row1, row2, own, [own[3], own[4]], plus_r, plus_c)
     col1, col2 = exchange(send1, send2, "col")
-    high, low = spread(send1)
+    matrix, late = spread(send1)
     fresh, send1, send2, own = call(
         ocean_kernel,
         [shape(fields * rows, width), shape(3, 8, width), shape(3, 8, width), shape(3, 8, width)],
-        [pltpu.VMEM((32, cells), BF16)],
+        [],
         [VMEM] * 11,
         100_000_000, 4_000_000,
-        row1, row2, col1, col2, own, high, low, state, velocity, diffusivity, wet,
+        row1, row2, col1, col2, own, matrix, late, state, velocity, diffusivity, wet,
         name="ocean",
     )
     row1, row2 = exchange(send1, send2, "row")

time: 39.7 us -> 39.2 us (0.987)
  Pallas kernels: 6.2 us -> 5.09 us
  waiting for transfers between devices: 6.48 us -> 7.01 us
    pallas_call x5, Pallas kernels: 6.2 us -> 5.09 us  [call(): pl.pallas_call(kernel, out_shape=outs, in_specs=specs, out_specs=out_spec...]
    ppermute x4, waiting for transfers between devices: 3.47 us -> 4.01 us  [exchange(): two = lax.ppermute(send2, axis, near)]
  transfers between devices with their start and end apart: 8 -> 8, of which waited for: 4 -> 4; matrix products, arithmetic and copies ran while one was open for 0% -> 0% of each run, Pallas kernels for 6% -> 5%
where the time goes in v6:
time: 39.2 us; the launch traced here: 38.8 us
  starting transfers between devices  25.8 us (66%)
  waiting for transfers between devices  7.01 us (18%)
  Pallas kernels  5.09 us (13%)
  between operations  0.81 us (2%)
    ppermute x4, starting transfers between devices, exchange(): one = lax.ppermute(send1, axis, far)  13.4 us
    ppermute x4, starting transfers between devices, exchange(): two = lax.ppermute(send2, axis, near)  12.5 us
    pallas_call x5, Pallas kernels, call(): pl.pallas_call(kernel, out_shape=outs, in_specs=specs, out_specs=out_spec...  5.09 us
    ppermute x4, waiting for transfers between devices, exchange(): two = lax.ppermute(send2, axis, near)  4.01 us
    ppermute x4, waiting for transfers between devices, exchange(): one = lax.ppermute(send1, axis, far)  3.01 us
  transfers between devices with their start and end apart: 8, of which 4 were waited for; matrix products, arithmetic and copies ran while one was open for 0% of the time, Pallas kernels for 5%

profile of v6, /device:TPU:430, one launch (start us, length us, event | category | flops | bytes accessed | tf_op | source)
XLA Modules:
  0.0 38.8 jit_solution(12315280668219942425)
XLA Ops:
  0.6 1.2 %pack.1 = (f32[4,8,128]{2,1,0:T(8,128)S(1)}, f32[4,8,128]{2,1,0:T(8,128)S(1)}, f32[5,8,128]{2,1,0:T(8,128)S(1)}, s32[9,1,48]{2,1,0:T(1,128)S(1)}, s32[3,1,3]{2,1...) custom-call(f32[20,96]{1,0:T(8,128)} %flux.1, ...), custom_call_target="tpu_custom_call" | custom-call | flops 100000 | bytes 1000000 | tf_op jit(solution)/shard_map/pack/pallas_call | solution.py:295
  1.8 1.9 %collective-permute-start = (f32[4,8,128]{2,1,0:T(8,128)S(1)}, f32[4,8,128]{2,1,0:T(8,128)S(1)}, u32[]{:S(2)}, u32[]{:S(2)}) collective-permute-start(f32[4,8,128]{2,1,0:T(8,128)S(1)} %get-tuple-element.27), channel_id=1, source_target_pairs={{64,128},{192,256},{320,384},{448,512},{576,640},{704,768},{832,89... | collective-permute-start | bytes 49160 | tf_op jit(solution)/shard_map/ppermute | solution.py:276
  3.8 3.7 %collective-permute-start.1 = (f32[4,8,128]{2,1,0:T(8,128)S(1)}, f32[4,8,128]{2,1,0:T(8,128)S(1)}, u32[]{:S(2)}, u32[]{:S(2)}) collective-permute-start(f32[4,8,128]{2,1,0:T(8,128)S(1)} %get-tuple-element.29), channel_id=1, source_target_pairs={{0,64},{64,0},{128,192},{192,128},{256,320},{320,256},{384,448},{4... | collective-permute-start | bytes 49160 | tf_op jit(solution)/shard_map/ppermute | solution.py:278
  7.5 0.8 %collective-permute-done.1.row2 = f32[4,8,128]{2,1,0:T(8,128)S(1)} collective-permute-done((f32[4,8,128]{2,1,0:T(8,128)S(1)}, f32[4,8,128]{2,1,0:T(8,128)S(1)}, u32[]{:S(2)}, u32[]{:S(2)}) %collective-permute-start.1) | collective-permute-done | bytes 16416 | tf_op jit(solution)/shard_map/ppermute | solution.py:278
  8.3 0.0 collective-permute-done.row1
  8.3 6.2 %collective-permute-start.2 = (f32[4,8,128]{2,1,0:T(8,128)S(1)}, f32[4,8,128]{2,1,0:T(8,128)S(1)}, u32[]{:S(2)}, u32[]{:S(2)}) collective-permute-start(f32[4,8,128]{2,1,0:T(8,128)S(1)} %get-tuple-element.49.after), channel_id=1, source_target_pairs={{1,2},{3,4},{5,6},{7,8},{9,10},{11,12},{13,14},{15,16},{17,18},{19... | collective-permute-start | bytes 49160 | tf_op jit(solution)/shard_map/ppermute | solution.py:276
  14.6 1.9 %collective-permute-start.3 = (f32[4,8,128]{2,1,0:T(8,128)S(1)}, f32[4,8,128]{2,1,0:T(8,128)S(1)}, u32[]{:S(2)}, u32[]{:S(2)}) collective-permute-start(f32[4,8,128]{2,1,0:T(8,128)S(1)} %get-tuple-element.31), channel_id=1, source_target_pairs={{0,1},{1,0},{2,3},{3,2},{4,5},{5,4},{6,7},{7,6},{8,9},{9,8},{10,11... | collective-permute-start | bytes 49160 | tf_op jit(solution)/shard_map/ppermute | solution.py:278
  16.5 1.3 %spread.1 = (bf16[432,2048]{1,0:T(8,128)(2,1)S(1)}, f32[8,432]{1,0:T(8,128)S(1)}) custom-call(s32[9,1,48]{2,1,0:T(1,128)S(1)} %get-tuple-element.32.start, f32[1,3,3,48,128]{4,3,2,1,0:T(8,128)S(1)} %get-tuple-element.33.weight, f32[4,8,128]{2,1,0:T(8,128)S(1)} %get-tuple-element.49.after), custom_call_target="tpu_custom_call" | custom-call | flops 20000000 | bytes 4000000 | tf_op jit(solution)/shard_map/spread/pallas_call | solution.py:295
  17.8 0.0 collective-permute-done.2.col1
  17.8 2.4 %collective-permute-done.3.col2 = f32[4,8,128]{2,1,0:T(8,128)S(1)} collective-permute-done((f32[4,8,128]{2,1,0:T(8,128)S(1)}, f32[4,8,128]{2,1,0:T(8,128)S(1)}, u32[]{:S(2)}, u32[]{:S(2)}) %collective-permute-start.3) | collective-permute-done | bytes 16416 | tf_op jit(solution)/shard_map/ppermute | solution.py:278
  20.2 1.1 %ocean.1 = (f32[128,128]{1,0:T(8,128)S(1)}, f32[3,8,128]{2,1,0:T(8,128)S(1)}, f32[3,8,128]{2,1,0:T(8,128)S(1)}, f32[3,8,128]{2,1,0:T(8,128)S(1)}) custom-call(f32[4,8,128]{2,1,0:T(8,128)S(1)} %collective-permute-done.row1, f32[4,8,128]{2,1,0:T(8,128)S(1)} %collective-permute-done.1.row2, f32[4,8,128]{2,1,0:T(8,128)S(1)} %collective-permute-done.2.col1, ...), custom_call_target="tpu_custom_call" | custom-call | flops 100000000 | bytes 4000000 | tf_op jit(solution)/shard_map/ocean/pallas_call | solution.py:295
  21.3 1.9 %collective-permute-start.5 = (f32[3,8,128]{2,1,0:T(8,128)S(1)}, f32[3,8,128]{2,1,0:T(8,128)S(1)}, u32[]{:S(2)}, u32[]{:S(2)}) collective-permute-start(f32[3,8,128]{2,1,0:T(8,128)S(1)} %get-tuple-element.42), channel_id=1, source_target_pairs={{64,128},{192,256},{320,384},{448,512},{576,640},{704,768},{832,89... | collective-permute-start | bytes 36872 | tf_op jit(solution)/shard_map/ppermute | solution.py:276
  23.2 4.9 %collective-permute-start.4 = (f32[3,8,128]{2,1,0:T(8,128)S(1)}, f32[3,8,128]{2,1,0:T(8,128)S(1)}, u32[]{:S(2)}, u32[]{:S(2)}) collective-permute-start(f32[3,8,128]{2,1,0:T(8,128)S(1)} %get-tuple-element.43), channel_id=1, source_target_pairs={{0,64},{64,0},{128,192},{192,128},{256,320},{320,256},{384,448},{4... | collective-permute-start | bytes 36872 | tf_op jit(solution)/shard_map/ppermute | solution.py:278
  28.2 0.8 %collective-permute-done.4.row2 = f32[3,8,128]{2,1,0:T(8,128)S(1)} collective-permute-done((f32[3,8,128]{2,1,0:T(8,128)S(1)}, f32[3,8,128]{2,1,0:T(8,128)S(1)}, u32[]{:S(2)}, u32[]{:S(2)}) %collective-permute-start.4) | collective-permute-done | bytes 12320 | tf_op jit(solution)/shard_map/ppermute | solution.py:278
  29.0 0.0 collective-permute-done.5.row1
  29.0 3.3 %collective-permute-start.6 = (f32[3,8,128]{2,1,0:T(8,128)S(1)}, f32[3,8,128]{2,1,0:T(8,128)S(1)}, u32[]{:S(2)}, u32[]{:S(2)}) collective-permute-start(f32[3,8,128]{2,1,0:T(8,128)S(1)} %get-tuple-element.53.after), channel_id=1, source_target_pairs={{1,2},{3,4},{5,6},{7,8},{9,10},{11,12},{13,14},{15,16},{17,18},{19... | collective-permute-start | bytes 36872 | tf_op jit(solution)/shard_map/ppermute | solution.py:276
  32.3 1.9 %collective-permute-start.7 = (f32[3,8,128]{2,1,0:T(8,128)S(1)}, f32[3,8,128]{2,1,0:T(8,128)S(1)}, u32[]{:S(2)}, u32[]{:S(2)}) collective-permute-start(f32[3,8,128]{2,1,0:T(8,128)S(1)} %get-tuple-element.46), channel_id=1, source_target_pairs={{0,1},{1,0},{2,3},{3,2},{4,5},{5,4},{6,7},{7,6},{8,9},{9,8},{10,11... | collective-permute-start | bytes 36872 | tf_op jit(solution)/shard_map/ppermute | solution.py:278
  34.3 0.6 %hot.1 = (bf16[1152,96]{1,0:T(8,128)(2,1)S(1)}, f32[128,128]{1,0:T(8,128)}) custom-call(s32[9,1,48]{2,1,0:T(1,128)S(1)} %get-tuple-element.25.index, s32[3,1,3]{2,1,0:T(1,128)S(1)} %get-tuple-element.26.count, f32[128,128]{1,0:T(8,128)S(1)} %get-tuple-element.40.fresh, f32[3,8,128]{2,1,0:T(8,128)S(1)} %get-tuple-element.53.after), custom_call_target="tpu_custom_call" | custom-call | flops 1000000 | bytes 200000 | tf_op jit(solution)/shard_map/hot/pallas_call | solution.py:295
  34.9 3.0 %collective-permute-done.6.col1 = f32[3,8,128]{2,1,0:T(8,128)S(1)} collective-permute-done((f32[3,8,128]{2,1,0:T(8,128)S(1)}, f32[3,8,128]{2,1,0:T(8,128)S(1)}, u32[]{:S(2)}, u32[]{:S(2)}) %collective-permute-start.6) | collective-permute-done | bytes 12320 | tf_op jit(solution)/shard_map/ppermute | solution.py:276
  37.9 0.0 collective-permute-done.7.col2
  37.9 0.8 %surface.1 = f32[8,96]{1,0:T(8,128)} custom-call(f32[3,8,128]{2,1,0:T(8,128)S(1)} %collective-permute-done.5.row1, f32[3,8,128]{2,1,0:T(8,128)S(1)} %collective-permute-done.4.row2, f32[3,8,128]{2,1,0:T(8,128)S(1)} %collective-permute-done.6.col1, f32[3,8,128]{2,1,0:T(8,128)S(1)} %collective-permute-done.7.col2, f32[3,8,128]{2,1,0:T(8,128)S(1)} %get-tuple-element.44.own, ...), custom_call_target="tpu_custom_call" | custom-call | flops 1000000 | bytes 200000 | tf_op jit(solution)/shard_map/surface/pallas_call | solution.py:295
  (9 shorter events, 0.0 us)
Async XLA Ops:
  1.8 6.5 %collective-permute-start = (f32[4,8,128]{2,1,0:T(8,128)S(1)}, f32[4,8,128]{2,1,0:T(8,128)S(1)}, u32[]{:S(2)}, u32[]{:S(2)}) collective-permute-start(f32[4,8,128]{2,1,0:T(8,128)S(1)} %get-tuple-element.27), channel_id=1, source_target_pairs={{64,128},{192,256},{320,384},{448,512},{576,640},{704,768},{832,89... | collective-permute-start | bytes 49160 | tf_op jit(solution)/shard_map/ppermute | solution.py:276
  3.8 4.5 %collective-permute-start.1 = (f32[4,8,128]{2,1,0:T(8,128)S(1)}, f32[4,8,128]{2,1,0:T(8,128)S(1)}, u32[]{:S(2)}, u32[]{:S(2)}) collective-permute-start(f32[4,8,128]{2,1,0:T(8,128)S(1)} %get-tuple-element.29), channel_id=1, source_target_pairs={{0,64},{64,0},{128,192},{192,128},{256,320},{320,256},{384,448},{4... | collective-permute-start | bytes 49160 | tf_op jit(solution)/shard_map/ppermute | solution.py:278
  8.3 9.4 %collective-permute-start.2 = (f32[4,8,128]{2,1,0:T(8,128)S(1)}, f32[4,8,128]{2,1,0:T(8,128)S(1)}, u32[]{:S(2)}, u32[]{:S(2)}) collective-permute-start(f32[4,8,128]{2,1,0:T(8,128)S(1)} %get-tuple-element.49.after), channel_id=1, source_target_pairs={{1,2},{3,4},{5,6},{7,8},{9,10},{11,12},{13,14},{15,16},{17,18},{19... | collective-permute-start | bytes 49160 | tf_op jit(solution)/shard_map/ppermute | solution.py:276
  14.6 5.6 %collective-permute-start.3 = (f32[4,8,128]{2,1,0:T(8,128)S(1)}, f32[4,8,128]{2,1,0:T(8,128)S(1)}, u32[]{:S(2)}, u32[]{:S(2)}) collective-permute-start(f32[4,8,128]{2,1,0:T(8,128)S(1)} %get-tuple-element.31), channel_id=1, source_target_pairs={{0,1},{1,0},{2,3},{3,2},{4,5},{5,4},{6,7},{7,6},{8,9},{9,8},{10,11... | collective-permute-start | bytes 49160 | tf_op jit(solution)/shard_map/ppermute | solution.py:278
  21.3 7.7 %collective-permute-start.5 = (f32[3,8,128]{2,1,0:T(8,128)S(1)}, f32[3,8,128]{2,1,0:T(8,128)S(1)}, u32[]{:S(2)}, u32[]{:S(2)}) collective-permute-start(f32[3,8,128]{2,1,0:T(8,128)S(1)} %get-tuple-element.42), channel_id=1, source_target_pairs={{64,128},{192,256},{320,384},{448,512},{576,640},{704,768},{832,89... | collective-permute-start | bytes 36872 | tf_op jit(solution)/shard_map/ppermute | solution.py:276
  23.2 5.7 %collective-permute-start.4 = (f32[3,8,128]{2,1,0:T(8,128)S(1)}, f32[3,8,128]{2,1,0:T(8,128)S(1)}, u32[]{:S(2)}, u32[]{:S(2)}) collective-permute-start(f32[3,8,128]{2,1,0:T(8,128)S(1)} %get-tuple-element.43), channel_id=1, source_target_pairs={{0,64},{64,0},{128,192},{192,128},{256,320},{320,256},{384,448},{4... | collective-permute-start | bytes 36872 | tf_op jit(solution)/shard_map/ppermute | solution.py:278
  29.0 8.9 %collective-permute-start.6 = (f32[3,8,128]{2,1,0:T(8,128)S(1)}, f32[3,8,128]{2,1,0:T(8,128)S(1)}, u32[]{:S(2)}, u32[]{:S(2)}) collective-permute-start(f32[3,8,128]{2,1,0:T(8,128)S(1)} %get-tuple-element.53.after), channel_id=1, source_target_pairs={{1,2},{3,4},{5,6},{7,8},{9,10},{11,12},{13,14},{15,16},{17,18},{19... | collective-permute-start | bytes 36872 | tf_op jit(solution)/shard_map/ppermute | solution.py:276
  32.3 5.6 %collective-permute-start.7 = (f32[3,8,128]{2,1,0:T(8,128)S(1)}, f32[3,8,128]{2,1,0:T(8,128)S(1)}, u32[]{:S(2)}, u32[]{:S(2)}) collective-permute-start(f32[3,8,128]{2,1,0:T(8,128)S(1)} %get-tuple-element.46), channel_id=1, source_target_pairs={{0,1},{1,0},{2,3},{3,2},{4,5},{5,4},{6,7},{7,6},{8,9},{9,8},{10,11... | collective-permute-start | bytes 36872 | tf_op jit(solution)/shard_map/ppermute | solution.py:278

commit v7 on v6

--- a/solution.py
+++ b/solution.py
@@ -126,21 +126,21 @@
             matrix[at_rows, 2 * y * width : 2 * (y + 1) * width] = pair
 
 
-def hot_kernel(index, count, fresh, after, hot, new_state, index_scr, sem):
+def hot_kernel(index, count, fresh, hot, new_state, index_scr, sem):
     store = pltpu.make_async_copy(fresh, new_state, sem)
     store.start()
     slots = index.shape[2]
-    cells, width = hot.shape[1], index_scr.shape[1]
-    index_scr[...] = jnp.zeros_like(index_scr)
-    for i in range(9):
-        index_scr[i : i + 1, 0:slots] = index[i]
-    lane = lanes_of((1, width))
-    used = [lane < jnp.broadcast_to(count[i // 3][:, i % 3 : i % 3 + 1], (1, width)) for i in range(9)]
-    places = [jnp.where(used[i], index_scr[i : i + 1, :], -1) for i in range(9)]
-    turned = jnp.concatenate(places + [places[0]] * 7, axis=0).astype(F32).T.astype(jnp.int32)
-    cell = lanes_of((width, cells))
-    for i in range(9):
-        here = jnp.broadcast_to(turned[:, i : i + 1], (width, cells)) == cell
+    wide, width = hot.shape[1], index_scr.shape[1]
+    index_scr[...] = jnp.full_like(index_scr, -1)
+    lane = lanes_of((1, slots))
+    for i in range(9):
+        used = lane < jnp.broadcast_to(count[i // 3][:, i % 3 : i % 3 + 1], (1, slots))
+        index_scr[i : i + 1, 0:slots] = jnp.where(used, index[i], -1)
+        index_scr[i : i + 1, OFF : OFF + slots] = jnp.where(used, index[i] + wide // 2, -1)
+    turned = index_scr[...].astype(F32).T.astype(jnp.int32)
+    cell = lanes_of((width, wide))
+    for i in range(9):
+        here = jnp.broadcast_to(turned[:, i : i + 1], (width, wide)) == cell
         hot[i * width : (i + 1) * width, :] = here.astype(F32).astype(BF16)
     store.wait()
 
@@ -254,14 +254,13 @@
             jnp.where(plus_c, col1[a], col2[a]),
         ]
     values = jnp.concatenate(blocks, axis=1)
-    weights = jnp.concatenate([pltpu.roll(block, OFF, 1) for block in blocks], axis=1)
     value_high = values.astype(BF16).astype(F32)
-    weight_high = weights.astype(BF16).astype(F32)
-    left = jnp.concatenate([value_high, weight_high, values - value_high, weights - weight_high], axis=0)
-    total = jnp.dot(left.astype(BF16), hot[...], preferred_element_type=F32)
-    total = total[0:16] + total[16:32]
-    cover = jnp.maximum(jnp.broadcast_to(total[8:9], (8, cells)), 1.0)
-    result[...] = total[0:8] / cover
+    left = jnp.concatenate([value_high, values - value_high], axis=0).astype(BF16)
+    total = jnp.dot(left, hot[...], preferred_element_type=F32)
+    total = total[0:8] + total[8:16]
+    half = total.shape[1] // 2
+    cover = jnp.maximum(jnp.broadcast_to(total[0:1, half : half + cells], (8, cells)), 1.0)
+    result[...] = total[:, 0:cells] / cover
 
 
 def swaps(count):
@@ -271,10 +270,13 @@
     return near, far
 
 
-def exchange(send1, send2, axis):
+def exchange(send1, send2, axis, far_first=True):
     near, far = swaps(lax.axis_size(axis))
+    if far_first:
+        send2, _ = lax.optimization_barrier((send2, send1))
+    else:
+        send1, _ = lax.optimization_barrier((send1, send2))
     one = lax.ppermute(send1, axis, far)
-    send2, _ = lax.optimization_barrier((send2, send1))
     two = lax.ppermute(send2, axis, near)
     return one, two
 
@@ -373,19 +375,20 @@
         row1, row2, col1, col2, own, matrix, late, state, velocity, diffusivity, wet,
         name="ocean",
     )
-    row1, row2 = exchange(send1, send2, "row")
-    send1, send2 = column_sends(row1, row2, own, [], plus_r, plus_c)
-    col1, col2 = exchange(send1, send2, "col")
+    row1, row2 = exchange(send1, send2, "row", far_first=False)
     hot, new_state = call(
         hot_kernel,
-        [shape(9 * width, atm_cells, dtype=BF16), shape(fields * rows, width)],
+        [shape(9 * width, 2 * width, dtype=BF16), shape(fields * rows, width)],
         [pltpu.VMEM((16, width), jnp.int32), pltpu.SemaphoreType.DMA],
-        [VMEM] * 4,
+        [VMEM] * 3,
         1_000_000, 200_000,
-        index, count, fresh, send1,
+        index, count, fresh,
         out_specs=[VMEM, HBM],
         name="hot",
     )
+    row1, row2, hot = lax.optimization_barrier((row1, row2, hot))
+    send1, send2 = column_sends(row1, row2, own, [], plus_r, plus_c)
+    col1, col2 = exchange(send1, send2, "col")
     (result,) = call(
         surface_kernel,
         [shape(fields, atm_cells)],

time: 39.2 us -> 40.5 us (1.033)
  the two profiles are of different devices: /device:TPU:430 before, /device:TPU:1 now
where the time goes in v7:
time: 40.5 us; the launch traced here: 40.1 us
  starting transfers between devices  28.2 us (70%)
  waiting for transfers between devices  6 us (15%)
  Pallas kernels  5.04 us (12%)
  between operations  0.83 us (2%)
    ppermute x4, starting transfers between devices, exchange(): two = lax.ppermute(send2, axis, near)  20.2 us
    ppermute x4, starting transfers between devices, exchange(): one = lax.ppermute(send1, axis, far)  7.95 us
    pallas_call x5, Pallas kernels, call(): pl.pallas_call(kernel, out_shape=outs, in_specs=specs, out_specs=out_spec...  5.04 us
    ppermute x4, waiting for transfers between devices, exchange(): two = lax.ppermute(send2, axis, near)  3.57 us
    ppermute x4, waiting for transfers between devices, exchange(): one = lax.ppermute(send1, axis, far)  2.43 us
  transfers between devices with their start and end apart: 8, of which 4 were waited for; matrix products, arithmetic and copies ran while one was open for 0% of the time, Pallas kernels for 5%

profile of v7, /device:TPU:1, one launch (start us, length us, event | category | flops | bytes accessed | tf_op | source)
XLA Modules:
  0.0 40.1 jit_solution(2299657697208475798)
XLA Ops:
  0.6 1.2 %pack.1 = (f32[4,8,128]{2,1,0:T(8,128)S(1)}, f32[4,8,128]{2,1,0:T(8,128)S(1)}, f32[5,8,128]{2,1,0:T(8,128)S(1)}, s32[9,1,48]{2,1,0:T(1,128)S(1)}, s32[3,1,3]{2,1...) custom-call(f32[20,96]{1,0:T(8,128)} %flux.1, ...), custom_call_target="tpu_custom_call" | custom-call | flops 100000 | bytes 1000000 | tf_op jit(solution)/shard_map/pack/pallas_call | solution.py:297
  1.8 4.7 %collective-permute-start = (f32[4,8,128]{2,1,0:T(8,128)S(1)}, f32[4,8,128]{2,1,0:T(8,128)S(1)}, u32[]{:S(2)}, u32[]{:S(2)}) collective-permute-start(f32[4,8,128]{2,1,0:T(8,128)S(1)} %get-tuple-element.30), channel_id=1, source_target_pairs={{64,128},{192,256},{320,384},{448,512},{576,640},{704,768},{832,89... | collective-permute-start | bytes 49160 | tf_op jit(solution)/shard_map/ppermute | solution.py:279
  6.6 12.0 %collective-permute-start.1 = (f32[4,8,128]{2,1,0:T(8,128)S(1)}, f32[4,8,128]{2,1,0:T(8,128)S(1)}, u32[]{:S(2)}, u32[]{:S(2)}) collective-permute-start(f32[4,8,128]{2,1,0:T(8,128)S(1)} %get-tuple-element.32), channel_id=1, source_target_pairs={{0,64},{64,0},{128,192},{192,128},{256,320},{320,256},{384,448},{4... | collective-permute-start | bytes 49160 | tf_op jit(solution)/shard_map/ppermute | solution.py:280
  18.6 0.8 %collective-permute-done.1.row2 = f32[4,8,128]{2,1,0:T(8,128)S(1)} collective-permute-done((f32[4,8,128]{2,1,0:T(8,128)S(1)}, f32[4,8,128]{2,1,0:T(8,128)S(1)}, u32[]{:S(2)}, u32[]{:S(2)}) %collective-permute-start.1) | collective-permute-done | bytes 16416 | tf_op jit(solution)/shard_map/ppermute | solution.py:280
  19.4 0.0 collective-permute-done.row1
  19.4 0.7 %collective-permute-start.2 = (f32[4,8,128]{2,1,0:T(8,128)S(1)}, f32[4,8,128]{2,1,0:T(8,128)S(1)}, u32[]{:S(2)}, u32[]{:S(2)}) collective-permute-start(f32[4,8,128]{2,1,0:T(8,128)S(1)} %get-tuple-element.55.after), channel_id=1, source_target_pairs={{1,2},{3,4},{5,6},{7,8},{9,10},{11,12},{13,14},{15,16},{17,18},{19... | collective-permute-start | bytes 49160 | tf_op jit(solution)/shard_map/ppermute | solution.py:279
  20.1 1.9 %collective-permute-start.3 = (f32[4,8,128]{2,1,0:T(8,128)S(1)}, f32[4,8,128]{2,1,0:T(8,128)S(1)}, u32[]{:S(2)}, u32[]{:S(2)}) collective-permute-start(f32[4,8,128]{2,1,0:T(8,128)S(1)} %get-tuple-element.34), channel_id=1, source_target_pairs={{0,1},{1,0},{2,3},{3,2},{4,5},{5,4},{6,7},{7,6},{8,9},{9,8},{10,11... | collective-permute-start | bytes 49160 | tf_op jit(solution)/shard_map/ppermute | solution.py:280
  22.0 1.3 %spread.1 = (bf16[432,2048]{1,0:T(8,128)(2,1)S(1)}, f32[8,432]{1,0:T(8,128)S(1)}) custom-call(s32[9,1,48]{2,1,0:T(1,128)S(1)} %get-tuple-element.35.start, f32[1,3,3,48,128]{4,3,2,1,0:T(8,128)S(1)} %get-tuple-element.36.weight, f32[4,8,128]{2,1,0:T(8,128)S(1)} %get-tuple-element.55.after), custom_call_target="tpu_custom_call" | custom-call | flops 20000000 | bytes 4000000 | tf_op jit(solution)/shard_map/spread/pallas_call | solution.py:297
  23.3 0.0 collective-permute-done.2.col1
  23.3 1.3 %collective-permute-done.3.col2 = f32[4,8,128]{2,1,0:T(8,128)S(1)} collective-permute-done((f32[4,8,128]{2,1,0:T(8,128)S(1)}, f32[4,8,128]{2,1,0:T(8,128)S(1)}, u32[]{:S(2)}, u32[]{:S(2)}) %collective-permute-start.3) | collective-permute-done | bytes 16416 | tf_op jit(solution)/shard_map/ppermute | solution.py:280
  24.6 1.1 %ocean.1 = (f32[128,128]{1,0:T(8,128)S(1)}, f32[3,8,128]{2,1,0:T(8,128)S(1)}, f32[3,8,128]{2,1,0:T(8,128)S(1)}, f32[3,8,128]{2,1,0:T(8,128)S(1)}) custom-call(f32[4,8,128]{2,1,0:T(8,128)S(1)} %collective-permute-done.row1, f32[4,8,128]{2,1,0:T(8,128)S(1)} %collective-permute-done.1.row2, f32[4,8,128]{2,1,0:T(8,128)S(1)} %collective-permute-done.2.col1, ...), custom_call_target="tpu_custom_call" | custom-call | flops 100000000 | bytes 4000000 | tf_op jit(solution)/shard_map/ocean/pallas_call | solution.py:297
  25.7 3.4 %collective-permute-start.5 = (f32[3,8,128]{2,1,0:T(8,128)S(1)}, f32[3,8,128]{2,1,0:T(8,128)S(1)}, u32[]{:S(2)}, u32[]{:S(2)}) collective-permute-start(f32[3,8,128]{2,1,0:T(8,128)S(1)} %get-tuple-element.46), channel_id=1, source_target_pairs={{0,64},{64,0},{128,192},{192,128},{256,320},{320,256},{384,448},{4... | collective-permute-start | bytes 36872 | tf_op jit(solution)/shard_map/ppermute | solution.py:280
  29.1 1.9 %collective-permute-start.4 = (f32[3,8,128]{2,1,0:T(8,128)S(1)}, f32[3,8,128]{2,1,0:T(8,128)S(1)}, u32[]{:S(2)}, u32[]{:S(2)}) collective-permute-start(f32[3,8,128]{2,1,0:T(8,128)S(1)} %get-tuple-element.47), channel_id=1, source_target_pairs={{64,128},{192,256},{320,384},{448,512},{576,640},{704,768},{832,89... | collective-permute-start | bytes 36872 | tf_op jit(solution)/shard_map/ppermute | solution.py:279
  31.1 0.6 %hot.1 = (bf16[1152,256]{1,0:T(8,128)(2,1)S(1)}, f32[128,128]{1,0:T(8,128)}) custom-call(s32[9,1,48]{2,1,0:T(1,128)S(1)} %get-tuple-element.28.index, s32[3,1,3]{2,1,0:T(1,128)S(1)} %get-tuple-element.29.count, f32[128,128]{1,0:T(8,128)S(1)} %get-tuple-element.43.fresh), custom_call_target="tpu_custom_call" | custom-call | flops 1000000 | bytes 200000 | tf_op jit(solution)/shard_map/hot/pallas_call | solution.py:297
  31.7 2.4 %collective-permute-done.4.row1 = f32[3,8,128]{2,1,0:T(8,128)S(1)} collective-permute-done((f32[3,8,128]{2,1,0:T(8,128)S(1)}, f32[3,8,128]{2,1,0:T(8,128)S(1)}, u32[]{:S(2)}, u32[]{:S(2)}) %collective-permute-start.4) | collective-permute-done | bytes 12320 | tf_op jit(solution)/shard_map/ppermute | solution.py:279
  34.1 0.0 collective-permute-done.5.row2
  34.2 0.7 %collective-permute-start.6 = (f32[3,8,128]{2,1,0:T(8,128)S(1)}, f32[3,8,128]{2,1,0:T(8,128)S(1)}, u32[]{:S(2)}, u32[]{:S(2)}) collective-permute-start(f32[3,8,128]{2,1,0:T(8,128)S(1)} %get-tuple-element.59), channel_id=1, source_target_pairs={{1,2},{3,4},{5,6},{7,8},{9,10},{11,12},{13,14},{15,16},{17,18},{19... | collective-permute-start | bytes 36872 | tf_op jit(solution)/shard_map/ppermute | solution.py:279
  34.9 2.9 %collective-permute-start.7 = (f32[3,8,128]{2,1,0:T(8,128)S(1)}, f32[3,8,128]{2,1,0:T(8,128)S(1)}, u32[]{:S(2)}, u32[]{:S(2)}) collective-permute-start(f32[3,8,128]{2,1,0:T(8,128)S(1)} %get-tuple-element.52), channel_id=1, source_target_pairs={{0,1},{1,0},{2,3},{3,2},{4,5},{5,4},{6,7},{7,6},{8,9},{9,8},{10,11... | collective-permute-start | bytes 36872 | tf_op jit(solution)/shard_map/ppermute | solution.py:280
  37.8 0.0 collective-permute-done.6.col1
  37.8 1.5 %collective-permute-done.7.col2 = f32[3,8,128]{2,1,0:T(8,128)S(1)} collective-permute-done((f32[3,8,128]{2,1,0:T(8,128)S(1)}, f32[3,8,128]{2,1,0:T(8,128)S(1)}, u32[]{:S(2)}, u32[]{:S(2)}) %collective-permute-start.7) | collective-permute-done | bytes 12320 | tf_op jit(solution)/shard_map/ppermute | solution.py:280
  39.3 0.8 %surface.1 = f32[8,96]{1,0:T(8,128)} custom-call(f32[3,8,128]{2,1,0:T(8,128)S(1)} %collective-permute-done.4.row1, f32[3,8,128]{2,1,0:T(8,128)S(1)} %collective-permute-done.5.row2, f32[3,8,128]{2,1,0:T(8,128)S(1)} %collective-permute-done.6.col1, f32[3,8,128]{2,1,0:T(8,128)S(1)} %collective-permute-done.7.col2, f32[3,8,128]{2,1,0:T(8,128)S(1)} %get-tuple-element.51.own, ...), custom_call_target="tpu_custom_call" | custom-call | flops 1000000 | bytes 200000 | tf_op jit(solution)/shard_map/surface/pallas_call | solution.py:297
  (9 shorter events, 0.0 us)
Async XLA Ops:
  1.8 17.6 %collective-permute-start = (f32[4,8,128]{2,1,0:T(8,128)S(1)}, f32[4,8,128]{2,1,0:T(8,128)S(1)}, u32[]{:S(2)}, u32[]{:S(2)}) collective-permute-start(f32[4,8,128]{2,1,0:T(8,128)S(1)} %get-tuple-element.30), channel_id=1, source_target_pairs={{64,128},{192,256},{320,384},{448,512},{576,640},{704,768},{832,89... | collective-permute-start | bytes 49160 | tf_op jit(solution)/shard_map/ppermute | solution.py:279
  6.6 12.8 %collective-permute-start.1 = (f32[4,8,128]{2,1,0:T(8,128)S(1)}, f32[4,8,128]{2,1,0:T(8,128)S(1)}, u32[]{:S(2)}, u32[]{:S(2)}) collective-permute-start(f32[4,8,128]{2,1,0:T(8,128)S(1)} %get-tuple-element.32), channel_id=1, source_target_pairs={{0,64},{64,0},{128,192},{192,128},{256,320},{320,256},{384,448},{4... | collective-permute-start | bytes 49160 | tf_op jit(solution)/shard_map/ppermute | solution.py:280
  19.4 3.9 %collective-permute-start.2 = (f32[4,8,128]{2,1,0:T(8,128)S(1)}, f32[4,8,128]{2,1,0:T(8,128)S(1)}, u32[]{:S(2)}, u32[]{:S(2)}) collective-permute-start(f32[4,8,128]{2,1,0:T(8,128)S(1)} %get-tuple-element.55.after), channel_id=1, source_target_pairs={{1,2},{3,4},{5,6},{7,8},{9,10},{11,12},{13,14},{15,16},{17,18},{19... | collective-permute-start | bytes 49160 | tf_op jit(solution)/shard_map/ppermute | solution.py:279
  20.1 4.5 %collective-permute-start.3 = (f32[4,8,128]{2,1,0:T(8,128)S(1)}, f32[4,8,128]{2,1,0:T(8,128)S(1)}, u32[]{:S(2)}, u32[]{:S(2)}) collective-permute-start(f32[4,8,128]{2,1,0:T(8,128)S(1)} %get-tuple-element.34), channel_id=1, source_target_pairs={{0,1},{1,0},{2,3},{3,2},{4,5},{5,4},{6,7},{7,6},{8,9},{9,8},{10,11... | collective-permute-start | bytes 49160 | tf_op jit(solution)/shard_map/ppermute | solution.py:280
  25.7 8.4 %collective-permute-start.5 = (f32[3,8,128]{2,1,0:T(8,128)S(1)}, f32[3,8,128]{2,1,0:T(8,128)S(1)}, u32[]{:S(2)}, u32[]{:S(2)}) collective-permute-start(f32[3,8,128]{2,1,0:T(8,128)S(1)} %get-tuple-element.46), channel_id=1, source_target_pairs={{0,64},{64,0},{128,192},{192,128},{256,320},{320,256},{384,448},{4... | collective-permute-start | bytes 36872 | tf_op jit(solution)/shard_map/ppermute | solution.py:280
  29.1 5.0 %collective-permute-start.4 = (f32[3,8,128]{2,1,0:T(8,128)S(1)}, f32[3,8,128]{2,1,0:T(8,128)S(1)}, u32[]{:S(2)}, u32[]{:S(2)}) collective-permute-start(f32[3,8,128]{2,1,0:T(8,128)S(1)} %get-tuple-element.47), channel_id=1, source_target_pairs={{64,128},{192,256},{320,384},{448,512},{576,640},{704,768},{832,89... | collective-permute-start | bytes 36872 | tf_op jit(solution)/shard_map/ppermute | solution.py:279
  34.2 3.6 %collective-permute-start.6 = (f32[3,8,128]{2,1,0:T(8,128)S(1)}, f32[3,8,128]{2,1,0:T(8,128)S(1)}, u32[]{:S(2)}, u32[]{:S(2)}) collective-permute-start(f32[3,8,128]{2,1,0:T(8,128)S(1)} %get-tuple-element.59), channel_id=1, source_target_pairs={{1,2},{3,4},{5,6},{7,8},{9,10},{11,12},{13,14},{15,16},{17,18},{19... | collective-permute-start | bytes 36872 | tf_op jit(solution)/shard_map/ppermute | solution.py:279
  34.9 4.4 %collective-permute-start.7 = (f32[3,8,128]{2,1,0:T(8,128)S(1)}, f32[3,8,128]{2,1,0:T(8,128)S(1)}, u32[]{:S(2)}, u32[]{:S(2)}) collective-permute-start(f32[3,8,128]{2,1,0:T(8,128)S(1)} %get-tuple-element.52), channel_id=1, source_target_pairs={{0,1},{1,0},{2,3},{3,2},{4,5},{5,4},{6,7},{7,6},{8,9},{9,8},{10,11... | collective-permute-start | bytes 36872 | tf_op jit(solution)/shard_map/ppermute | solution.py:280

commit v8 on v6

--- a/solution.py
+++ b/solution.py
@@ -38,7 +38,7 @@
     for copy in copies:
         copy.start()
     slots = index.shape[2]
-    plus = far_is_plus("row")
+    plus = far_is_plus("col")
     index_scr[...] = jnp.zeros_like(index_scr)
     flux_scr[...] = jnp.zeros_like(flux_scr)
     for copy in copies[:5]:
@@ -63,8 +63,6 @@
         line = state_kept[pl.ds(y, 8, stride=rows), :]
         west = jnp.where(lane == y, jnp.broadcast_to(line[:, 0:1], mapped.shape), west)
         east = jnp.where(lane == y, jnp.broadcast_to(line[:, width - 1 : width], mapped.shape), east)
-    own[3] = west
-    own[4] = east
     groups = []
     for a in range(3):
         for b in range(3):
@@ -73,15 +71,15 @@
             picked = pick(mapped, places)
             flag = ((lane >= OFF) & (lane < OFF + used)).astype(F32)
             groups.append(jnp.where(lane < used, picked, flag))
-    for b in range(3):
-        up, down = groups[6 + b], groups[b]
-        send1[b] = jnp.where(plus, up, down)
-        send2[b] = jnp.where(plus, down, up)
-        own[b] = groups[3 + b]
-    first = state_kept[pl.ds(0, 8, stride=rows), :]
-    last = state_kept[pl.ds(rows - 1, 8, stride=rows), :]
-    send1[3] = jnp.where(plus, last, first)
-    send2[3] = jnp.where(plus, first, last)
+    for a in range(3):
+        up, down = groups[3 * a + 2], groups[3 * a]
+        send1[a] = jnp.where(plus, up, down)
+        send2[a] = jnp.where(plus, down, up)
+        own[a] = groups[3 * a + 1]
+    send1[3] = jnp.where(plus, east, west)
+    send2[3] = jnp.where(plus, west, east)
+    own[3] = state_kept[pl.ds(0, 8, stride=rows), :]
+    own[4] = state_kept[pl.ds(rows - 1, 8, stride=rows), :]
     for copy in copies[5:]:
         copy.wait()
 
@@ -161,10 +159,10 @@
     def from_minus(one, two, plus, i):
         return jnp.where(plus, two[i], one[i])
 
-    middle = [from_minus(row1, row2, plus_r, 1), own[1], from_plus(row1, row2, plus_r, 1)]
-    blocks = []
-    for p in range(3):
-        blocks += [from_minus(col1, col2, plus_c, p), middle[p], from_plus(col1, col2, plus_c, p)]
+    middle = [from_minus(col1, col2, plus_c, 1), own[1], from_plus(col1, col2, plus_c, 1)]
+    blocks = [from_minus(row1, row2, plus_r, q) for q in range(3)]
+    blocks += middle
+    blocks += [from_plus(row1, row2, plus_r, q) for q in range(3)]
     south_edge = from_minus(row1, row2, plus_r, 3)
     north_edge = from_plus(row1, row2, plus_r, 3)
     west_edge = from_minus(col1, col2, plus_c, 3)
@@ -279,12 +277,12 @@
     return one, two
 
 
-def column_sends(row1, row2, own, extra, plus_r, plus_c):
-    minus = jnp.where(plus_r, row2, row1)
-    plus = jnp.where(plus_r, row1, row2)
-    low = jnp.stack([minus[0], own[0], plus[0]] + [edge for edge in extra[:1]])
-    high = jnp.stack([minus[2], own[2], plus[2]] + [edge for edge in extra[1:]])
-    return jnp.where(plus_c, high, low), jnp.where(plus_c, low, high)
+def forward_sends(one, two, own, extra, plus_before, plus_next):
+    minus = jnp.where(plus_before, two, one)
+    plus = jnp.where(plus_before, one, two)
+    low = jnp.stack([minus[0], own[0], plus[0]] + extra[:1])
+    high = jnp.stack([minus[2], own[2], plus[2]] + extra[1:])
+    return jnp.where(plus_next, high, low), jnp.where(plus_next, low, high)
 
 
 def in_hbm(array):
@@ -360,10 +358,11 @@
             name="spread",
         )
 
+    col1, col2 = exchange(send1, send2, "col")
+    matrix, late = spread(own)
+    col1, col2, matrix = lax.optimization_barrier((col1, col2, matrix))
+    send1, send2 = forward_sends(col1, col2, own, [own[3], own[4]], plus_c, plus_r)
     row1, row2 = exchange(send1, send2, "row")
-    send1, send2 = column_sends(row1, row2, own, [own[3], own[4]], plus_r, plus_c)
-    col1, col2 = exchange(send1, send2, "col")
-    matrix, late = spread(send1)
     fresh, send1, send2, own = call(
         ocean_kernel,
         [shape(fields * rows, width), shape(3, 8, width), shape(3, 8, width), shape(3, 8, width)],
@@ -374,7 +373,7 @@
         name="ocean",
     )
     row1, row2 = exchange(send1, send2, "row")
-    send1, send2 = column_sends(row1, row2, own, [], plus_r, plus_c)
+    send1, send2 = forward_sends(row1, row2, own, [], plus_r, plus_c)
     col1, col2 = exchange(send1, send2, "col")
     hot, new_state = call(
         hot_kernel,

time: 39.2 us -> 39.2 us (level)
  no operation moved by 1% of the time
where the time goes in v8:
time: 39.2 us; the launch traced here: 38.8 us
  starting transfers between devices  25.8 us (66%)
  waiting for transfers between devices  7.03 us (18%)
  Pallas kernels  5.09 us (13%)
  between operations  0.81 us (2%)
    ppermute x4, starting transfers between devices, exchange(): one = lax.ppermute(send1, axis, far)  13.6 us
    ppermute x4, starting transfers between devices, exchange(): two = lax.ppermute(send2, axis, near)  12.2 us
    pallas_call x5, Pallas kernels, call(): pl.pallas_call(kernel, out_shape=outs, in_specs=specs, out_specs=out_spec...  5.09 us
    ppermute x4, waiting for transfers between devices, exchange(): two = lax.ppermute(send2, axis, near)  4 us
    ppermute x4, waiting for transfers between devices, exchange(): one = lax.ppermute(send1, axis, far)  3.03 us
  transfers between devices with their start and end apart: 8, of which 4 were waited for; matrix products, arithmetic and copies ran while one was open for 0% of the time, Pallas kernels for 5%

profile of v8, /device:TPU:430, one launch (start us, length us, event | category | flops | bytes accessed | tf_op | source)
XLA Modules:
  0.0 38.8 jit_solution(9008736555604381277)
XLA Ops:
  0.6 1.2 %pack.1 = (f32[4,8,128]{2,1,0:T(8,128)S(1)}, f32[4,8,128]{2,1,0:T(8,128)S(1)}, f32[5,8,128]{2,1,0:T(8,128)S(1)}, s32[9,1,48]{2,1,0:T(1,128)S(1)}, s32[3,1,3]{2,1...) custom-call(f32[20,96]{1,0:T(8,128)} %flux.1, ...), custom_call_target="tpu_custom_call" | custom-call | flops 100000 | bytes 1000000 | tf_op jit(solution)/shard_map/pack/pallas_call | solution.py:293
  1.9 6.2 %collective-permute-start = (f32[4,8,128]{2,1,0:T(8,128)S(1)}, f32[4,8,128]{2,1,0:T(8,128)S(1)}, u32[]{:S(2)}, u32[]{:S(2)}) collective-permute-start(f32[4,8,128]{2,1,0:T(8,128)S(1)} %get-tuple-element.30), channel_id=1, source_target_pairs={{1,2},{3,4},{5,6},{7,8},{9,10},{11,12},{13,14},{15,16},{17,18},{19... | collective-permute-start | bytes 49160 | tf_op jit(solution)/shard_map/ppermute | solution.py:274
  8.1 1.9 %collective-permute-start.1 = (f32[4,8,128]{2,1,0:T(8,128)S(1)}, f32[4,8,128]{2,1,0:T(8,128)S(1)}, u32[]{:S(2)}, u32[]{:S(2)}) collective-permute-start(f32[4,8,128]{2,1,0:T(8,128)S(1)} %get-tuple-element.32), channel_id=1, source_target_pairs={{0,1},{1,0},{2,3},{3,2},{4,5},{5,4},{6,7},{7,6},{8,9},{9,8},{10,11... | collective-permute-start | bytes 49160 | tf_op jit(solution)/shard_map/ppermute | solution.py:276
  10.0 1.3 %spread.1 = (bf16[432,2048]{1,0:T(8,128)(2,1)S(1)}, f32[8,432]{1,0:T(8,128)S(1)}) custom-call(s32[9,1,48]{2,1,0:T(1,128)S(1)} %get-tuple-element.33.start, f32[1,3,3,48,128]{4,3,2,1,0:T(8,128)S(1)} %get-tuple-element.34.weight, f32[5,8,128]{2,1,0:T(8,128)S(1)} %get-tuple-element.35.after.own), custom_call_target="tpu_custom_call" | custom-call | flops 20000000 | bytes 4000000 | tf_op jit(solution)/shard_map/spread/pallas_call | solution.py:293
  11.3 2.4 %collective-permute-done.1.col2 = f32[4,8,128]{2,1,0:T(8,128)S(1)} collective-permute-done((f32[4,8,128]{2,1,0:T(8,128)S(1)}, f32[4,8,128]{2,1,0:T(8,128)S(1)}, u32[]{:S(2)}, u32[]{:S(2)}) %collective-permute-start.1) | collective-permute-done | bytes 16416 | tf_op jit(solution)/shard_map/ppermute | solution.py:276
  13.7 0.0 collective-permute-done.col1
  13.7 1.9 %collective-permute-start.2 = (f32[4,8,128]{2,1,0:T(8,128)S(1)}, f32[4,8,128]{2,1,0:T(8,128)S(1)}, u32[]{:S(2)}, u32[]{:S(2)}) collective-permute-start(f32[4,8,128]{2,1,0:T(8,128)S(1)} %get-tuple-element.55), channel_id=1, source_target_pairs={{64,128},{192,256},{320,384},{448,512},{576,640},{704,768},{832,89... | collective-permute-start | bytes 49160 | tf_op jit(solution)/shard_map/ppermute | solution.py:274
  15.7 3.7 %collective-permute-start.3 = (f32[4,8,128]{2,1,0:T(8,128)S(1)}, f32[4,8,128]{2,1,0:T(8,128)S(1)}, u32[]{:S(2)}, u32[]{:S(2)}) collective-permute-start(f32[4,8,128]{2,1,0:T(8,128)S(1)} %get-tuple-element.39), channel_id=1, source_target_pairs={{0,64},{64,0},{128,192},{192,128},{256,320},{320,256},{384,448},{4... | collective-permute-start | bytes 49160 | tf_op jit(solution)/shard_map/ppermute | solution.py:276
  19.4 0.0 collective-permute-done.2.row1
  19.4 0.8 %collective-permute-done.3.row2 = f32[4,8,128]{2,1,0:T(8,128)S(1)} collective-permute-done((f32[4,8,128]{2,1,0:T(8,128)S(1)}, f32[4,8,128]{2,1,0:T(8,128)S(1)}, u32[]{:S(2)}, u32[]{:S(2)}) %collective-permute-start.3) | collective-permute-done | bytes 16416 | tf_op jit(solution)/shard_map/ppermute | solution.py:276
  20.2 1.1 %ocean.1 = (f32[128,128]{1,0:T(8,128)S(1)}, f32[3,8,128]{2,1,0:T(8,128)S(1)}, f32[3,8,128]{2,1,0:T(8,128)S(1)}, f32[3,8,128]{2,1,0:T(8,128)S(1)}) custom-call(f32[4,8,128]{2,1,0:T(8,128)S(1)} %collective-permute-done.2.row1, f32[4,8,128]{2,1,0:T(8,128)S(1)} %collective-permute-done.3.row2, f32[4,8,128]{2,1,0:T(8,128)S(1)} %collective-permute-done.col1, ...), custom_call_target="tpu_custom_call" | custom-call | flops 100000000 | bytes 4000000 | tf_op jit(solution)/shard_map/ocean/pallas_call | solution.py:293
  21.3 2.2 %collective-permute-start.5 = (f32[3,8,128]{2,1,0:T(8,128)S(1)}, f32[3,8,128]{2,1,0:T(8,128)S(1)}, u32[]{:S(2)}, u32[]{:S(2)}) collective-permute-start(f32[3,8,128]{2,1,0:T(8,128)S(1)} %get-tuple-element.48), channel_id=1, source_target_pairs={{64,128},{192,256},{320,384},{448,512},{576,640},{704,768},{832,89... | collective-permute-start | bytes 36872 | tf_op jit(solution)/shard_map/ppermute | solution.py:274
  23.5 4.6 %collective-permute-start.4 = (f32[3,8,128]{2,1,0:T(8,128)S(1)}, f32[3,8,128]{2,1,0:T(8,128)S(1)}, u32[]{:S(2)}, u32[]{:S(2)}) collective-permute-start(f32[3,8,128]{2,1,0:T(8,128)S(1)} %get-tuple-element.49), channel_id=1, source_target_pairs={{0,64},{64,0},{128,192},{192,128},{256,320},{320,256},{384,448},{4... | collective-permute-start | bytes 36872 | tf_op jit(solution)/shard_map/ppermute | solution.py:276
  28.2 0.8 %collective-permute-done.4.row2 = f32[3,8,128]{2,1,0:T(8,128)S(1)} collective-permute-done((f32[3,8,128]{2,1,0:T(8,128)S(1)}, f32[3,8,128]{2,1,0:T(8,128)S(1)}, u32[]{:S(2)}, u32[]{:S(2)}) %collective-permute-start.4) | collective-permute-done | bytes 12320 | tf_op jit(solution)/shard_map/ppermute | solution.py:276
  29.0 0.0 collective-permute-done.5.row1
  29.0 3.3 %collective-permute-start.6 = (f32[3,8,128]{2,1,0:T(8,128)S(1)}, f32[3,8,128]{2,1,0:T(8,128)S(1)}, u32[]{:S(2)}, u32[]{:S(2)}) collective-permute-start(f32[3,8,128]{2,1,0:T(8,128)S(1)} %get-tuple-element.59.after), channel_id=1, source_target_pairs={{1,2},{3,4},{5,6},{7,8},{9,10},{11,12},{13,14},{15,16},{17,18},{19... | collective-permute-start | bytes 36872 | tf_op jit(solution)/shard_map/ppermute | solution.py:274
  32.3 1.9 %collective-permute-start.7 = (f32[3,8,128]{2,1,0:T(8,128)S(1)}, f32[3,8,128]{2,1,0:T(8,128)S(1)}, u32[]{:S(2)}, u32[]{:S(2)}) collective-permute-start(f32[3,8,128]{2,1,0:T(8,128)S(1)} %get-tuple-element.52), channel_id=1, source_target_pairs={{0,1},{1,0},{2,3},{3,2},{4,5},{5,4},{6,7},{7,6},{8,9},{9,8},{10,11... | collective-permute-start | bytes 36872 | tf_op jit(solution)/shard_map/ppermute | solution.py:276
  34.2 0.6 %hot.1 = (bf16[1152,96]{1,0:T(8,128)(2,1)S(1)}, f32[128,128]{1,0:T(8,128)}) custom-call(s32[9,1,48]{2,1,0:T(1,128)S(1)} %get-tuple-element.28.index, s32[3,1,3]{2,1,0:T(1,128)S(1)} %get-tuple-element.29.count, f32[128,128]{1,0:T(8,128)S(1)} %get-tuple-element.46.fresh, f32[3,8,128]{2,1,0:T(8,128)S(1)} %get-tuple-element.59.after), custom_call_target="tpu_custom_call" | custom-call | flops 1000000 | bytes 200000 | tf_op jit(solution)/shard_map/hot/pallas_call | solution.py:293
  34.9 3.0 %collective-permute-done.6.col1 = f32[3,8,128]{2,1,0:T(8,128)S(1)} collective-permute-done((f32[3,8,128]{2,1,0:T(8,128)S(1)}, f32[3,8,128]{2,1,0:T(8,128)S(1)}, u32[]{:S(2)}, u32[]{:S(2)}) %collective-permute-start.6) | collective-permute-done | bytes 12320 | tf_op jit(solution)/shard_map/ppermute | solution.py:274
  37.9 0.0 collective-permute-done.7.col2
  37.9 0.8 %surface.1 = f32[8,96]{1,0:T(8,128)} custom-call(f32[3,8,128]{2,1,0:T(8,128)S(1)} %collective-permute-done.5.row1, f32[3,8,128]{2,1,0:T(8,128)S(1)} %collective-permute-done.4.row2, f32[3,8,128]{2,1,0:T(8,128)S(1)} %collective-permute-done.6.col1, f32[3,8,128]{2,1,0:T(8,128)S(1)} %collective-permute-done.7.col2, f32[3,8,128]{2,1,0:T(8,128)S(1)} %get-tuple-element.50.own, ...), custom_call_target="tpu_custom_call" | custom-call | flops 1000000 | bytes 200000 | tf_op jit(solution)/shard_map/surface/pallas_call | solution.py:293
  (9 shorter events, 0.0 us)
Async XLA Ops:
  1.9 11.8 %collective-permute-start = (f32[4,8,128]{2,1,0:T(8,128)S(1)}, f32[4,8,128]{2,1,0:T(8,128)S(1)}, u32[]{:S(2)}, u32[]{:S(2)}) collective-permute-start(f32[4,8,128]{2,1,0:T(8,128)S(1)} %get-tuple-element.30), channel_id=1, source_target_pairs={{1,2},{3,4},{5,6},{7,8},{9,10},{11,12},{13,14},{15,16},{17,18},{19... | collective-permute-start | bytes 49160 | tf_op jit(solution)/shard_map/ppermute | solution.py:274
  8.1 5.6 %collective-permute-start.1 = (f32[4,8,128]{2,1,0:T(8,128)S(1)}, f32[4,8,128]{2,1,0:T(8,128)S(1)}, u32[]{:S(2)}, u32[]{:S(2)}) collective-permute-start(f32[4,8,128]{2,1,0:T(8,128)S(1)} %get-tuple-element.32), channel_id=1, source_target_pairs={{0,1},{1,0},{2,3},{3,2},{4,5},{5,4},{6,7},{7,6},{8,9},{9,8},{10,11... | collective-permute-start | bytes 49160 | tf_op jit(solution)/shard_map/ppermute | solution.py:276
  13.7 5.6 %collective-permute-start.2 = (f32[4,8,128]{2,1,0:T(8,128)S(1)}, f32[4,8,128]{2,1,0:T(8,128)S(1)}, u32[]{:S(2)}, u32[]{:S(2)}) collective-permute-start(f32[4,8,128]{2,1,0:T(8,128)S(1)} %get-tuple-element.55), channel_id=1, source_target_pairs={{64,128},{192,256},{320,384},{448,512},{576,640},{704,768},{832,89... | collective-permute-start | bytes 49160 | tf_op jit(solution)/shard_map/ppermute | solution.py:274
  15.7 4.5 %collective-permute-start.3 = (f32[4,8,128]{2,1,0:T(8,128)S(1)}, f32[4,8,128]{2,1,0:T(8,128)S(1)}, u32[]{:S(2)}, u32[]{:S(2)}) collective-permute-start(f32[4,8,128]{2,1,0:T(8,128)S(1)} %get-tuple-element.39), channel_id=1, source_target_pairs={{0,64},{64,0},{128,192},{192,128},{256,320},{320,256},{384,448},{4... | collective-permute-start | bytes 49160 | tf_op jit(solution)/shard_map/ppermute | solution.py:276
  21.3 7.7 %collective-permute-start.5 = (f32[3,8,128]{2,1,0:T(8,128)S(1)}, f32[3,8,128]{2,1,0:T(8,128)S(1)}, u32[]{:S(2)}, u32[]{:S(2)}) collective-permute-start(f32[3,8,128]{2,1,0:T(8,128)S(1)} %get-tuple-element.48), channel_id=1, source_target_pairs={{64,128},{192,256},{320,384},{448,512},{576,640},{704,768},{832,89... | collective-permute-start | bytes 36872 | tf_op jit(solution)/shard_map/ppermute | solution.py:274
  23.5 5.5 %collective-permute-start.4 = (f32[3,8,128]{2,1,0:T(8,128)S(1)}, f32[3,8,128]{2,1,0:T(8,128)S(1)}, u32[]{:S(2)}, u32[]{:S(2)}) collective-permute-start(f32[3,8,128]{2,1,0:T(8,128)S(1)} %get-tuple-element.49), channel_id=1, source_target_pairs={{0,64},{64,0},{128,192},{192,128},{256,320},{320,256},{384,448},{4... | collective-permute-start | bytes 36872 | tf_op jit(solution)/shard_map/ppermute | solution.py:276
  29.0 8.9 %collective-permute-start.6 = (f32[3,8,128]{2,1,0:T(8,128)S(1)}, f32[3,8,128]{2,1,0:T(8,128)S(1)}, u32[]{:S(2)}, u32[]{:S(2)}) collective-permute-start(f32[3,8,128]{2,1,0:T(8,128)S(1)} %get-tuple-element.59.after), channel_id=1, source_target_pairs={{1,2},{3,4},{5,6},{7,8},{9,10},{11,12},{13,14},{15,16},{17,18},{19... | collective-permute-start | bytes 36872 | tf_op jit(solution)/shard_map/ppermute | solution.py:274
  32.3 5.6 %collective-permute-start.7 = (f32[3,8,128]{2,1,0:T(8,128)S(1)}, f32[3,8,128]{2,1,0:T(8,128)S(1)}, u32[]{:S(2)}, u32[]{:S(2)}) collective-permute-start(f32[3,8,128]{2,1,0:T(8,128)S(1)} %get-tuple-element.52), channel_id=1, source_target_pairs={{0,1},{1,0},{2,3},{3,2},{4,5},{5,4},{6,7},{7,6},{8,9},{9,8},{10,11... | collective-permute-start | bytes 36872 | tf_op jit(solution)/shard_map/ppermute | solution.py:276

commit v9 on v7

--- a/solution.py
+++ b/solution.py
@@ -270,13 +270,10 @@
     return near, far
 
 
-def exchange(send1, send2, axis, far_first=True):
+def exchange(send1, send2, axis):
     near, far = swaps(lax.axis_size(axis))
-    if far_first:
-        send2, _ = lax.optimization_barrier((send2, send1))
-    else:
-        send1, _ = lax.optimization_barrier((send1, send2))
     one = lax.ppermute(send1, axis, far)
+    send2, _ = lax.optimization_barrier((send2, send1))
     two = lax.ppermute(send2, axis, near)
     return one, two
 
@@ -375,7 +372,7 @@
         row1, row2, col1, col2, own, matrix, late, state, velocity, diffusivity, wet,
         name="ocean",
     )
-    row1, row2 = exchange(send1, send2, "row", far_first=False)
+    row1, row2 = exchange(send1, send2, "row")
     hot, new_state = call(
         hot_kernel,
         [shape(9 * width, 2 * width, dtype=BF16), shape(fields * rows, width)],

time: 40.5 us -> 39.1 us (0.965)
  the two profiles are of different devices: /device:TPU:1 before, /device:TPU:430 now
where the time goes in v9:
time: 39.1 us; the launch traced here: 38.7 us
  starting transfers between devices  25.8 us (66%)
  waiting for transfers between devices  7.02 us (18%)
  Pallas kernels  5.04 us (13%)
  between operations  0.81 us (2%)
    ppermute x4, starting transfers between devices, exchange(): one = lax.ppermute(send1, axis, far)  13.4 us
    ppermute x4, starting transfers between devices, exchange(): two = lax.ppermute(send2, axis, near)  12.5 us
    pallas_call x5, Pallas kernels, call(): pl.pallas_call(kernel, out_shape=outs, in_specs=specs, out_specs=out_spec...  5.04 us
    ppermute x4, waiting for transfers between devices, exchange(): one = lax.ppermute(send1, axis, far)  3.66 us
    ppermute x4, waiting for transfers between devices, exchange(): two = lax.ppermute(send2, axis, near)  3.36 us
  transfers between devices with their start and end apart: 8, of which 4 were waited for; matrix products, arithmetic and copies ran while one was open for 0% of the time, Pallas kernels for 5%

profile of v9, /device:TPU:430, one launch (start us, length us, event | category | flops | bytes accessed | tf_op | source)
XLA Modules:
  0.0 38.7 jit_solution(16273070596880615135)
XLA Ops:
  0.6 1.2 %pack.1 = (f32[4,8,128]{2,1,0:T(8,128)S(1)}, f32[4,8,128]{2,1,0:T(8,128)S(1)}, f32[5,8,128]{2,1,0:T(8,128)S(1)}, s32[9,1,48]{2,1,0:T(1,128)S(1)}, s32[3,1,3]{2,1...) custom-call(f32[20,96]{1,0:T(8,128)} %flux.1, ...), custom_call_target="tpu_custom_call" | custom-call | flops 100000 | bytes 1000000 | tf_op jit(solution)/shard_map/pack/pallas_call | solution.py:294
  1.8 1.9 %collective-permute-start = (f32[4,8,128]{2,1,0:T(8,128)S(1)}, f32[4,8,128]{2,1,0:T(8,128)S(1)}, u32[]{:S(2)}, u32[]{:S(2)}) collective-permute-start(f32[4,8,128]{2,1,0:T(8,128)S(1)} %get-tuple-element.30), channel_id=1, source_target_pairs={{64,128},{192,256},{320,384},{448,512},{576,640},{704,768},{832,89... | collective-permute-start | bytes 49160 | tf_op jit(solution)/shard_map/ppermute | solution.py:275
  3.8 3.7 %collective-permute-start.1 = (f32[4,8,128]{2,1,0:T(8,128)S(1)}, f32[4,8,128]{2,1,0:T(8,128)S(1)}, u32[]{:S(2)}, u32[]{:S(2)}) collective-permute-start(f32[4,8,128]{2,1,0:T(8,128)S(1)} %get-tuple-element.32), channel_id=1, source_target_pairs={{0,64},{64,0},{128,192},{192,128},{256,320},{320,256},{384,448},{4... | collective-permute-start | bytes 49160 | tf_op jit(solution)/shard_map/ppermute | solution.py:277
  7.5 0.8 %collective-permute-done.1.row2 = f32[4,8,128]{2,1,0:T(8,128)S(1)} collective-permute-done((f32[4,8,128]{2,1,0:T(8,128)S(1)}, f32[4,8,128]{2,1,0:T(8,128)S(1)}, u32[]{:S(2)}, u32[]{:S(2)}) %collective-permute-start.1) | collective-permute-done | bytes 16416 | tf_op jit(solution)/shard_map/ppermute | solution.py:277
  8.3 0.0 collective-permute-done.row1
  8.3 6.2 %collective-permute-start.2 = (f32[4,8,128]{2,1,0:T(8,128)S(1)}, f32[4,8,128]{2,1,0:T(8,128)S(1)}, u32[]{:S(2)}, u32[]{:S(2)}) collective-permute-start(f32[4,8,128]{2,1,0:T(8,128)S(1)} %get-tuple-element.55.after), channel_id=1, source_target_pairs={{1,2},{3,4},{5,6},{7,8},{9,10},{11,12},{13,14},{15,16},{17,18},{19... | collective-permute-start | bytes 49160 | tf_op jit(solution)/shard_map/ppermute | solution.py:275
  14.6 1.9 %collective-permute-start.3 = (f32[4,8,128]{2,1,0:T(8,128)S(1)}, f32[4,8,128]{2,1,0:T(8,128)S(1)}, u32[]{:S(2)}, u32[]{:S(2)}) collective-permute-start(f32[4,8,128]{2,1,0:T(8,128)S(1)} %get-tuple-element.34), channel_id=1, source_target_pairs={{0,1},{1,0},{2,3},{3,2},{4,5},{5,4},{6,7},{7,6},{8,9},{9,8},{10,11... | collective-permute-start | bytes 49160 | tf_op jit(solution)/shard_map/ppermute | solution.py:277
  16.5 1.3 %spread.1 = (bf16[432,2048]{1,0:T(8,128)(2,1)S(1)}, f32[8,432]{1,0:T(8,128)S(1)}) custom-call(s32[9,1,48]{2,1,0:T(1,128)S(1)} %get-tuple-element.35.start, f32[1,3,3,48,128]{4,3,2,1,0:T(8,128)S(1)} %get-tuple-element.36.weight, f32[4,8,128]{2,1,0:T(8,128)S(1)} %get-tuple-element.55.after), custom_call_target="tpu_custom_call" | custom-call | flops 20000000 | bytes 4000000 | tf_op jit(solution)/shard_map/spread/pallas_call | solution.py:294
  17.8 0.0 collective-permute-done.2.col1
  17.8 2.4 %collective-permute-done.3.col2 = f32[4,8,128]{2,1,0:T(8,128)S(1)} collective-permute-done((f32[4,8,128]{2,1,0:T(8,128)S(1)}, f32[4,8,128]{2,1,0:T(8,128)S(1)}, u32[]{:S(2)}, u32[]{:S(2)}) %collective-permute-start.3) | collective-permute-done | bytes 16416 | tf_op jit(solution)/shard_map/ppermute | solution.py:277
  20.2 1.1 %ocean.1 = (f32[128,128]{1,0:T(8,128)S(1)}, f32[3,8,128]{2,1,0:T(8,128)S(1)}, f32[3,8,128]{2,1,0:T(8,128)S(1)}, f32[3,8,128]{2,1,0:T(8,128)S(1)}) custom-call(f32[4,8,128]{2,1,0:T(8,128)S(1)} %collective-permute-done.row1, f32[4,8,128]{2,1,0:T(8,128)S(1)} %collective-permute-done.1.row2, f32[4,8,128]{2,1,0:T(8,128)S(1)} %collective-permute-done.2.col1, ...), custom_call_target="tpu_custom_call" | custom-call | flops 100000000 | bytes 4000000 | tf_op jit(solution)/shard_map/ocean/pallas_call | solution.py:294
  21.3 1.9 %collective-permute-start.4 = (f32[3,8,128]{2,1,0:T(8,128)S(1)}, f32[3,8,128]{2,1,0:T(8,128)S(1)}, u32[]{:S(2)}, u32[]{:S(2)}) collective-permute-start(f32[3,8,128]{2,1,0:T(8,128)S(1)} %get-tuple-element.45), channel_id=1, source_target_pairs={{64,128},{192,256},{320,384},{448,512},{576,640},{704,768},{832,89... | collective-permute-start | bytes 36872 | tf_op jit(solution)/shard_map/ppermute | solution.py:275
  23.2 4.9 %collective-permute-start.5 = (f32[3,8,128]{2,1,0:T(8,128)S(1)}, f32[3,8,128]{2,1,0:T(8,128)S(1)}, u32[]{:S(2)}, u32[]{:S(2)}) collective-permute-start(f32[3,8,128]{2,1,0:T(8,128)S(1)} %get-tuple-element.47), channel_id=1, source_target_pairs={{0,64},{64,0},{128,192},{192,128},{256,320},{320,256},{384,448},{4... | collective-permute-start | bytes 36872 | tf_op jit(solution)/shard_map/ppermute | solution.py:277
  28.2 0.6 %hot.1 = (bf16[1152,256]{1,0:T(8,128)(2,1)S(1)}, f32[128,128]{1,0:T(8,128)}) custom-call(s32[9,1,48]{2,1,0:T(1,128)S(1)} %get-tuple-element.28.index, s32[3,1,3]{2,1,0:T(1,128)S(1)} %get-tuple-element.29.count, f32[128,128]{1,0:T(8,128)S(1)} %get-tuple-element.43.fresh), custom_call_target="tpu_custom_call" | custom-call | flops 1000000 | bytes 200000 | tf_op jit(solution)/shard_map/hot/pallas_call | solution.py:294
  28.8 0.1 collective-permute-done.5.row2
  29.0 0.0 collective-permute-done.4.row1
  29.0 3.3 %collective-permute-start.6 = (f32[3,8,128]{2,1,0:T(8,128)S(1)}, f32[3,8,128]{2,1,0:T(8,128)S(1)}, u32[]{:S(2)}, u32[]{:S(2)}) collective-permute-start(f32[3,8,128]{2,1,0:T(8,128)S(1)} %get-tuple-element.59), channel_id=1, source_target_pairs={{1,2},{3,4},{5,6},{7,8},{9,10},{11,12},{13,14},{15,16},{17,18},{19... | collective-permute-start | bytes 36872 | tf_op jit(solution)/shard_map/ppermute | solution.py:275
  32.3 1.9 %collective-permute-start.7 = (f32[3,8,128]{2,1,0:T(8,128)S(1)}, f32[3,8,128]{2,1,0:T(8,128)S(1)}, u32[]{:S(2)}, u32[]{:S(2)}) collective-permute-start(f32[3,8,128]{2,1,0:T(8,128)S(1)} %get-tuple-element.52), channel_id=1, source_target_pairs={{0,1},{1,0},{2,3},{3,2},{4,5},{5,4},{6,7},{7,6},{8,9},{9,8},{10,11... | collective-permute-start | bytes 36872 | tf_op jit(solution)/shard_map/ppermute | solution.py:277
  34.3 3.7 %collective-permute-done.6.col1 = f32[3,8,128]{2,1,0:T(8,128)S(1)} collective-permute-done((f32[3,8,128]{2,1,0:T(8,128)S(1)}, f32[3,8,128]{2,1,0:T(8,128)S(1)}, u32[]{:S(2)}, u32[]{:S(2)}) %collective-permute-start.6) | collective-permute-done | bytes 12320 | tf_op jit(solution)/shard_map/ppermute | solution.py:275
  37.9 0.0 collective-permute-done.7.col2
  37.9 0.8 %surface.1 = f32[8,96]{1,0:T(8,128)} custom-call(f32[3,8,128]{2,1,0:T(8,128)S(1)} %collective-permute-done.4.row1, f32[3,8,128]{2,1,0:T(8,128)S(1)} %collective-permute-done.5.row2, f32[3,8,128]{2,1,0:T(8,128)S(1)} %collective-permute-done.6.col1, f32[3,8,128]{2,1,0:T(8,128)S(1)} %collective-permute-done.7.col2, f32[3,8,128]{2,1,0:T(8,128)S(1)} %get-tuple-element.51.own, ...), custom_call_target="tpu_custom_call" | custom-call | flops 1000000 | bytes 200000 | tf_op jit(solution)/shard_map/surface/pallas_call | solution.py:294
  (9 shorter events, 0.0 us)
Async XLA Ops:
  1.8 6.5 %collective-permute-start = (f32[4,8,128]{2,1,0:T(8,128)S(1)}, f32[4,8,128]{2,1,0:T(8,128)S(1)}, u32[]{:S(2)}, u32[]{:S(2)}) collective-permute-start(f32[4,8,128]{2,1,0:T(8,128)S(1)} %get-tuple-element.30), channel_id=1, source_target_pairs={{64,128},{192,256},{320,384},{448,512},{576,640},{704,768},{832,89... | collective-permute-start | bytes 49160 | tf_op jit(solution)/shard_map/ppermute | solution.py:275
  3.8 4.5 %collective-permute-start.1 = (f32[4,8,128]{2,1,0:T(8,128)S(1)}, f32[4,8,128]{2,1,0:T(8,128)S(1)}, u32[]{:S(2)}, u32[]{:S(2)}) collective-permute-start(f32[4,8,128]{2,1,0:T(8,128)S(1)} %get-tuple-element.32), channel_id=1, source_target_pairs={{0,64},{64,0},{128,192},{192,128},{256,320},{320,256},{384,448},{4... | collective-permute-start | bytes 49160 | tf_op jit(solution)/shard_map/ppermute | solution.py:277
  8.3 9.4 %collective-permute-start.2 = (f32[4,8,128]{2,1,0:T(8,128)S(1)}, f32[4,8,128]{2,1,0:T(8,128)S(1)}, u32[]{:S(2)}, u32[]{:S(2)}) collective-permute-start(f32[4,8,128]{2,1,0:T(8,128)S(1)} %get-tuple-element.55.after), channel_id=1, source_target_pairs={{1,2},{3,4},{5,6},{7,8},{9,10},{11,12},{13,14},{15,16},{17,18},{19... | collective-permute-start | bytes 49160 | tf_op jit(solution)/shard_map/ppermute | solution.py:275
  14.6 5.6 %collective-permute-start.3 = (f32[4,8,128]{2,1,0:T(8,128)S(1)}, f32[4,8,128]{2,1,0:T(8,128)S(1)}, u32[]{:S(2)}, u32[]{:S(2)}) collective-permute-start(f32[4,8,128]{2,1,0:T(8,128)S(1)} %get-tuple-element.34), channel_id=1, source_target_pairs={{0,1},{1,0},{2,3},{3,2},{4,5},{5,4},{6,7},{7,6},{8,9},{9,8},{10,11... | collective-permute-start | bytes 49160 | tf_op jit(solution)/shard_map/ppermute | solution.py:277
  21.3 7.7 %collective-permute-start.4 = (f32[3,8,128]{2,1,0:T(8,128)S(1)}, f32[3,8,128]{2,1,0:T(8,128)S(1)}, u32[]{:S(2)}, u32[]{:S(2)}) collective-permute-start(f32[3,8,128]{2,1,0:T(8,128)S(1)} %get-tuple-element.45), channel_id=1, source_target_pairs={{64,128},{192,256},{320,384},{448,512},{576,640},{704,768},{832,89... | collective-permute-start | bytes 36872 | tf_op jit(solution)/shard_map/ppermute | solution.py:275
  23.2 5.7 %collective-permute-start.5 = (f32[3,8,128]{2,1,0:T(8,128)S(1)}, f32[3,8,128]{2,1,0:T(8,128)S(1)}, u32[]{:S(2)}, u32[]{:S(2)}) collective-permute-start(f32[3,8,128]{2,1,0:T(8,128)S(1)} %get-tuple-element.47), channel_id=1, source_target_pairs={{0,64},{64,0},{128,192},{192,128},{256,320},{320,256},{384,448},{4... | collective-permute-start | bytes 36872 | tf_op jit(solution)/shard_map/ppermute | solution.py:277
  29.0 8.9 %collective-permute-start.6 = (f32[3,8,128]{2,1,0:T(8,128)S(1)}, f32[3,8,128]{2,1,0:T(8,128)S(1)}, u32[]{:S(2)}, u32[]{:S(2)}) collective-permute-start(f32[3,8,128]{2,1,0:T(8,128)S(1)} %get-tuple-element.59), channel_id=1, source_target_pairs={{1,2},{3,4},{5,6},{7,8},{9,10},{11,12},{13,14},{15,16},{17,18},{19... | collective-permute-start | bytes 36872 | tf_op jit(solution)/shard_map/ppermute | solution.py:275
  32.3 5.6 %collective-permute-start.7 = (f32[3,8,128]{2,1,0:T(8,128)S(1)}, f32[3,8,128]{2,1,0:T(8,128)S(1)}, u32[]{:S(2)}, u32[]{:S(2)}) collective-permute-start(f32[3,8,128]{2,1,0:T(8,128)S(1)} %get-tuple-element.52), channel_id=1, source_target_pairs={{0,1},{1,0},{2,3},{3,2},{4,5},{5,4},{6,7},{7,6},{8,9},{9,8},{10,11... | collective-permute-start | bytes 36872 | tf_op jit(solution)/shard_map/ppermute | solution.py:277

commit v10 on v9

--- a/solution.py
+++ b/solution.py
@@ -126,7 +126,7 @@
             matrix[at_rows, 2 * y * width : 2 * (y + 1) * width] = pair
 
 
-def hot_kernel(index, count, fresh, hot, new_state, index_scr, sem):
+def hot_kernel(index, count, fresh, after, hot, new_state, index_scr, sem):
     store = pltpu.make_async_copy(fresh, new_state, sem)
     store.start()
     slots = index.shape[2]
@@ -373,19 +373,18 @@
         name="ocean",
     )
     row1, row2 = exchange(send1, send2, "row")
+    send1, send2 = column_sends(row1, row2, own, [], plus_r, plus_c)
+    col1, col2 = exchange(send1, send2, "col")
     hot, new_state = call(
         hot_kernel,
         [shape(9 * width, 2 * width, dtype=BF16), shape(fields * rows, width)],
         [pltpu.VMEM((16, width), jnp.int32), pltpu.SemaphoreType.DMA],
-        [VMEM] * 3,
+        [VMEM] * 4,
         1_000_000, 200_000,
-        index, count, fresh,
+        index, count, fresh, send1,
         out_specs=[VMEM, HBM],
         name="hot",
     )
-    row1, row2, hot = lax.optimization_barrier((row1, row2, hot))
-    send1, send2 = column_sends(row1, row2, own, [], plus_r, plus_c)
-    col1, col2 = exchange(send1, send2, "col")
     (result,) = call(
         surface_kernel,
         [shape(fields, atm_cells)],

time: 39.1 us -> 39.1 us (level)
    ppermute x4, waiting for transfers between devices: 3.66 us -> 3.01 us  [exchange(): one = lax.ppermute(send1, axis, far)]
    ppermute x4, waiting for transfers between devices: 3.36 us -> 4.01 us  [exchange(): two = lax.ppermute(send2, axis, near)]
where the time goes in v10:
time: 39.1 us; the launch traced here: 38.7 us
  starting transfers between devices  25.8 us (66%)
  waiting for transfers between devices  7.02 us (18%)
  Pallas kernels  5.04 us (13%)
  between operations  0.81 us (2%)
    ppermute x4, starting transfers between devices, exchange(): one = lax.ppermute(send1, axis, far)  13.4 us
    ppermute x4, starting transfers between devices, exchange(): two = lax.ppermute(send2, axis, near)  12.5 us
    pallas_call x5, Pallas kernels, call(): pl.pallas_call(kernel, out_shape=outs, in_specs=specs, out_specs=out_spec...  5.04 us
    ppermute x4, waiting for transfers between devices, exchange(): two = lax.ppermute(send2, axis, near)  4.01 us
    ppermute x4, waiting for transfers between devices, exchange(): one = lax.ppermute(send1, axis, far)  3.01 us
  transfers between devices with their start and end apart: 8, of which 4 were waited for; matrix products, arithmetic and copies ran while one was open for 0% of the time, Pallas kernels for 5%

profile of v10, /device:TPU:430, one launch (start us, length us, event | category | flops | bytes accessed | tf_op | source)
XLA Modules:
  0.0 38.7 jit_solution(16898313389434626027)
XLA Ops:
  0.6 1.2 %pack.1 = (f32[4,8,128]{2,1,0:T(8,128)S(1)}, f32[4,8,128]{2,1,0:T(8,128)S(1)}, f32[5,8,128]{2,1,0:T(8,128)S(1)}, s32[9,1,48]{2,1,0:T(1,128)S(1)}, s32[3,1,3]{2,1...) custom-call(f32[20,96]{1,0:T(8,128)} %flux.1, ...), custom_call_target="tpu_custom_call" | custom-call | flops 100000 | bytes 1000000 | tf_op jit(solution)/shard_map/pack/pallas_call | solution.py:294
  1.8 1.9 %collective-permute-start = (f32[4,8,128]{2,1,0:T(8,128)S(1)}, f32[4,8,128]{2,1,0:T(8,128)S(1)}, u32[]{:S(2)}, u32[]{:S(2)}) collective-permute-start(f32[4,8,128]{2,1,0:T(8,128)S(1)} %get-tuple-element.27), channel_id=1, source_target_pairs={{64,128},{192,256},{320,384},{448,512},{576,640},{704,768},{832,89... | collective-permute-start | bytes 49160 | tf_op jit(solution)/shard_map/ppermute | solution.py:275
  3.8 3.7 %collective-permute-start.1 = (f32[4,8,128]{2,1,0:T(8,128)S(1)}, f32[4,8,128]{2,1,0:T(8,128)S(1)}, u32[]{:S(2)}, u32[]{:S(2)}) collective-permute-start(f32[4,8,128]{2,1,0:T(8,128)S(1)} %get-tuple-element.29), channel_id=1, source_target_pairs={{0,64},{64,0},{128,192},{192,128},{256,320},{320,256},{384,448},{4... | collective-permute-start | bytes 49160 | tf_op jit(solution)/shard_map/ppermute | solution.py:277
  7.5 0.8 %collective-permute-done.1.row2 = f32[4,8,128]{2,1,0:T(8,128)S(1)} collective-permute-done((f32[4,8,128]{2,1,0:T(8,128)S(1)}, f32[4,8,128]{2,1,0:T(8,128)S(1)}, u32[]{:S(2)}, u32[]{:S(2)}) %collective-permute-start.1) | collective-permute-done | bytes 16416 | tf_op jit(solution)/shard_map/ppermute | solution.py:277
  8.3 0.0 collective-permute-done.row1
  8.3 6.2 %collective-permute-start.2 = (f32[4,8,128]{2,1,0:T(8,128)S(1)}, f32[4,8,128]{2,1,0:T(8,128)S(1)}, u32[]{:S(2)}, u32[]{:S(2)}) collective-permute-start(f32[4,8,128]{2,1,0:T(8,128)S(1)} %get-tuple-element.49.after), channel_id=1, source_target_pairs={{1,2},{3,4},{5,6},{7,8},{9,10},{11,12},{13,14},{15,16},{17,18},{19... | collective-permute-start | bytes 49160 | tf_op jit(solution)/shard_map/ppermute | solution.py:275
  14.6 1.9 %collective-permute-start.3 = (f32[4,8,128]{2,1,0:T(8,128)S(1)}, f32[4,8,128]{2,1,0:T(8,128)S(1)}, u32[]{:S(2)}, u32[]{:S(2)}) collective-permute-start(f32[4,8,128]{2,1,0:T(8,128)S(1)} %get-tuple-element.31), channel_id=1, source_target_pairs={{0,1},{1,0},{2,3},{3,2},{4,5},{5,4},{6,7},{7,6},{8,9},{9,8},{10,11... | collective-permute-start | bytes 49160 | tf_op jit(solution)/shard_map/ppermute | solution.py:277
  16.5 1.3 %spread.1 = (bf16[432,2048]{1,0:T(8,128)(2,1)S(1)}, f32[8,432]{1,0:T(8,128)S(1)}) custom-call(s32[9,1,48]{2,1,0:T(1,128)S(1)} %get-tuple-element.32.start, f32[1,3,3,48,128]{4,3,2,1,0:T(8,128)S(1)} %get-tuple-element.33.weight, f32[4,8,128]{2,1,0:T(8,128)S(1)} %get-tuple-element.49.after), custom_call_target="tpu_custom_call" | custom-call | flops 20000000 | bytes 4000000 | tf_op jit(solution)/shard_map/spread/pallas_call | solution.py:294
  17.8 0.0 collective-permute-done.2.col1
  17.8 2.4 %collective-permute-done.3.col2 = f32[4,8,128]{2,1,0:T(8,128)S(1)} collective-permute-done((f32[4,8,128]{2,1,0:T(8,128)S(1)}, f32[4,8,128]{2,1,0:T(8,128)S(1)}, u32[]{:S(2)}, u32[]{:S(2)}) %collective-permute-start.3) | collective-permute-done | bytes 16416 | tf_op jit(solution)/shard_map/ppermute | solution.py:277
  20.2 1.1 %ocean.1 = (f32[128,128]{1,0:T(8,128)S(1)}, f32[3,8,128]{2,1,0:T(8,128)S(1)}, f32[3,8,128]{2,1,0:T(8,128)S(1)}, f32[3,8,128]{2,1,0:T(8,128)S(1)}) custom-call(f32[4,8,128]{2,1,0:T(8,128)S(1)} %collective-permute-done.row1, f32[4,8,128]{2,1,0:T(8,128)S(1)} %collective-permute-done.1.row2, f32[4,8,128]{2,1,0:T(8,128)S(1)} %collective-permute-done.2.col1, ...), custom_call_target="tpu_custom_call" | custom-call | flops 100000000 | bytes 4000000 | tf_op jit(solution)/shard_map/ocean/pallas_call | solution.py:294
  21.3 1.9 %collective-permute-start.5 = (f32[3,8,128]{2,1,0:T(8,128)S(1)}, f32[3,8,128]{2,1,0:T(8,128)S(1)}, u32[]{:S(2)}, u32[]{:S(2)}) collective-permute-start(f32[3,8,128]{2,1,0:T(8,128)S(1)} %get-tuple-element.42), channel_id=1, source_target_pairs={{64,128},{192,256},{320,384},{448,512},{576,640},{704,768},{832,89... | collective-permute-start | bytes 36872 | tf_op jit(solution)/shard_map/ppermute | solution.py:275
  23.2 4.9 %collective-permute-start.4 = (f32[3,8,128]{2,1,0:T(8,128)S(1)}, f32[3,8,128]{2,1,0:T(8,128)S(1)}, u32[]{:S(2)}, u32[]{:S(2)}) collective-permute-start(f32[3,8,128]{2,1,0:T(8,128)S(1)} %get-tuple-element.43), channel_id=1, source_target_pairs={{0,64},{64,0},{128,192},{192,128},{256,320},{320,256},{384,448},{4... | collective-permute-start | bytes 36872 | tf_op jit(solution)/shard_map/ppermute | solution.py:277
  28.2 0.8 %collective-permute-done.4.row2 = f32[3,8,128]{2,1,0:T(8,128)S(1)} collective-permute-done((f32[3,8,128]{2,1,0:T(8,128)S(1)}, f32[3,8,128]{2,1,0:T(8,128)S(1)}, u32[]{:S(2)}, u32[]{:S(2)}) %collective-permute-start.4) | collective-permute-done | bytes 12320 | tf_op jit(solution)/shard_map/ppermute | solution.py:277
  29.0 0.0 collective-permute-done.5.row1
  29.0 3.3 %collective-permute-start.6 = (f32[3,8,128]{2,1,0:T(8,128)S(1)}, f32[3,8,128]{2,1,0:T(8,128)S(1)}, u32[]{:S(2)}, u32[]{:S(2)}) collective-permute-start(f32[3,8,128]{2,1,0:T(8,128)S(1)} %get-tuple-element.53.after), channel_id=1, source_target_pairs={{1,2},{3,4},{5,6},{7,8},{9,10},{11,12},{13,14},{15,16},{17,18},{19... | collective-permute-start | bytes 36872 | tf_op jit(solution)/shard_map/ppermute | solution.py:275
  32.3 1.9 %collective-permute-start.7 = (f32[3,8,128]{2,1,0:T(8,128)S(1)}, f32[3,8,128]{2,1,0:T(8,128)S(1)}, u32[]{:S(2)}, u32[]{:S(2)}) collective-permute-start(f32[3,8,128]{2,1,0:T(8,128)S(1)} %get-tuple-element.46), channel_id=1, source_target_pairs={{0,1},{1,0},{2,3},{3,2},{4,5},{5,4},{6,7},{7,6},{8,9},{9,8},{10,11... | collective-permute-start | bytes 36872 | tf_op jit(solution)/shard_map/ppermute | solution.py:277
  34.3 0.6 %hot.1 = (bf16[1152,256]{1,0:T(8,128)(2,1)S(1)}, f32[128,128]{1,0:T(8,128)}) custom-call(s32[9,1,48]{2,1,0:T(1,128)S(1)} %get-tuple-element.25.index, s32[3,1,3]{2,1,0:T(1,128)S(1)} %get-tuple-element.26.count, f32[128,128]{1,0:T(8,128)S(1)} %get-tuple-element.40.fresh, f32[3,8,128]{2,1,0:T(8,128)S(1)} %get-tuple-element.53.after), custom_call_target="tpu_custom_call" | custom-call | flops 1000000 | bytes 200000 | tf_op jit(solution)/shard_map/hot/pallas_call | solution.py:294
  34.9 3.0 %collective-permute-done.6.col1 = f32[3,8,128]{2,1,0:T(8,128)S(1)} collective-permute-done((f32[3,8,128]{2,1,0:T(8,128)S(1)}, f32[3,8,128]{2,1,0:T(8,128)S(1)}, u32[]{:S(2)}, u32[]{:S(2)}) %collective-permute-start.6) | collective-permute-done | bytes 12320 | tf_op jit(solution)/shard_map/ppermute | solution.py:275
  37.9 0.0 collective-permute-done.7.col2
  37.9 0.8 %surface.1 = f32[8,96]{1,0:T(8,128)} custom-call(f32[3,8,128]{2,1,0:T(8,128)S(1)} %collective-permute-done.5.row1, f32[3,8,128]{2,1,0:T(8,128)S(1)} %collective-permute-done.4.row2, f32[3,8,128]{2,1,0:T(8,128)S(1)} %collective-permute-done.6.col1, f32[3,8,128]{2,1,0:T(8,128)S(1)} %collective-permute-done.7.col2, f32[3,8,128]{2,1,0:T(8,128)S(1)} %get-tuple-element.44.own, ...), custom_call_target="tpu_custom_call" | custom-call | flops 1000000 | bytes 200000 | tf_op jit(solution)/shard_map/surface/pallas_call | solution.py:294
  (9 shorter events, 0.0 us)
Async XLA Ops:
  1.8 6.5 %collective-permute-start = (f32[4,8,128]{2,1,0:T(8,128)S(1)}, f32[4,8,128]{2,1,0:T(8,128)S(1)}, u32[]{:S(2)}, u32[]{:S(2)}) collective-permute-start(f32[4,8,128]{2,1,0:T(8,128)S(1)} %get-tuple-element.27), channel_id=1, source_target_pairs={{64,128},{192,256},{320,384},{448,512},{576,640},{704,768},{832,89... | collective-permute-start | bytes 49160 | tf_op jit(solution)/shard_map/ppermute | solution.py:275
  3.8 4.5 %collective-permute-start.1 = (f32[4,8,128]{2,1,0:T(8,128)S(1)}, f32[4,8,128]{2,1,0:T(8,128)S(1)}, u32[]{:S(2)}, u32[]{:S(2)}) collective-permute-start(f32[4,8,128]{2,1,0:T(8,128)S(1)} %get-tuple-element.29), channel_id=1, source_target_pairs={{0,64},{64,0},{128,192},{192,128},{256,320},{320,256},{384,448},{4... | collective-permute-start | bytes 49160 | tf_op jit(solution)/shard_map/ppermute | solution.py:277
  8.3 9.4 %collective-permute-start.2 = (f32[4,8,128]{2,1,0:T(8,128)S(1)}, f32[4,8,128]{2,1,0:T(8,128)S(1)}, u32[]{:S(2)}, u32[]{:S(2)}) collective-permute-start(f32[4,8,128]{2,1,0:T(8,128)S(1)} %get-tuple-element.49.after), channel_id=1, source_target_pairs={{1,2},{3,4},{5,6},{7,8},{9,10},{11,12},{13,14},{15,16},{17,18},{19... | collective-permute-start | bytes 49160 | tf_op jit(solution)/shard_map/ppermute | solution.py:275
  14.6 5.6 %collective-permute-start.3 = (f32[4,8,128]{2,1,0:T(8,128)S(1)}, f32[4,8,128]{2,1,0:T(8,128)S(1)}, u32[]{:S(2)}, u32[]{:S(2)}) collective-permute-start(f32[4,8,128]{2,1,0:T(8,128)S(1)} %get-tuple-element.31), channel_id=1, source_target_pairs={{0,1},{1,0},{2,3},{3,2},{4,5},{5,4},{6,7},{7,6},{8,9},{9,8},{10,11... | collective-permute-start | bytes 49160 | tf_op jit(solution)/shard_map/ppermute | solution.py:277
  21.3 7.7 %collective-permute-start.5 = (f32[3,8,128]{2,1,0:T(8,128)S(1)}, f32[3,8,128]{2,1,0:T(8,128)S(1)}, u32[]{:S(2)}, u32[]{:S(2)}) collective-permute-start(f32[3,8,128]{2,1,0:T(8,128)S(1)} %get-tuple-element.42), channel_id=1, source_target_pairs={{64,128},{192,256},{320,384},{448,512},{576,640},{704,768},{832,89... | collective-permute-start | bytes 36872 | tf_op jit(solution)/shard_map/ppermute | solution.py:275
  23.2 5.7 %collective-permute-start.4 = (f32[3,8,128]{2,1,0:T(8,128)S(1)}, f32[3,8,128]{2,1,0:T(8,128)S(1)}, u32[]{:S(2)}, u32[]{:S(2)}) collective-permute-start(f32[3,8,128]{2,1,0:T(8,128)S(1)} %get-tuple-element.43), channel_id=1, source_target_pairs={{0,64},{64,0},{128,192},{192,128},{256,320},{320,256},{384,448},{4... | collective-permute-start | bytes 36872 | tf_op jit(solution)/shard_map/ppermute | solution.py:277
  29.0 8.9 %collective-permute-start.6 = (f32[3,8,128]{2,1,0:T(8,128)S(1)}, f32[3,8,128]{2,1,0:T(8,128)S(1)}, u32[]{:S(2)}, u32[]{:S(2)}) collective-permute-start(f32[3,8,128]{2,1,0:T(8,128)S(1)} %get-tuple-element.53.after), channel_id=1, source_target_pairs={{1,2},{3,4},{5,6},{7,8},{9,10},{11,12},{13,14},{15,16},{17,18},{19... | collective-permute-start | bytes 36872 | tf_op jit(solution)/shard_map/ppermute | solution.py:275
  32.3 5.6 %collective-permute-start.7 = (f32[3,8,128]{2,1,0:T(8,128)S(1)}, f32[3,8,128]{2,1,0:T(8,128)S(1)}, u32[]{:S(2)}, u32[]{:S(2)}) collective-permute-start(f32[3,8,128]{2,1,0:T(8,128)S(1)} %get-tuple-element.46), channel_id=1, source_target_pairs={{0,1},{1,0},{2,3},{3,2},{4,5},{5,4},{6,7},{7,6},{8,9},{9,8},{10,11... | collective-permute-start | bytes 36872 | tf_op jit(solution)/shard_map/ppermute | solution.py:277
